TPU v7x, 32 devices: a whole 2x2x4 slice. The times are simulated.
32 devices in a mesh: tile: 16 (over z, y, x), dp: 2 (over core).
Axes of the slice: x: 2, y: 2, z: 4, core: 2. Of those that a mesh axis runs over, the one named last changes fastest.
Arguments:
- features: bfloat16 [2, 192, 384, 128], P('dp', 'tile'), may hold values from -6 to 6
- cotangent: bfloat16 [2, 192, 384, 128], P('dp', 'tile'), may hold values from -6 to 6
- tile_mask: int32 [2, 16, 32], P('dp', 'tile'), may hold values from 0 to 1, as said below
- work_lists: int32 [2, 16, 22], P('dp'), may hold values from 0 to 511, as said below
- dilations: int32 [2, 16], P('dp'), may hold values from 1 to 2
- conv_weight: bfloat16 [3, 3, 128, 128], replicated, may hold values from -0.1875 to 0.1875
- conv_bias: float32 [128], replicated, may hold values from -4 to 4
Outputs:
- input_grad: bfloat16 [2, 192, 384, 128], P('dp', 'tile')
- weight_grads: float32 [147456], P(('tile', 'dp'))
Inputs may be any that keep to these rules, and one draw needn't show every extreme that they name: `tile_mask`: exactly 352 tiles of each copy are 1. `work_lists`: for each copy, the work lists name every tile whose mask is 1 exactly once, as row * 32 + column, 22 for each worker; at most 2 of one worker's ids lie in one row of tiles, and in every draw some worker has 2 ids in one row.
All inputs are finite; a program needn't handle non-finite values.
Results may differ from a plain program's by a relative error of at most 0.0055.
Values may be sent and summed in bfloat16 or wider, within the bound.
No kernel may reach another device: no remote copies, remote signals or barrier semaphores. Data moves between devices by JAX's collectives and lax.ppermute only.
A program may use at most 128 MiB of HBM per device.

v0:
```python
import math

import jax
import jax.numpy as jnp
from jax import lax
from jax.experimental import pallas as pl
from jax.experimental.pallas import tpu as pltpu
from jax.sharding import PartitionSpec as P

TILE = 12
HALO = 2
LANES = 128
EDGE = 8
RATES = (1, 2)
VMEM_LIMIT = 40 * 1024 * 1024

F32 = jnp.float32
BF16 = jnp.bfloat16


def cell_masks(lists_ref, middle, tiles_row, columns):
    ids = lists_ref[...]
    workers, width = ids.shape
    tile = lax.broadcasted_iota(jnp.int32, (3 * tiles_row, width), 0)
    target = (middle - 1) * tiles_row + tile
    found = ids[0:1] == target
    for worker in range(1, workers):
        found = found | (ids[worker : worker + 1] == target)
    named = jnp.dot(
        jnp.where(found, 1.0, 0.0).astype(BF16),
        jnp.ones((width, LANES), BF16),
        preferred_element_type=F32,
    ).astype(BF16)
    first = TILE * lax.broadcasted_iota(jnp.int32, (columns, tiles_row), 1)
    cell = lax.broadcasted_iota(jnp.int32, (columns, tiles_row), 0)
    inside = jnp.where((cell >= first) & (cell < first + TILE), 1.0, 0.0).astype(BF16)
    return [
        jnp.dot(
            inside, named[k * tiles_row : (k + 1) * tiles_row], preferred_element_type=F32
        ).astype(BF16)
        for k in range(3)
    ]


def row_pairs(rate, rows):
    rows = list(rows)
    pairs = []
    for start in range(0, len(rows), 2 * rate):
        for k in range(rate):
            pairs.append((rows[start + k], rows[start + k + rate]))
    return pairs


def by_rate(rate, body):
    for value in RATES:
        pl.when(rate == value)(lambda value=value: body(value))


def clear_ends(pad_ref, count, columns):
    ends = jnp.zeros((EDGE, pad_ref.shape[-1]), F32)
    for k in range(count):
        pad_ref[k, :EDGE] = ends
        pad_ref[k, EDGE + columns :] = ends


def spread(value, pad_ref, slot, target_ref, offset):
    columns, channels = value.shape
    pad_ref[slot, EDGE : EDGE + columns] = value.astype(F32)
    target_ref[:, :channels] = pad_ref[slot, pl.ds(EDGE - offset, columns)].astype(BF16)
    target_ref[:, channels : 2 * channels] = value.astype(BF16)
    target_ref[:, 2 * channels :] = pad_ref[slot, pl.ds(EDGE + offset, columns)].astype(BF16)


def silu_grad(half_cot, half_pre):
    turn = jnp.tanh(half_pre)
    return half_cot * (1.0 + turn + half_pre * (1.0 - turn * turn))


def tap_sums(grads, xts, rate):
    flipped = jnp.concatenate(
        [
            jnp.concatenate([xts(row + rate * a) for row, _ in grads], axis=1)
            for a in (-1, 0, 1)
        ],
        axis=0,
    )
    return jnp.dot(
        flipped,
        jnp.concatenate([ref[...] for _, ref in grads], axis=0),
        preferred_element_type=F32,
    )


def pair_rows(pair, rate, rows):
    reach = [pair[0] + rate * (k - 1) for k in range(4)]
    inside = [k for k in range(4) if 0 <= reach[k] < rows]
    return [reach[k] for k in inside], inside[0], inside[-1] + 1


def input_sums(pair, rate, rows, grads, wide_ref):
    near, low, high = pair_rows(pair, rate, rows)
    lhs = jnp.concatenate([grads(row)[...] for row in near], axis=1)
    width = wide_ref.shape[1] // 4
    both = lax.dot_general(
        lhs,
        wide_ref[:, low * width : high * width],
        (((1,), (1,)), ((), ())),
        preferred_element_type=F32,
    )
    half = both.shape[1] // 2
    return both[:, :half], both[:, half:]


def first_kernel(
    rates_ref, lists_ref, x_hbm, cot_hbm, w_hbm, bias_ref,
    out_hbm, pre_ref, gcat_ref, xt_ref, total_ref, mask_ref, cot_ref, back_ref,
    xbuf, cbuf, wbuf, obuf, pad, xcat, wide, sems,
):
    rows, columns, channels = x_hbm.shape
    tiles_row = columns // TILE
    mine = lax.axis_index("tile")
    loads = [
        pltpu.make_async_copy(w_hbm, wbuf, sems.at[0]),
        pltpu.make_async_copy(x_hbm, xbuf, sems.at[1]),
        pltpu.make_async_copy(cot_hbm, cbuf, sems.at[2]),
    ]
    for load in loads:
        load.start()
    for k, value in enumerate(cell_masks(lists_ref, mine, tiles_row, columns)):
        mask_ref[k] = value
    clear_ends(pad, rows, columns)
    loads[0].wait()
    none = jnp.zeros((channels, channels), BF16)
    for row in range(4):
        for out in range(2):
            there = slice(out * channels, (out + 1) * channels)
            for col in range(3):
                start = (row * 3 + col) * channels
                here = slice(start, start + channels)
                tap = row - out
                wide[here, there] = wbuf[tap * 3 + col] if 0 <= tap < 3 else none
                tap = out + 2 - row
                back_ref[there, here] = wbuf[tap * 3 + col] if 0 <= tap < 3 else none
    loads[1].wait()
    loads[2].wait()
    half_bias = 0.5 * bias_ref[...]
    middle = range(2 * HALO, rows - 2 * HALO)
    store = pltpu.make_async_copy(
        obuf, out_hbm.at[pl.ds(middle.start, len(middle))], sems.at[3]
    )

    def body(rate):
        done = set()

        def prepare(row):
            if row in done:
                return
            done.add(row)
            value = xbuf[row] * mask_ref[1]
            spread(value, pad, row, xcat.at[row], rate)
            xt_ref[row] = value.T

        def convolve(pair):
            near, low, high = pair_rows(pair, rate, rows)
            for row in near:
                prepare(row)
            lhs = jnp.concatenate([xcat[row] for row in near], axis=1)
            width = wide.shape[0] // 4
            both = jnp.dot(
                lhs, wide[low * width : high * width], preferred_element_type=F32
            )
            return pair, (both[:, :channels], both[:, channels:])

        def finish(pair, sums):
            for row, value in zip(pair, sums):
                half_pre = 0.5 * value + half_bias
                half_cot = cbuf[row] * mask_ref[1] * 0.5
                if HALO <= row < rows - HALO:
                    grad = silu_grad(half_cot.astype(F32), half_pre)
                    spread(grad, pad, row, gcat_ref.at[row - HALO], -rate)
                    ready.append(row)
                else:
                    here = row if row < HALO else row - (rows - 2 * HALO)
                    pre_ref[here] = half_pre
                    cot_ref[here] = half_cot

        ready = []
        summed = []
        waiting = None
        for pair in row_pairs(rate, range(rows)) + [None]:
            result = convolve(pair) if pair else None
            if waiting:
                finish(*waiting)
            waiting = result
            while len(ready) >= 2:
                grads = [(row, gcat_ref.at[row - HALO]) for row in ready[:2]]
                part = tap_sums(grads, lambda row: xt_ref[row], rate)
                total_ref[...] = total_ref[...] + part if summed else part
                summed.extend(ready[:2])
                del ready[:2]
        for pair in row_pairs(rate, middle):
            sums = input_sums(pair, rate, rows, lambda row: gcat_ref.at[row - HALO], back_ref)
            for row, value in zip(pair, sums):
                value = (value + cbuf[row].astype(F32)).astype(BF16)
                obuf[row - middle.start] = value * mask_ref[1]

    by_rate(rates_ref[0, mine], body)
    store.start()
    store.wait()


def rims_kernel(
    rates_ref, low_ref, high_ref, pre_ref, cot_ref, mask_ref, w_ref,
    grad_low_ref, grad_high_ref, xt_ref,
    pad, xcat,
):
    _, columns, channels = low_ref.shape
    clear_ends(pad, 2 * HALO, columns)

    def body(rate):
        for side, ref in enumerate((low_ref, high_ref)):
            used = range(HALO - rate, HALO) if side == 0 else range(rate)
            for place, k in enumerate(used):
                value = ref[k] * mask_ref[2 * side]
                spread(
                    value, pad, side * HALO + k, xcat.at[pl.ds(place * columns, columns)], rate
                )
                xt_ref[side * HALO + k] = value.T
            taps = jnp.concatenate([w_ref[6 * side + b] for b in range(3)], axis=0)
            sums = jnp.dot(
                xcat[: rate * columns], taps, preferred_element_type=F32
            )
            for k in range(HALO):
                half_pre = pre_ref[side * HALO + k]
                place = k if side == 0 else k - (HALO - rate)
                if 0 <= place < rate:
                    half_pre += 0.5 * sums[place * columns : (place + 1) * columns]
                grad = silu_grad(cot_ref[side * HALO + k].astype(F32), half_pre)
                target = grad_high_ref if side else grad_low_ref
                target[k] = grad.astype(BF16)

    by_rate(rates_ref[0, lax.axis_index("tile")], body)


def taps_kernel(
    rates_ref, grad_low_ref, grad_high_ref, xt_own_ref, xt_halo_ref, total_ref,
    tap_ref, gcat_ref,
    pad, flat, *, scale,
):
    _, columns, channels = grad_low_ref.shape
    rows = xt_own_ref.shape[0]
    clear_ends(pad, 2 * HALO, columns)

    def flipped(row):
        if row < 0:
            return xt_halo_ref[row + HALO]
        return xt_own_ref[row] if row < rows else xt_halo_ref[row - rows + HALO]

    def body(rate):
        grads = []
        for side, ref in enumerate((grad_low_ref, grad_high_ref)):
            for k in range(HALO):
                slot = side * HALO + k
                spread(ref[k], pad, slot, gcat_ref.at[slot], -rate)
                grads.append((k + side * (rows - HALO), gcat_ref.at[slot]))
        total = (total_ref[...] + tap_sums(grads, flipped, rate)) * scale
        for a in range(3):
            for b in range(3):
                start = (a * 3 + b) * channels
                flat[start : start + channels] = total[
                    a * channels : (a + 1) * channels, b * channels : (b + 1) * channels
                ]

    by_rate(rates_ref[0, lax.axis_index("tile")], body)
    share = tap_ref.shape[1]
    for part in range(tap_ref.shape[0]):
        tap_ref[part] = flat[part * share : (part + 1) * share].astype(BF16)


def inputs_kernel(
    rates_ref, gcat_ref, gedge_ref, cot_hbm, mask_ref, back_ref, held_hbm,
    out_hbm, edge_ref,
    cbuf, obuf, sems,
):
    del held_hbm
    rows, columns, channels = cot_hbm.shape
    around = 2 * HALO
    loads = [
        pltpu.make_async_copy(
            cot_hbm.at[pl.ds(side * (rows - around), around)],
            cbuf.at[pl.ds(side * around, around)],
            sems.at[side],
        )
        for side in range(2)
    ]
    stores = [
        pltpu.make_async_copy(
            obuf.at[pl.ds(side * HALO, HALO)],
            out_hbm.at[pl.ds(HALO + side * (rows - 3 * HALO), HALO)],
            sems.at[2 + side],
        )
        for side in range(2)
    ]
    for load in loads:
        load.start()
    for load in loads:
        load.wait()

    def grads(row):
        if row < HALO:
            return gedge_ref.at[row]
        if row < rows - HALO:
            return gcat_ref.at[row - HALO]
        return gedge_ref.at[row - (rows - 2 * HALO)]

    def body(rate):
        for side in range(2):
            start = side * (rows - around)
            for pair in row_pairs(rate, range(start, start + around)):
                sums = input_sums(pair, rate, rows, grads, back_ref)
                for row, value in zip(pair, sums):
                    value = value + cbuf[row - start + side * around].astype(F32)
                    if HALO <= row < rows - HALO:
                        here = row - HALO if side == 0 else row - (rows - around) + HALO
                        obuf[here] = value.astype(BF16) * mask_ref[1]
                    else:
                        here = row if side == 0 else row - (rows - around)
                        edge_ref[here] = value

    by_rate(rates_ref[0, lax.axis_index("tile")], body)
    for store in stores:
        store.start()
    for store in stores:
        store.wait()


def edges_kernel(
    rates_ref, low_ref, high_ref, edge_ref, mask_ref, w_ref, received_ref, held_hbm,
    out_hbm, sum_ref,
    obuf, pad, gcat, sems,
):
    del held_hbm
    _, columns, channels = low_ref.shape
    rows = out_hbm.shape[0]
    mine = lax.axis_index("tile")
    last = rates_ref.shape[1] - 1
    clear_ends(pad, 2 * HALO, columns)
    stores = [
        pltpu.make_async_copy(
            obuf.at[pl.ds(HALO * side, HALO)],
            out_hbm.at[pl.ds((rows - HALO) * side, HALO)],
            sems.at[side],
        )
        for side in range(2)
    ]

    def one_side(side, rate):
        ref = high_ref if side else low_ref
        used = range(rate) if side else range(HALO - rate, HALO)
        for place, k in enumerate(used):
            spread(
                ref[k], pad, side * HALO + k, gcat.at[side, pl.ds(place * columns, columns)], -rate
            )
        taps = jnp.concatenate([w_ref[6 * (1 - side) + b] for b in range(3)], axis=1)
        sums = lax.dot_general(
            gcat[side, : rate * columns],
            taps,
            (((1,), (1,)), ((), ())),
            preferred_element_type=F32,
        )
        for k in range(HALO):
            value = edge_ref[side * HALO + k]
            place = k - (HALO - rate) if side else k
            if 0 <= place < rate:
                value = value + sums[place * columns : (place + 1) * columns]
            obuf[side * HALO + k] = value.astype(BF16) * mask_ref[1]

    near = (jnp.maximum(mine - 1, 0), jnp.minimum(mine + 1, last))
    for side in range(2):
        by_rate(rates_ref[0, near[side]], lambda rate, side=side: one_side(side, rate))
        stores[side].start()
    if sum_ref.shape == received_ref.shape[1:]:
        sum_ref[...] = jnp.sum(received_ref[...].astype(F32), axis=0)
    for store in stores:
        store.wait()


def exchange(to_next, to_previous, axis):
    count = lax.axis_size(axis)
    forward = [(i, i + 1) for i in range(count - 1)]
    backward = [(target, source) for source, target in forward]
    return lax.ppermute(to_next, axis, forward), lax.ppermute(to_previous, axis, backward)


def call(kernel, name, outs, specs, scratch, aliases=None):
    memory = {"s": pltpu.SMEM, "v": pltpu.VMEM, "h": pltpu.HBM}
    ins, results = (
        [pl.BlockSpec(memory_space=memory[letter]) for letter in part] for part in specs.split(">")
    )
    return pl.pallas_call(
        kernel,
        name=name,
        out_shape=tuple(jax.ShapeDtypeStruct(shape, dtype) for shape, dtype in outs),
        in_specs=ins,
        out_specs=tuple(results),
        scratch_shapes=scratch,
        input_output_aliases=aliases or {},
        cost_estimate=pl.CostEstimate(flops=0, bytes_accessed=0, transcendentals=0),
        compiler_params=pltpu.CompilerParams(vmem_limit_bytes=VMEM_LIMIT),
    )


def in_hbm(array):
    return pltpu.with_memory_space_constraint(array, pltpu.HBM)


def shards(features, cotangent, tile_mask, work_lists, dilations, conv_weight, conv_bias):
    x, cot, lists = features[0], in_hbm(cotangent[0]), in_hbm(work_lists[0])
    dilations = in_hbm(dilations)
    rows, columns, channels = x.shape
    axes = ("tile", "dp")
    devices = lax.axis_size("tile") * lax.axis_size("dp")
    weight = in_hbm(conv_weight.reshape(9, channels, channels))
    bias = in_hbm(conv_bias.reshape(1, channels))
    inner = rows - 2 * HALO
    wide_row = 3 * channels
    whole = ((rows, columns, channels), BF16)

    def pads(count):
        return pltpu.VMEM((count, columns + 2 * EDGE, channels), F32)

    low, high = exchange(x[rows - HALO :], x[:HALO], "tile")

    held, pre, gcat, xt, total, mask, cot_edge, back = call(
        first_kernel,
        "first",
        [
            whole,
            ((2 * HALO, columns, channels), F32),
            ((inner, columns, wide_row), BF16),
            ((rows, channels, columns), BF16),
            ((wide_row, wide_row), F32),
            ((3, columns, channels), BF16),
            ((2 * HALO, columns, channels), BF16),
            ((2 * channels, 4 * wide_row), BF16),
        ],
        "svhhhv>hvvvvvvv",
        [
            pltpu.VMEM((rows, columns, channels), BF16),
            pltpu.VMEM((rows, columns, channels), BF16),
            pltpu.VMEM((9, channels, channels), BF16),
            pltpu.VMEM((rows - 4 * HALO, columns, channels), BF16),
            pads(rows),
            pltpu.VMEM((rows, columns, wide_row), BF16),
            pltpu.VMEM((4 * wide_row, 2 * channels), BF16),
            pltpu.SemaphoreType.DMA((4,)),
        ],
    )(dilations, lists, in_hbm(x), cot, weight, bias)

    grad_low, grad_high, xt_halo = call(
        rims_kernel,
        "rims",
        [
            ((HALO, columns, channels), BF16),
            ((HALO, columns, channels), BF16),
            ((2 * HALO, channels, columns), BF16),
        ],
        "svvvvvv>vvv",
        [pads(2 * HALO), pltpu.VMEM((HALO * columns, wide_row), BF16)],
    )(dilations, low, high, pre, cot_edge, mask, weight)

    from_low, from_high = exchange(grad_high, grad_low, "tile")

    tap_rows = 9 * channels
    direct = tap_rows % devices == 0
    share = (devices, tap_rows // devices) if direct else (1, tap_rows)
    scale = 1.0 / math.sqrt(devices * lists.shape[1] * TILE * TILE)
    taps, gedge = call(
        lambda *refs: taps_kernel(*refs, scale=scale),
        "taps",
        [(share + (channels,), BF16), ((2 * HALO, columns, wide_row), BF16)],
        "svvvvv>vv",
        [pads(2 * HALO), pltpu.VMEM((tap_rows, channels), F32)],
    )(dilations, grad_low, grad_high, xt, xt_halo, total)
    if not direct:
        taps = taps.reshape(devices, -1)
    received = lax.all_to_all(taps, axes, 0, 0, tiled=True)

    held, edge = call(
        inputs_kernel,
        "inputs",
        [whole, ((2 * HALO, columns, channels), F32)],
        "svvhvvh>hv",
        [
            pltpu.VMEM((4 * HALO, columns, channels), BF16),
            pltpu.VMEM((2 * HALO, columns, channels), BF16),
            pltpu.SemaphoreType.DMA((4,)),
        ],
        {6: 0},
    )(dilations, gcat, gedge, cot, mask, back, held)

    part = received.shape[1:] if direct else (8, LANES)
    input_grad, summed = call(
        edges_kernel,
        "edges",
        [whole, (part, F32)],
        "svvvvvvh>hv",
        [
            pltpu.VMEM((2 * HALO, columns, channels), BF16),
            pads(2 * HALO),
            pltpu.VMEM((2, HALO * columns, wide_row), BF16),
            pltpu.SemaphoreType.DMA((2,)),
        ],
        {7: 0},
    )(dilations, from_low, from_high, edge, mask, weight, received if direct else mask, held)
    if not direct:
        summed = jnp.sum(received.astype(F32), axis=0)
    return (input_grad[None], summed.reshape(-1))


def solution(mesh):
    placed = (
        P("dp", "tile", None, None),
        P("dp", "tile", None, None),
        P("dp", "tile", None),
        P("dp", None, None),
        P("dp", None),
        P(),
        P(),
    )
    return jax.shard_map(
        shards,
        mesh=mesh,
        in_specs=placed,
        out_specs=(P("dp", "tile", None, None), P(("tile", "dp"))),
        check_vma=False,
    )
```

profile of v0, /device:TPU:0, one launch (start us, length us, event | category | flops | bytes accessed | tf_op | source)
XLA Modules:
  0.0 51.9 jit_solution(36336428476572089)
XLA Ops:
  0.6 1.1 %slice_bitcast_fusion = (bf16[2,384,128]{2,1,0:T(8,128)(2,1)S(1)}, bf16[2,384,128]{2,1,0:T(8,128)(2,1)S(1)}) fusion(bf16[1,12,384,128]{3,2,1,0:T(8,128)(2,1)} %param.7), kind=kLoop, calls=%fused_computation | loop fusion | bytes 786432 | tf_op jit(solution)/shard_map/slice | solution.py:432
  1.7 1.3 %collective-permute-start.1 = (bf16[2,384,128]{2,1,0:T(8,128)(2,1)S(1)}, bf16[2,384,128]{2,1,0:T(8,128)(2,1)S(1)}, u32[]{:S(2)}, u32[]{:S(2)}) collective-permute-start(bf16[2,384,128]{2,1,0:T(8,128)(2,1)S(1)} %get-tuple-element.36), channel_id=1, source_target_pairs={{2,0},{4,2},{6,4},{8,6},{10,8},{12,10},{14,12},{16,14},{18,16},{20... | collective-permute-start | bytes 589832 | tf_op jit(solution)/shard_map/ppermute | solution.py:392
  3.0 5.5 %collective-permute-start = (bf16[2,384,128]{2,1,0:T(8,128)(2,1)S(1)}, bf16[2,384,128]{2,1,0:T(8,128)(2,1)S(1)}, u32[]{:S(2)}, u32[]{:S(2)}) collective-permute-start(bf16[2,384,128]{2,1,0:T(8,128)(2,1)S(1)} %get-tuple-element.37), channel_id=1, source_target_pairs={{0,2},{2,4},{4,6},{6,8},{8,10},{10,12},{12,14},{14,16},{16,18},{18... | collective-permute-start | bytes 589832 | tf_op jit(solution)/shard_map/ppermute | solution.py:392
  8.5 8.0 %first.1 = (bf16[12,384,128]{2,1,0:T(8,128)(2,1)}, f32[4,384,128]{2,1,0:T(8,128)S(1)}, bf16[8,384,384]{2,1,0:T(8,128)(2,1)S(1)}, bf16[12,128,384]{2,1,0:T(8,128)...) custom-call(s32[1,16]{1,0:T(1,128)} %rates_ref.7, ...), custom_call_target="tpu_custom_call" | custom-call | tf_op jit(solution)/shard_map/first/pallas_call | solution.py:434
  16.5 0.0 copy-start.4
  16.5 0.0 collective-permute-done.1.high_ref
  16.5 0.3 collective-permute-done.low_ref
  16.7 1.5 %rims.1 = (bf16[2,384,128]{2,1,0:T(8,128)(2,1)S(1)}, bf16[2,384,128]{2,1,0:T(8,128)(2,1)S(1)}, bf16[4,128,384]{2,1,0:T(8,128)(2,1)S(1)}) custom-call(s32[1,16]{1,0:T(1,128)} %rates_ref.7, bf16[2,384,128]{2,1,0:T(8,128)(2,1)S(1)} %collective-permute-done.low_ref, bf16[2,384,128]{2,1,0:T(8,128)(2,1)S(1)} %collective-permute-done.1.high_ref, ...), custom_call_target="tpu_custom_call" | custom-call | tf_op jit(solution)/shard_map/rims/pallas_call | solution.py:460
  18.3 2.4 %taps.1 = (bf16[32,36,128]{2,1,0:T(8,128)(2,1)}, bf16[4,384,384]{2,1,0:T(8,128)(2,1)S(1)}) custom-call(s32[1,16]{1,0:T(1,128)} %rates_ref.7, bf16[2,384,128]{2,1,0:T(8,128)(2,1)S(1)} %get-tuple-element.23.refs_1_, bf16[2,384,128]{2,1,0:T(8,128)(2,1)S(1)} %get-tuple-element.22.refs_2_, bf16[12,128,384]{2,1,0:T(8,128)(2,1)S(1)} %get-tuple-element.25.refs_3_, ...), custom_call_target="tpu_custom_call" | custom-call | tf_op jit(solution)/shard_map/taps/pallas_call | solution.py:478
  20.7 0.0 copy-done.4
  20.7 0.0 copy-start
  20.7 1.0 %copy-done = bf16[4,384,384]{2,1,0:T(8,128)(2,1)} copy-done((bf16[4,384,384]{2,1,0:T(8,128)(2,1)}, bf16[4,384,384]{2,1,0:T(8,128)(2,1)S(1)}, u32[]{:S(2)}) %copy-start) | copy-done | bytes 1179672
  21.7 7.5 %all-to-all-start = ((bf16[32,36,128]{2,1,0:T(8,128)(2,1)}), bf16[32,36,128]{2,1,0:T(8,128)(2,1)S(1)}, u32[]{:S(2)}, u32[]{:S(2)}) async-start(bf16[32,36,128]{2,1,0:T(8,128)(2,1)} %get-tuple-element.32), calls=%async_computation | async-start | bytes 655360 | tf_op jit(solution)/shard_map/all_to_all | solution.py:487
  29.2 3.7 %collective-permute-start.2 = (bf16[2,384,128]{2,1,0:T(8,128)(2,1)S(1)}, bf16[2,384,128]{2,1,0:T(8,128)(2,1)S(1)}, u32[]{:S(2)}, u32[]{:S(2)}) collective-permute-start(bf16[2,384,128]{2,1,0:T(8,128)(2,1)S(1)} %get-tuple-element.22.refs_2_), channel_id=1, source_target_pairs={{0,2},{2,4},{4,6},{6,8},{8,10},{10,12},{12,14},{14,16},{16,18},{18... | collective-permute-start | bytes 589832 | tf_op jit(solution)/shard_map/ppermute | solution.py:392
  32.9 1.5 %collective-permute-start.3 = (bf16[2,384,128]{2,1,0:T(8,128)(2,1)S(1)}, bf16[2,384,128]{2,1,0:T(8,128)(2,1)S(1)}, u32[]{:S(2)}, u32[]{:S(2)}) collective-permute-start(bf16[2,384,128]{2,1,0:T(8,128)(2,1)S(1)} %get-tuple-element.23.refs_1_), channel_id=1, source_target_pairs={{2,0},{4,2},{6,4},{8,6},{10,8},{12,10},{14,12},{16,14},{18,16},{20... | collective-permute-start | bytes 589832 | tf_op jit(solution)/shard_map/ppermute | solution.py:392
  34.4 0.0 copy-start.1
  34.4 1.3 %copy-done.1 = bf16[4,384,384]{2,1,0:T(8,128)(2,1)S(1)} copy-done((bf16[4,384,384]{2,1,0:T(8,128)(2,1)S(1)}, bf16[4,384,384]{2,1,0:T(8,128)(2,1)}, u32[]{:S(2)}) %copy-start.1) | copy-done | bytes 1179672
  35.6 0.0 copy-start.5
  35.6 1.1 %copy-done.5 = bf16[256,1536]{1,0:T(8,128)(2,1)S(1)} copy-done((bf16[256,1536]{1,0:T(8,128)(2,1)S(1)}, bf16[256,1536]{1,0:T(8,128)(2,1)}, u32[]{:S(2)}) %copy-start.5) | copy-done | bytes 786456
  36.8 3.9 %inputs.1 = (bf16[12,384,128]{2,1,0:T(8,128)(2,1)}, f32[4,384,128]{2,1,0:T(8,128)S(1)}) custom-call(s32[1,16]{1,0:T(1,128)} %rates_ref.7, bf16[8,384,384]{2,1,0:T(8,128)(2,1)S(1)} %get-tuple-element.24.gcat_ref, bf16[4,384,384]{2,1,0:T(8,128)(2,1)S(1)} %copy-done.1, bf16[12,384,128]{2,1,0:T(8,128)(2,1)} %bitcast.12, ...), custom_call_target="tpu_custom_call", output_to_operand_aliasing={{0}: (6, {})} | custom-call | tf_op jit(solution)/shard_map/inputs/pallas_call | solution.py:489
  40.7 0.0 copy-start.2
  40.7 0.9 %copy-done.2 = f32[4,384,128]{2,1,0:T(8,128)} copy-done((f32[4,384,128]{2,1,0:T(8,128)}, f32[4,384,128]{2,1,0:T(8,128)S(1)}, u32[]{:S(2)}) %copy-start.2) | copy-done | bytes 786456
  41.5 1.6 %collective-permute-done.2.low_ref = bf16[2,384,128]{2,1,0:T(8,128)(2,1)S(1)} collective-permute-done((bf16[2,384,128]{2,1,0:T(8,128)(2,1)S(1)}, bf16[2,384,128]{2,1,0:T(8,128)(2,1)S(1)}, u32[]{:S(2)}, u32[]{:S(2)}) %collective-permute-start.2) | collective-permute-done | bytes 196640 | tf_op jit(solution)/shard_map/ppermute | solution.py:392
  43.1 0.0 copy-start.6
  43.1 0.7 %copy-done.6 = bf16[2,384,128]{2,1,0:T(8,128)(2,1)} copy-done((bf16[2,384,128]{2,1,0:T(8,128)(2,1)}, bf16[2,384,128]{2,1,0:T(8,128)(2,1)S(1)}, u32[]{:S(2)}) %copy-start.6) | copy-done | bytes 196632
  43.8 1.4 %collective-permute-done.3.high_ref = bf16[2,384,128]{2,1,0:T(8,128)(2,1)S(1)} collective-permute-done((bf16[2,384,128]{2,1,0:T(8,128)(2,1)S(1)}, bf16[2,384,128]{2,1,0:T(8,128)(2,1)S(1)}, u32[]{:S(2)}, u32[]{:S(2)}) %collective-permute-start.3) | collective-permute-done | bytes 196640 | tf_op jit(solution)/shard_map/ppermute | solution.py:392
  45.2 0.7 %copy-done.8 = bf16[2,384,128]{2,1,0:T(8,128)(2,1)} copy-done((bf16[2,384,128]{2,1,0:T(8,128)(2,1)}, bf16[2,384,128]{2,1,0:T(8,128)(2,1)S(1)}, u32[]{:S(2)}) %copy-start.8) | copy-done | bytes 196632
  45.9 0.0 all-to-all-done.received_ref
  45.9 1.1 %copy-done.3 = f32[4,384,128]{2,1,0:T(8,128)S(1)} copy-done((f32[4,384,128]{2,1,0:T(8,128)S(1)}, f32[4,384,128]{2,1,0:T(8,128)}, u32[]{:S(2)}) %copy-start.3) | copy-done | bytes 786456
  47.0 0.9 %copy-done.7 = bf16[2,384,128]{2,1,0:T(8,128)(2,1)S(1)} copy-done((bf16[2,384,128]{2,1,0:T(8,128)(2,1)S(1)}, bf16[2,384,128]{2,1,0:T(8,128)(2,1)}, u32[]{:S(2)}) %copy-start.7) | copy-done | bytes 196632
  47.9 0.9 %copy-done.9 = bf16[2,384,128]{2,1,0:T(8,128)(2,1)S(1)} copy-done((bf16[2,384,128]{2,1,0:T(8,128)(2,1)S(1)}, bf16[2,384,128]{2,1,0:T(8,128)(2,1)}, u32[]{:S(2)}) %copy-start.9) | copy-done | bytes 196632
  48.9 2.8 %edges.1 = (bf16[12,384,128]{2,1,0:T(8,128)(2,1)}, f32[36,128]{1,0:T(8,128)}) custom-call(s32[1,16]{1,0:T(1,128)} %rates_ref.7, bf16[2,384,128]{2,1,0:T(8,128)(2,1)S(1)} %copy-done.7, bf16[2,384,128]{2,1,0:T(8,128)(2,1)S(1)} %copy-done.9, f32[4,384,128]{2,1,0:T(8,128)S(1)} %copy-done.3, ...), custom_call_target="tpu_custom_call", output_to_operand_aliasing={{0}: (7, {})} | custom-call | tf_op jit(solution)/shard_map/edges/pallas_call | solution.py:503
  (4 shorter events, 0.0 us)
Async XLA Ops:
  1.7 14.8 %collective-permute-start.1 = (bf16[2,384,128]{2,1,0:T(8,128)(2,1)S(1)}, bf16[2,384,128]{2,1,0:T(8,128)(2,1)S(1)}, u32[]{:S(2)}, u32[]{:S(2)}) collective-permute-start(bf16[2,384,128]{2,1,0:T(8,128)(2,1)S(1)} %get-tuple-element.36), channel_id=1, source_target_pairs={{2,0},{4,2},{6,4},{8,6},{10,8},{12,10},{14,12},{16,14},{18,16},{20... | collective-permute-start | bytes 589832 | tf_op jit(solution)/shard_map/ppermute | solution.py:392
  3.0 13.8 %collective-permute-start = (bf16[2,384,128]{2,1,0:T(8,128)(2,1)S(1)}, bf16[2,384,128]{2,1,0:T(8,128)(2,1)S(1)}, u32[]{:S(2)}, u32[]{:S(2)}) collective-permute-start(bf16[2,384,128]{2,1,0:T(8,128)(2,1)S(1)} %get-tuple-element.37), channel_id=1, source_target_pairs={{0,2},{2,4},{4,6},{6,8},{8,10},{10,12},{12,14},{14,16},{16,18},{18... | collective-permute-start | bytes 589832 | tf_op jit(solution)/shard_map/ppermute | solution.py:392
  16.5 4.2 %copy-start.4 = (bf16[256,1536]{1,0:T(8,128)(2,1)}, bf16[256,1536]{1,0:T(8,128)(2,1)S(1)}, u32[]{:S(2)}) copy-start(bf16[256,1536]{1,0:T(8,128)(2,1)S(1)} %get-tuple-element.29.back_ref) | copy-start | bytes 2359300
  20.7 1.0 %copy-start = (bf16[4,384,384]{2,1,0:T(8,128)(2,1)}, bf16[4,384,384]{2,1,0:T(8,128)(2,1)S(1)}, u32[]{:S(2)}) copy-start(bf16[4,384,384]{2,1,0:T(8,128)(2,1)S(1)} %get-tuple-element.28.gedge_ref) | copy-start | bytes 3538948
  21.7 24.2 %all-to-all-start = ((bf16[32,36,128]{2,1,0:T(8,128)(2,1)}), bf16[32,36,128]{2,1,0:T(8,128)(2,1)S(1)}, u32[]{:S(2)}, u32[]{:S(2)}) async-start(bf16[32,36,128]{2,1,0:T(8,128)(2,1)} %get-tuple-element.32), calls=%async_computation | async-start | bytes 655360 | tf_op jit(solution)/shard_map/all_to_all | solution.py:487
  29.2 13.9 %collective-permute-start.2 = (bf16[2,384,128]{2,1,0:T(8,128)(2,1)S(1)}, bf16[2,384,128]{2,1,0:T(8,128)(2,1)S(1)}, u32[]{:S(2)}, u32[]{:S(2)}) collective-permute-start(bf16[2,384,128]{2,1,0:T(8,128)(2,1)S(1)} %get-tuple-element.22.refs_2_), channel_id=1, source_target_pairs={{0,2},{2,4},{4,6},{6,8},{8,10},{10,12},{12,14},{14,16},{16,18},{18... | collective-permute-start | bytes 589832 | tf_op jit(solution)/shard_map/ppermute | solution.py:392
  32.9 12.3 %collective-permute-start.3 = (bf16[2,384,128]{2,1,0:T(8,128)(2,1)S(1)}, bf16[2,384,128]{2,1,0:T(8,128)(2,1)S(1)}, u32[]{:S(2)}, u32[]{:S(2)}) collective-permute-start(bf16[2,384,128]{2,1,0:T(8,128)(2,1)S(1)} %get-tuple-element.23.refs_1_), channel_id=1, source_target_pairs={{2,0},{4,2},{6,4},{8,6},{10,8},{12,10},{14,12},{16,14},{18,16},{20... | collective-permute-start | bytes 589832 | tf_op jit(solution)/shard_map/ppermute | solution.py:392
  34.4 1.3 %copy-start.1 = (bf16[4,384,384]{2,1,0:T(8,128)(2,1)S(1)}, bf16[4,384,384]{2,1,0:T(8,128)(2,1)}, u32[]{:S(2)}) copy-start(bf16[4,384,384]{2,1,0:T(8,128)(2,1)} %copy-done) | copy-start | bytes 3538948
  35.6 1.1 %copy-start.5 = (bf16[256,1536]{1,0:T(8,128)(2,1)S(1)}, bf16[256,1536]{1,0:T(8,128)(2,1)}, u32[]{:S(2)}) copy-start(bf16[256,1536]{1,0:T(8,128)(2,1)} %copy-done.4) | copy-start | bytes 2359300
  40.7 0.9 %copy-start.2 = (f32[4,384,128]{2,1,0:T(8,128)}, f32[4,384,128]{2,1,0:T(8,128)S(1)}, u32[]{:S(2)}) copy-start(f32[4,384,128]{2,1,0:T(8,128)S(1)} %get-tuple-element.31.edge_ref) | copy-start | bytes 2359300
  43.1 0.7 %copy-start.6 = (bf16[2,384,128]{2,1,0:T(8,128)(2,1)}, bf16[2,384,128]{2,1,0:T(8,128)(2,1)S(1)}, u32[]{:S(2)}) copy-start(bf16[2,384,128]{2,1,0:T(8,128)(2,1)S(1)} %collective-permute-done.2.low_ref) | copy-start | bytes 589828
  45.2 0.7 %copy-start.8 = (bf16[2,384,128]{2,1,0:T(8,128)(2,1)}, bf16[2,384,128]{2,1,0:T(8,128)(2,1)S(1)}, u32[]{:S(2)}) copy-start(bf16[2,384,128]{2,1,0:T(8,128)(2,1)S(1)} %collective-permute-done.3.high_ref) | copy-start | bytes 589828
  45.9 1.1 %copy-start.3 = (f32[4,384,128]{2,1,0:T(8,128)S(1)}, f32[4,384,128]{2,1,0:T(8,128)}, u32[]{:S(2)}) copy-start(f32[4,384,128]{2,1,0:T(8,128)} %copy-done.2) | copy-start | bytes 2359300
  47.0 0.9 %copy-start.7 = (bf16[2,384,128]{2,1,0:T(8,128)(2,1)S(1)}, bf16[2,384,128]{2,1,0:T(8,128)(2,1)}, u32[]{:S(2)}) copy-start(bf16[2,384,128]{2,1,0:T(8,128)(2,1)} %copy-done.6) | copy-start | bytes 589828
  47.9 0.9 %copy-start.9 = (bf16[2,384,128]{2,1,0:T(8,128)(2,1)S(1)}, bf16[2,384,128]{2,1,0:T(8,128)(2,1)}, u32[]{:S(2)}) copy-start(bf16[2,384,128]{2,1,0:T(8,128)(2,1)} %copy-done.8) | copy-start | bytes 589828
where the time goes:
time: 52.5 us; the launch traced here: 51.9 us
  starting transfers between devices  19.4 us (37%)
  Pallas kernels  18.6 us (35%)
  local copies, waits for them, and re-layouts  9.72 us (19%)
  waiting for transfers between devices  3.24 us (6%)
  between operations  0.9 us (2%)
    ppermute x2, starting transfers between devices, exchange(): lax.ppermute(to_next, axis, forward)  9.17 us
    unnamed x20, local copies, waits for them, and re-layouts  8.66 us
    pallas_call x1, Pallas kernels, shards(): call(first_kernel, 'first', [whole, ((2 * HALO, columns, channels), F32),...  7.97 us
    all_to_all x1, starting transfers between devices, shards(): received = lax.all_to_all(taps, axes, 0, 0, tiled=True)  7.49 us
    pallas_call x1, Pallas kernels, shards(): call(inputs_kernel, 'inputs', [whole, ((2 * HALO, columns, channels), F32...  3.87 us
    pallas_call x1, Pallas kernels, shards(): call(edges_kernel, 'edges', [whole, (part, F32)], 'svvvvvvh>hv', [pltpu.V...  2.85 us
    ppermute x2, starting transfers between devices, exchange(): lax.ppermute(to_previous, axis, backward)  2.76 us
    pallas_call x1, Pallas kernels, shards(): call(lambda *refs: taps_kernel(*refs, scale=scale), 'taps', [(share + (ch...  2.36 us
  transfers between devices with their start and end apart: 5, of which 3 were waited for; matrix products, arithmetic and copies ran while one was open for 0% of the time, Pallas kernels for 23%

commit v1 on v0

--- a/solution.py
+++ b/solution.py
@@ -13,6 +13,7 @@
 EDGE = 8
 RATES = (1, 2)
 VMEM_LIMIT = 40 * 1024 * 1024
+BUSY = 20_000_000_000
 
 F32 = jnp.float32
 BF16 = jnp.bfloat16
@@ -100,20 +101,15 @@
 def input_sums(pair, rate, rows, grads, wide_ref):
     near, low, high = pair_rows(pair, rate, rows)
     lhs = jnp.concatenate([grads(row)[...] for row in near], axis=1)
-    width = wide_ref.shape[1] // 4
-    both = lax.dot_general(
-        lhs,
-        wide_ref[:, low * width : high * width],
-        (((1,), (1,)), ((), ())),
-        preferred_element_type=F32,
-    )
+    width = wide_ref.shape[0] // 4
+    both = jnp.dot(lhs, wide_ref[low * width : high * width], preferred_element_type=F32)
     half = both.shape[1] // 2
     return both[:, :half], both[:, half:]
 
 
 def first_kernel(
     rates_ref, lists_ref, x_hbm, cot_hbm, w_hbm, bias_ref,
-    out_hbm, pre_ref, gcat_ref, xt_ref, total_ref, mask_ref, cot_ref, back_ref,
+    out_hbm, pre_ref, gcat_ref, xt_ref, total_ref, mask_ref, cot_ref, back_ref, near_ref, far_ref,
     xbuf, cbuf, wbuf, obuf, pad, xcat, wide, sems,
 ):
     rows, columns, channels = x_hbm.shape
@@ -131,16 +127,21 @@
     clear_ends(pad, rows, columns)
     loads[0].wait()
     none = jnp.zeros((channels, channels), BF16)
-    for row in range(4):
-        for out in range(2):
-            there = slice(out * channels, (out + 1) * channels)
-            for col in range(3):
-                start = (row * 3 + col) * channels
-                here = slice(start, start + channels)
+    for col in range(3):
+        there = slice(col * channels, (col + 1) * channels)
+        turned = [wbuf[tap * 3 + col].T for tap in range(3)]
+        for side in range(2):
+            near_ref[side, there] = wbuf[6 * side + col]
+            far_ref[side, there] = turned[2 - 2 * side]
+        for row in range(4):
+            start = (row * 3 + col) * channels
+            here = slice(start, start + channels)
+            for out in range(2):
+                there = slice(out * channels, (out + 1) * channels)
                 tap = row - out
                 wide[here, there] = wbuf[tap * 3 + col] if 0 <= tap < 3 else none
                 tap = out + 2 - row
-                back_ref[there, here] = wbuf[tap * 3 + col] if 0 <= tap < 3 else none
+                back_ref[here, there] = turned[tap] if 0 <= tap < 3 else none
     loads[1].wait()
     loads[2].wait()
     half_bias = 0.5 * bias_ref[...]
@@ -210,7 +211,7 @@
 
 
 def rims_kernel(
-    rates_ref, low_ref, high_ref, pre_ref, cot_ref, mask_ref, w_ref,
+    rates_ref, low_ref, high_ref, pre_ref, cot_ref, mask_ref, near_ref,
     grad_low_ref, grad_high_ref, xt_ref,
     pad, xcat,
 ):
@@ -226,9 +227,8 @@
                     value, pad, side * HALO + k, xcat.at[pl.ds(place * columns, columns)], rate
                 )
                 xt_ref[side * HALO + k] = value.T
-            taps = jnp.concatenate([w_ref[6 * side + b] for b in range(3)], axis=0)
             sums = jnp.dot(
-                xcat[: rate * columns], taps, preferred_element_type=F32
+                xcat[: rate * columns], near_ref[side], preferred_element_type=F32
             )
             for k in range(HALO):
                 half_pre = pre_ref[side * HALO + k]
@@ -242,45 +242,11 @@
     by_rate(rates_ref[0, lax.axis_index("tile")], body)
 
 
-def taps_kernel(
+def second_kernel(
     rates_ref, grad_low_ref, grad_high_ref, xt_own_ref, xt_halo_ref, total_ref,
-    tap_ref, gcat_ref,
-    pad, flat, *, scale,
-):
-    _, columns, channels = grad_low_ref.shape
-    rows = xt_own_ref.shape[0]
-    clear_ends(pad, 2 * HALO, columns)
-
-    def flipped(row):
-        if row < 0:
-            return xt_halo_ref[row + HALO]
-        return xt_own_ref[row] if row < rows else xt_halo_ref[row - rows + HALO]
-
-    def body(rate):
-        grads = []
-        for side, ref in enumerate((grad_low_ref, grad_high_ref)):
-            for k in range(HALO):
-                slot = side * HALO + k
-                spread(ref[k], pad, slot, gcat_ref.at[slot], -rate)
-                grads.append((k + side * (rows - HALO), gcat_ref.at[slot]))
-        total = (total_ref[...] + tap_sums(grads, flipped, rate)) * scale
-        for a in range(3):
-            for b in range(3):
-                start = (a * 3 + b) * channels
-                flat[start : start + channels] = total[
-                    a * channels : (a + 1) * channels, b * channels : (b + 1) * channels
-                ]
-
-    by_rate(rates_ref[0, lax.axis_index("tile")], body)
-    share = tap_ref.shape[1]
-    for part in range(tap_ref.shape[0]):
-        tap_ref[part] = flat[part * share : (part + 1) * share].astype(BF16)
-
-
-def inputs_kernel(
-    rates_ref, gcat_ref, gedge_ref, cot_hbm, mask_ref, back_ref, held_hbm,
-    out_hbm, edge_ref,
-    cbuf, obuf, sems,
+    gcat_ref, cot_hbm, mask_ref, back_ref, held_hbm,
+    out_hbm, edge_ref, tap_ref,
+    cbuf, obuf, pad, gedge, flat, sems, *, scale,
 ):
     del held_hbm
     rows, columns, channels = cot_hbm.shape
@@ -303,17 +269,29 @@
     ]
     for load in loads:
         load.start()
+    clear_ends(pad, 2 * HALO, columns)
     for load in loads:
         load.wait()
 
+    def flipped(row):
+        if row < 0:
+            return xt_halo_ref[row + HALO]
+        return xt_own_ref[row] if row < rows else xt_halo_ref[row - rows + HALO]
+
     def grads(row):
         if row < HALO:
-            return gedge_ref.at[row]
+            return gedge.at[row]
         if row < rows - HALO:
             return gcat_ref.at[row - HALO]
-        return gedge_ref.at[row - (rows - 2 * HALO)]
+        return gedge.at[row - (rows - 2 * HALO)]
 
     def body(rate):
+        edges = []
+        for side, ref in enumerate((grad_low_ref, grad_high_ref)):
+            for k in range(HALO):
+                slot = side * HALO + k
+                spread(ref[k], pad, slot, gedge.at[slot], -rate)
+                edges.append((k + side * (rows - HALO), gedge.at[slot]))
         for side in range(2):
             start = side * (rows - around)
             for pair in row_pairs(rate, range(start, start + around)):
@@ -326,16 +304,25 @@
                     else:
                         here = row if side == 0 else row - (rows - around)
                         edge_ref[here] = value
+            stores[side].start()
+        total = (total_ref[...] + tap_sums(edges, flipped, rate)) * scale
+        for a in range(3):
+            for b in range(3):
+                start = (a * 3 + b) * channels
+                flat[start : start + channels] = total[
+                    a * channels : (a + 1) * channels, b * channels : (b + 1) * channels
+                ]
 
     by_rate(rates_ref[0, lax.axis_index("tile")], body)
-    for store in stores:
-        store.start()
+    share = tap_ref.shape[1]
+    for part in range(tap_ref.shape[0]):
+        tap_ref[part] = flat[part * share : (part + 1) * share].astype(BF16)
     for store in stores:
         store.wait()
 
 
 def edges_kernel(
-    rates_ref, low_ref, high_ref, edge_ref, mask_ref, w_ref, received_ref, held_hbm,
+    rates_ref, low_ref, high_ref, edge_ref, mask_ref, far_ref, received_ref, held_hbm,
     out_hbm, sum_ref,
     obuf, pad, gcat, sems,
 ):
@@ -361,12 +348,8 @@
             spread(
                 ref[k], pad, side * HALO + k, gcat.at[side, pl.ds(place * columns, columns)], -rate
             )
-        taps = jnp.concatenate([w_ref[6 * (1 - side) + b] for b in range(3)], axis=1)
-        sums = lax.dot_general(
-            gcat[side, : rate * columns],
-            taps,
-            (((1,), (1,)), ((), ())),
-            preferred_element_type=F32,
+        sums = jnp.dot(
+            gcat[side, : rate * columns], far_ref[side], preferred_element_type=F32
         )
         for k in range(HALO):
             value = edge_ref[side * HALO + k]
@@ -392,7 +375,7 @@
     return lax.ppermute(to_next, axis, forward), lax.ppermute(to_previous, axis, backward)
 
 
-def call(kernel, name, outs, specs, scratch, aliases=None):
+def call(kernel, name, outs, specs, scratch, aliases=None, flops=0):
     memory = {"s": pltpu.SMEM, "v": pltpu.VMEM, "h": pltpu.HBM}
     ins, results = (
         [pl.BlockSpec(memory_space=memory[letter]) for letter in part] for part in specs.split(">")
@@ -405,7 +388,7 @@
         out_specs=tuple(results),
         scratch_shapes=scratch,
         input_output_aliases=aliases or {},
-        cost_estimate=pl.CostEstimate(flops=0, bytes_accessed=0, transcendentals=0),
+        cost_estimate=pl.CostEstimate(flops=flops, bytes_accessed=0, transcendentals=0),
         compiler_params=pltpu.CompilerParams(vmem_limit_bytes=VMEM_LIMIT),
     )
 
@@ -431,7 +414,7 @@
 
     low, high = exchange(x[rows - HALO :], x[:HALO], "tile")
 
-    held, pre, gcat, xt, total, mask, cot_edge, back = call(
+    held, pre, gcat, xt, total, mask, cot_edge, back, near, far = call(
         first_kernel,
         "first",
         [
@@ -442,9 +425,11 @@
             ((wide_row, wide_row), F32),
             ((3, columns, channels), BF16),
             ((2 * HALO, columns, channels), BF16),
-            ((2 * channels, 4 * wide_row), BF16),
+            ((4 * wide_row, 2 * channels), BF16),
+            ((2, wide_row, channels), BF16),
+            ((2, wide_row, channels), BF16),
         ],
-        "svhhhv>hvvvvvvv",
+        "svhhhv>hvvvvvvvvv",
         [
             pltpu.VMEM((rows, columns, channels), BF16),
             pltpu.VMEM((rows, columns, channels), BF16),
@@ -455,6 +440,7 @@
             pltpu.VMEM((4 * wide_row, 2 * channels), BF16),
             pltpu.SemaphoreType.DMA((4,)),
         ],
+        flops=BUSY,
     )(dilations, lists, in_hbm(x), cot, weight, bias)
 
     grad_low, grad_high, xt_halo = call(
@@ -467,7 +453,7 @@
         ],
         "svvvvvv>vvv",
         [pads(2 * HALO), pltpu.VMEM((HALO * columns, wide_row), BF16)],
-    )(dilations, low, high, pre, cot_edge, mask, weight)
+    )(dilations, low, high, pre, cot_edge, mask, near)
 
     from_low, from_high = exchange(grad_high, grad_low, "tile")
 
@@ -475,29 +461,25 @@
     direct = tap_rows % devices == 0
     share = (devices, tap_rows // devices) if direct else (1, tap_rows)
     scale = 1.0 / math.sqrt(devices * lists.shape[1] * TILE * TILE)
-    taps, gedge = call(
-        lambda *refs: taps_kernel(*refs, scale=scale),
-        "taps",
-        [(share + (channels,), BF16), ((2 * HALO, columns, wide_row), BF16)],
-        "svvvvv>vv",
-        [pads(2 * HALO), pltpu.VMEM((tap_rows, channels), F32)],
-    )(dilations, grad_low, grad_high, xt, xt_halo, total)
+    held, edge, taps = call(
+        lambda *refs: second_kernel(*refs, scale=scale),
+        "second",
+        [whole, ((2 * HALO, columns, channels), F32), (share + (channels,), BF16)],
+        "svvvvvvhvvh>hvv",
+        [
+            pltpu.VMEM((4 * HALO, columns, channels), BF16),
+            pltpu.VMEM((2 * HALO, columns, channels), BF16),
+            pads(2 * HALO),
+            pltpu.VMEM((2 * HALO, columns, wide_row), BF16),
+            pltpu.VMEM((tap_rows, channels), F32),
+            pltpu.SemaphoreType.DMA((4,)),
+        ],
+        {10: 0},
+        flops=BUSY,
+    )(dilations, grad_low, grad_high, xt, xt_halo, total, gcat, cot, mask, back, held)
     if not direct:
         taps = taps.reshape(devices, -1)
     received = lax.all_to_all(taps, axes, 0, 0, tiled=True)
-
-    held, edge = call(
-        inputs_kernel,
-        "inputs",
-        [whole, ((2 * HALO, columns, channels), F32)],
-        "svvhvvh>hv",
-        [
-            pltpu.VMEM((4 * HALO, columns, channels), BF16),
-            pltpu.VMEM((2 * HALO, columns, channels), BF16),
-            pltpu.SemaphoreType.DMA((4,)),
-        ],
-        {6: 0},
-    )(dilations, gcat, gedge, cot, mask, back, held)
 
     part = received.shape[1:] if direct else (8, LANES)
     input_grad, summed = call(
@@ -512,7 +494,7 @@
             pltpu.SemaphoreType.DMA((2,)),
         ],
         {7: 0},
-    )(dilations, from_low, from_high, edge, mask, weight, received if direct else mask, held)
+    )(dilations, from_low, from_high, edge, mask, far, received if direct else mask, held)
     if not direct:
         summed = jnp.sum(received.astype(F32), axis=0)
     return (input_grad[None], summed.reshape(-1))

time: 52.5 us -> 48.8 us (0.930)
  local copies, waits for them, and re-layouts: 9.72 us -> 1.05 us
  waiting for transfers between devices: 3.24 us -> 11.3 us
  Pallas kernels: 18.6 us -> 16.5 us
  starting transfers between devices: 19.4 us -> 18.7 us
    unnamed x20 -> x0, local copies, waits for them, and re-layouts: 8.66 us -> none
    ppermute x2, waiting for transfers between devices: 1.87 us -> 9.22 us  [exchange(): lax.ppermute(to_next, axis, forward)]
    pallas_call x2 -> x1, Pallas kernels: 6.24 us -> 4.76 us  [shards(): call(lambda *refs: second_kernel(*refs, scale=scale), 'second', [whole, (...]
    ppermute x2, waiting for transfers between devices: 1.36 us -> 2.04 us  [exchange(): lax.ppermute(to_previous, axis, backward)]
  transfers between devices with their start and end apart: 5 -> 5, of which waited for: 3 -> 3; matrix products, arithmetic and copies ran while one was open for 0% -> 0% of each run, Pallas kernels for 23% -> 16%
where the time goes in v1:
time: 48.8 us; the launch traced here: 48.4 us
  starting transfers between devices  18.7 us (38%)
  Pallas kernels  16.5 us (34%)
  waiting for transfers between devices  11.3 us (23%)
  local copies, waits for them, and re-layouts  1.05 us (2%)
  between operations  0.87 us (2%)
    ppermute x2, waiting for transfers between devices, exchange(): lax.ppermute(to_next, axis, forward)  9.22 us
    ppermute x2, starting transfers between devices, exchange(): lax.ppermute(to_next, axis, forward)  9.17 us
    pallas_call x1, Pallas kernels, shards(): call(first_kernel, 'first', [whole, ((2 * HALO, columns, channels), F32),...  7.98 us
    all_to_all x1, starting transfers between devices, shards(): received = lax.all_to_all(taps, axes, 0, 0, tiled=True)  6.97 us
    pallas_call x1, Pallas kernels, shards(): call(lambda *refs: second_kernel(*refs, scale=scale), 'second', [whole, (...  4.76 us
    ppermute x2, starting transfers between devices, exchange(): lax.ppermute(to_previous, axis, backward)  2.58 us
    pallas_call x1, Pallas kernels, shards(): call(edges_kernel, 'edges', [whole, (part, F32)], 'svvvvvvh>hv', [pltpu.V...  2.52 us
    ppermute x2, waiting for transfers between devices, exchange(): lax.ppermute(to_previous, axis, backward)  2.04 us
  transfers between devices with their start and end apart: 5, of which 3 were waited for; matrix products, arithmetic and copies ran while one was open for 0% of the time, Pallas kernels for 16%

profile of v1, /device:TPU:0, one launch (start us, length us, event | category | flops | bytes accessed | tf_op | source)
XLA Modules:
  0.0 48.4 jit_solution(18319751050028108478)
XLA Ops:
  0.6 1.1 %slice_bitcast_fusion = (bf16[2,384,128]{2,1,0:T(8,128)(2,1)S(1)}, bf16[2,384,128]{2,1,0:T(8,128)(2,1)S(1)}) fusion(bf16[1,12,384,128]{3,2,1,0:T(8,128)(2,1)} %param.7), kind=kLoop, calls=%fused_computation | loop fusion | bytes 786432 | tf_op jit(solution)/shard_map/slice | solution.py:415
  1.7 1.3 %collective-permute-start.1 = (bf16[2,384,128]{2,1,0:T(8,128)(2,1)S(1)}, bf16[2,384,128]{2,1,0:T(8,128)(2,1)S(1)}, u32[]{:S(2)}, u32[]{:S(2)}) collective-permute-start(bf16[2,384,128]{2,1,0:T(8,128)(2,1)S(1)} %get-tuple-element.38), channel_id=1, source_target_pairs={{2,0},{4,2},{6,4},{8,6},{10,8},{12,10},{14,12},{16,14},{18,16},{20... | collective-permute-start | bytes 589832 | tf_op jit(solution)/shard_map/ppermute | solution.py:375
  3.0 5.5 %collective-permute-start = (bf16[2,384,128]{2,1,0:T(8,128)(2,1)S(1)}, bf16[2,384,128]{2,1,0:T(8,128)(2,1)S(1)}, u32[]{:S(2)}, u32[]{:S(2)}) collective-permute-start(bf16[2,384,128]{2,1,0:T(8,128)(2,1)S(1)} %get-tuple-element.39), channel_id=1, source_target_pairs={{0,2},{2,4},{4,6},{6,8},{8,10},{10,12},{12,14},{14,16},{16,18},{18... | collective-permute-start | bytes 589832 | tf_op jit(solution)/shard_map/ppermute | solution.py:375
  8.5 8.0 %first.1 = (bf16[12,384,128]{2,1,0:T(8,128)(2,1)}, f32[4,384,128]{2,1,0:T(8,128)S(1)}, bf16[8,384,384]{2,1,0:T(8,128)(2,1)S(1)}, bf16[12,128,384]{2,1,0:T(8,128)...) custom-call(s32[1,16]{1,0:T(1,128)} %rates_ref.5, ...), custom_call_target="tpu_custom_call" | custom-call | flops 20000000000 | tf_op jit(solution)/shard_map/first/pallas_call | solution.py:417
  16.5 0.0 collective-permute-done.1.high_ref
  16.5 0.3 collective-permute-done.low_ref
  16.7 1.2 %rims.1 = (bf16[2,384,128]{2,1,0:T(8,128)(2,1)S(1)}, bf16[2,384,128]{2,1,0:T(8,128)(2,1)S(1)}, bf16[4,128,384]{2,1,0:T(8,128)(2,1)S(1)}) custom-call(s32[1,16]{1,0:T(1,128)} %rates_ref.5, bf16[2,384,128]{2,1,0:T(8,128)(2,1)S(1)} %collective-permute-done.low_ref, bf16[2,384,128]{2,1,0:T(8,128)(2,1)S(1)} %collective-permute-done.1.high_ref, ...), custom_call_target="tpu_custom_call" | custom-call | tf_op jit(solution)/shard_map/rims/pallas_call | solution.py:446
  18.0 4.8 %second.1 = (bf16[12,384,128]{2,1,0:T(8,128)(2,1)}, f32[4,384,128]{2,1,0:T(8,128)S(1)}, bf16[32,36,128]{2,1,0:T(8,128)(2,1)}) custom-call(s32[1,16]{1,0:T(1,128)} %rates_ref.5, bf16[2,384,128]{2,1,0:T(8,128)(2,1)S(1)} %get-tuple-element.25.refs_1_, bf16[2,384,128]{2,1,0:T(8,128)(2,1)S(1)} %get-tuple-element.24.refs_2_, ...), custom_call_target="tpu_custom_call", output_to_operand_aliasing={{0}: (10, {})} | custom-call | flops 20000000000 | tf_op jit(solution)/shard_map/second/pallas_call | solution.py:464
  22.8 7.0 %all-to-all-start = ((bf16[32,36,128]{2,1,0:T(8,128)(2,1)}), bf16[32,36,128]{2,1,0:T(8,128)(2,1)S(1)}, u32[]{:S(2)}, u32[]{:S(2)}) async-start(bf16[32,36,128]{2,1,0:T(8,128)(2,1)} %get-tuple-element.34), calls=%async_computation | async-start | bytes 655360 | tf_op jit(solution)/shard_map/all_to_all | solution.py:482
  29.7 3.7 %collective-permute-start.2 = (bf16[2,384,128]{2,1,0:T(8,128)(2,1)S(1)}, bf16[2,384,128]{2,1,0:T(8,128)(2,1)S(1)}, u32[]{:S(2)}, u32[]{:S(2)}) collective-permute-start(bf16[2,384,128]{2,1,0:T(8,128)(2,1)S(1)} %get-tuple-element.24.refs_2_), channel_id=1, source_target_pairs={{0,2},{2,4},{4,6},{6,8},{8,10},{10,12},{12,14},{14,16},{16,18},{18... | collective-permute-start | bytes 589832 | tf_op jit(solution)/shard_map/ppermute | solution.py:375
  33.4 1.3 %collective-permute-start.3 = (bf16[2,384,128]{2,1,0:T(8,128)(2,1)S(1)}, bf16[2,384,128]{2,1,0:T(8,128)(2,1)S(1)}, u32[]{:S(2)}, u32[]{:S(2)}) collective-permute-start(bf16[2,384,128]{2,1,0:T(8,128)(2,1)S(1)} %get-tuple-element.25.refs_1_), channel_id=1, source_target_pairs={{2,0},{4,2},{6,4},{8,6},{10,8},{12,10},{14,12},{16,14},{18,16},{20... | collective-permute-start | bytes 589832 | tf_op jit(solution)/shard_map/ppermute | solution.py:375
  34.7 8.9 %collective-permute-done.2.low_ref = bf16[2,384,128]{2,1,0:T(8,128)(2,1)S(1)} collective-permute-done((bf16[2,384,128]{2,1,0:T(8,128)(2,1)S(1)}, bf16[2,384,128]{2,1,0:T(8,128)(2,1)S(1)}, u32[]{:S(2)}, u32[]{:S(2)}) %collective-permute-start.2) | collective-permute-done | bytes 196640 | tf_op jit(solution)/shard_map/ppermute | solution.py:375
  43.7 2.0 %collective-permute-done.3.high_ref = bf16[2,384,128]{2,1,0:T(8,128)(2,1)S(1)} collective-permute-done((bf16[2,384,128]{2,1,0:T(8,128)(2,1)S(1)}, bf16[2,384,128]{2,1,0:T(8,128)(2,1)S(1)}, u32[]{:S(2)}, u32[]{:S(2)}) %collective-permute-start.3) | collective-permute-done | bytes 196640 | tf_op jit(solution)/shard_map/ppermute | solution.py:375
  45.7 0.0 all-to-all-done.received_ref
  45.7 2.5 %edges.1 = (bf16[12,384,128]{2,1,0:T(8,128)(2,1)}, f32[36,128]{1,0:T(8,128)}) custom-call(s32[1,16]{1,0:T(1,128)} %rates_ref.5, bf16[2,384,128]{2,1,0:T(8,128)(2,1)S(1)} %collective-permute-done.2.low_ref, bf16[2,384,128]{2,1,0:T(8,128)(2,1)S(1)} %collective-permute-done.3.high_ref, ...), custom_call_target="tpu_custom_call", output_to_operand_aliasing={{0}: (7, {})} | custom-call | tf_op jit(solution)/shard_map/edges/pallas_call | solution.py:485
Async XLA Ops:
  1.7 14.8 %collective-permute-start.1 = (bf16[2,384,128]{2,1,0:T(8,128)(2,1)S(1)}, bf16[2,384,128]{2,1,0:T(8,128)(2,1)S(1)}, u32[]{:S(2)}, u32[]{:S(2)}) collective-permute-start(bf16[2,384,128]{2,1,0:T(8,128)(2,1)S(1)} %get-tuple-element.38), channel_id=1, source_target_pairs={{2,0},{4,2},{6,4},{8,6},{10,8},{12,10},{14,12},{16,14},{18,16},{20... | collective-permute-start | bytes 589832 | tf_op jit(solution)/shard_map/ppermute | solution.py:375
  3.0 13.8 %collective-permute-start = (bf16[2,384,128]{2,1,0:T(8,128)(2,1)S(1)}, bf16[2,384,128]{2,1,0:T(8,128)(2,1)S(1)}, u32[]{:S(2)}, u32[]{:S(2)}) collective-permute-start(bf16[2,384,128]{2,1,0:T(8,128)(2,1)S(1)} %get-tuple-element.39), channel_id=1, source_target_pairs={{0,2},{2,4},{4,6},{6,8},{8,10},{10,12},{12,14},{14,16},{16,18},{18... | collective-permute-start | bytes 589832 | tf_op jit(solution)/shard_map/ppermute | solution.py:375
  22.8 23.0 %all-to-all-start = ((bf16[32,36,128]{2,1,0:T(8,128)(2,1)}), bf16[32,36,128]{2,1,0:T(8,128)(2,1)S(1)}, u32[]{:S(2)}, u32[]{:S(2)}) async-start(bf16[32,36,128]{2,1,0:T(8,128)(2,1)} %get-tuple-element.34), calls=%async_computation | async-start | bytes 655360 | tf_op jit(solution)/shard_map/all_to_all | solution.py:482
  29.7 13.9 %collective-permute-start.2 = (bf16[2,384,128]{2,1,0:T(8,128)(2,1)S(1)}, bf16[2,384,128]{2,1,0:T(8,128)(2,1)S(1)}, u32[]{:S(2)}, u32[]{:S(2)}) collective-permute-start(bf16[2,384,128]{2,1,0:T(8,128)(2,1)S(1)} %get-tuple-element.24.refs_2_), channel_id=1, source_target_pairs={{0,2},{2,4},{4,6},{6,8},{8,10},{10,12},{12,14},{14,16},{16,18},{18... | collective-permute-start | bytes 589832 | tf_op jit(solution)/shard_map/ppermute | solution.py:375
  33.4 12.3 %collective-permute-start.3 = (bf16[2,384,128]{2,1,0:T(8,128)(2,1)S(1)}, bf16[2,384,128]{2,1,0:T(8,128)(2,1)S(1)}, u32[]{:S(2)}, u32[]{:S(2)}) collective-permute-start(bf16[2,384,128]{2,1,0:T(8,128)(2,1)S(1)} %get-tuple-element.25.refs_1_), channel_id=1, source_target_pairs={{2,0},{4,2},{6,4},{8,6},{10,8},{12,10},{14,12},{16,14},{18,16},{20... | collective-permute-start | bytes 589832 | tf_op jit(solution)/shard_map/ppermute | solution.py:375

commit v2 on v1

--- a/solution.py
+++ b/solution.py
@@ -322,8 +322,8 @@
 
 
 def edges_kernel(
-    rates_ref, low_ref, high_ref, edge_ref, mask_ref, far_ref, received_ref, held_hbm,
-    out_hbm, sum_ref,
+    rates_ref, low_ref, high_ref, edge_ref, mask_ref, far_ref, held_hbm,
+    out_hbm,
     obuf, pad, gcat, sems,
 ):
     del held_hbm
@@ -362,8 +362,6 @@
     for side in range(2):
         by_rate(rates_ref[0, near[side]], lambda rate, side=side: one_side(side, rate))
         stores[side].start()
-    if sum_ref.shape == received_ref.shape[1:]:
-        sum_ref[...] = jnp.sum(received_ref[...].astype(F32), axis=0)
     for store in stores:
         store.wait()
 
@@ -481,22 +479,21 @@
         taps = taps.reshape(devices, -1)
     received = lax.all_to_all(taps, axes, 0, 0, tiled=True)
 
-    part = received.shape[1:] if direct else (8, LANES)
-    input_grad, summed = call(
+    (input_grad,) = call(
         edges_kernel,
         "edges",
-        [whole, (part, F32)],
-        "svvvvvvh>hv",
+        [whole],
+        "svvvvvh>h",
         [
             pltpu.VMEM((2 * HALO, columns, channels), BF16),
             pads(2 * HALO),
             pltpu.VMEM((2, HALO * columns, wide_row), BF16),
             pltpu.SemaphoreType.DMA((2,)),
         ],
-        {7: 0},
-    )(dilations, from_low, from_high, edge, mask, far, received if direct else mask, held)
-    if not direct:
-        summed = jnp.sum(received.astype(F32), axis=0)
+        {6: 0},
+        flops=BUSY,
+    )(dilations, from_low, from_high, edge, mask, far, held)
+    summed = jnp.sum(received.astype(F32), axis=0)
     return (input_grad[None], summed.reshape(-1))
 
 

time: 48.8 us -> 48.6 us (level)
  waiting for transfers between devices: 11.3 us -> 10.1 us
  starting transfers between devices: 18.7 us -> 19.7 us
  other arithmetic: 0 us -> 0.67 us
  Pallas kernels: 16.5 us -> 16 us
    all_to_all x1, waiting for transfers between devices: 0.01 us -> 9.96 us  [shards(): received = lax.all_to_all(taps, axes, 0, 0, tiled=True)]
    ppermute x2, waiting for transfers between devices: 9.22 us -> 0.11 us  [exchange(): lax.ppermute(to_next, axis, forward)]
    ppermute x2, waiting for transfers between devices: 2.04 us -> 0.01 us  [exchange(): lax.ppermute(to_previous, axis, backward)]
    ppermute x2, starting transfers between devices: 9.17 us -> 9.86 us  [exchange(): lax.ppermute(to_next, axis, forward)]
    reduce_sum x0 -> x1, other arithmetic: none -> 0.67 us  [shards(): summed = jnp.sum(received.astype(F32), axis=0)]
    pallas_call x1, Pallas kernels: 2.52 us -> 2 us  [shards(): call(edges_kernel, 'edges', [whole], 'svvvvvh>h', [pltpu.VMEM((2 * HALO,...]
  transfers between devices with their start and end apart: 5 -> 5, of which waited for: 3 -> 2; matrix products, arithmetic and copies ran while one was open for 0% -> 0% of each run, Pallas kernels for 16% -> 30%
where the time goes in v2:
time: 48.6 us; the launch traced here: 48.2 us
  starting transfers between devices  19.7 us (41%)
  Pallas kernels  16 us (33%)
  waiting for transfers between devices  10.1 us (21%)
  local copies, waits for them, and re-layouts  1.05 us (2%)
  between operations  0.73 us (2%)
  other arithmetic  0.67 us (1%)
    all_to_all x1, waiting for transfers between devices, shards(): received = lax.all_to_all(taps, axes, 0, 0, tiled=True)  9.96 us
    ppermute x2, starting transfers between devices, exchange(): lax.ppermute(to_next, axis, forward)  9.86 us
    pallas_call x1, Pallas kernels, shards(): call(first_kernel, 'first', [whole, ((2 * HALO, columns, channels), F32),...  8.15 us
    all_to_all x1, starting transfers between devices, shards(): received = lax.all_to_all(taps, axes, 0, 0, tiled=True)  7.24 us
    pallas_call x1, Pallas kernels, shards(): call(lambda *refs: second_kernel(*refs, scale=scale), 'second', [whole, (...  4.47 us
    ppermute x2, starting transfers between devices, exchange(): lax.ppermute(to_previous, axis, backward)  2.58 us
    pallas_call x1, Pallas kernels, shards(): call(edges_kernel, 'edges', [whole], 'svvvvvh>h', [pltpu.VMEM((2 * HALO,...  2 us
    pallas_call x1, Pallas kernels, shards(): call(rims_kernel, 'rims', [((HALO, columns, channels), BF16), ((HALO, col...  1.42 us
  transfers between devices with their start and end apart: 5, of which 2 were waited for; matrix products, arithmetic and copies ran while one was open for 0% of the time, Pallas kernels for 30%

profile of v2, /device:TPU:0, one launch (start us, length us, event | category | flops | bytes accessed | tf_op | source)
XLA Modules:
  0.0 48.2 jit_solution(6067317786992709130)
XLA Ops:
  0.6 1.1 %slice_bitcast_fusion = (bf16[2,384,128]{2,1,0:T(8,128)(2,1)S(1)}, bf16[2,384,128]{2,1,0:T(8,128)(2,1)S(1)}) fusion(bf16[1,12,384,128]{3,2,1,0:T(8,128)(2,1)} %param.7), kind=kLoop, calls=%fused_computation.1 | loop fusion | bytes 786432 | tf_op jit(solution)/shard_map/slice | solution.py:413
  1.7 1.3 %collective-permute-start.1 = (bf16[2,384,128]{2,1,0:T(8,128)(2,1)S(1)}, bf16[2,384,128]{2,1,0:T(8,128)(2,1)S(1)}, u32[]{:S(2)}, u32[]{:S(2)}) collective-permute-start(bf16[2,384,128]{2,1,0:T(8,128)(2,1)S(1)} %get-tuple-element.34), channel_id=1, source_target_pairs={{2,0},{4,2},{6,4},{8,6},{10,8},{12,10},{14,12},{16,14},{18,16},{20... | collective-permute-start | bytes 589832 | tf_op jit(solution)/shard_map/ppermute | solution.py:373
  3.0 5.5 %collective-permute-start = (bf16[2,384,128]{2,1,0:T(8,128)(2,1)S(1)}, bf16[2,384,128]{2,1,0:T(8,128)(2,1)S(1)}, u32[]{:S(2)}, u32[]{:S(2)}) collective-permute-start(bf16[2,384,128]{2,1,0:T(8,128)(2,1)S(1)} %get-tuple-element.35), channel_id=1, source_target_pairs={{0,2},{2,4},{4,6},{6,8},{8,10},{10,12},{12,14},{14,16},{16,18},{18... | collective-permute-start | bytes 589832 | tf_op jit(solution)/shard_map/ppermute | solution.py:373
  8.5 8.1 %first.1 = (bf16[12,384,128]{2,1,0:T(8,128)(2,1)}, f32[4,384,128]{2,1,0:T(8,128)S(1)}, bf16[8,384,384]{2,1,0:T(8,128)(2,1)S(1)}, bf16[12,128,384]{2,1,0:T(8,128)...) custom-call(s32[1,16]{1,0:T(1,128)} %rates_ref.5, ...), custom_call_target="tpu_custom_call" | custom-call | flops 20000000000 | tf_op jit(solution)/shard_map/first/pallas_call | solution.py:415
  16.6 0.0 collective-permute-done.1.high_ref
  16.6 0.1 collective-permute-done.low_ref
  16.7 1.4 %rims.1 = (bf16[2,384,128]{2,1,0:T(8,128)(2,1)S(1)}, bf16[2,384,128]{2,1,0:T(8,128)(2,1)S(1)}, bf16[4,128,384]{2,1,0:T(8,128)(2,1)S(1)}) custom-call(s32[1,16]{1,0:T(1,128)} %rates_ref.5, bf16[2,384,128]{2,1,0:T(8,128)(2,1)S(1)} %collective-permute-done.low_ref, bf16[2,384,128]{2,1,0:T(8,128)(2,1)S(1)} %collective-permute-done.1.high_ref, ...), custom_call_target="tpu_custom_call" | custom-call | tf_op jit(solution)/shard_map/rims/pallas_call | solution.py:444
  18.2 4.4 %collective-permute-start.2 = (bf16[2,384,128]{2,1,0:T(8,128)(2,1)S(1)}, bf16[2,384,128]{2,1,0:T(8,128)(2,1)S(1)}, u32[]{:S(2)}, u32[]{:S(2)}) collective-permute-start(bf16[2,384,128]{2,1,0:T(8,128)(2,1)S(1)} %get-tuple-element.22.refs_2_), channel_id=1, source_target_pairs={{0,2},{2,4},{4,6},{6,8},{8,10},{10,12},{12,14},{14,16},{16,18},{18... | collective-permute-start | bytes 589832 | tf_op jit(solution)/shard_map/ppermute | solution.py:373
  22.6 1.3 %collective-permute-start.3 = (bf16[2,384,128]{2,1,0:T(8,128)(2,1)S(1)}, bf16[2,384,128]{2,1,0:T(8,128)(2,1)S(1)}, u32[]{:S(2)}, u32[]{:S(2)}) collective-permute-start(bf16[2,384,128]{2,1,0:T(8,128)(2,1)S(1)} %get-tuple-element.23.refs_1_), channel_id=1, source_target_pairs={{2,0},{4,2},{6,4},{8,6},{10,8},{12,10},{14,12},{16,14},{18,16},{20... | collective-permute-start | bytes 589832 | tf_op jit(solution)/shard_map/ppermute | solution.py:373
  23.9 4.5 %second.1 = (bf16[12,384,128]{2,1,0:T(8,128)(2,1)}, f32[4,384,128]{2,1,0:T(8,128)S(1)}, bf16[32,36,128]{2,1,0:T(8,128)(2,1)}) custom-call(s32[1,16]{1,0:T(1,128)} %rates_ref.5, bf16[2,384,128]{2,1,0:T(8,128)(2,1)S(1)} %get-tuple-element.23.refs_1_, bf16[2,384,128]{2,1,0:T(8,128)(2,1)S(1)} %get-tuple-element.22.refs_2_, ...), custom_call_target="tpu_custom_call", output_to_operand_aliasing={{0}: (10, {})} | custom-call | flops 20000000000 | tf_op jit(solution)/shard_map/second/pallas_call | solution.py:462
  28.3 7.2 %all-to-all-start = ((bf16[32,36,128]{2,1,0:T(8,128)(2,1)}), bf16[32,36,128]{2,1,0:T(8,128)(2,1)S(1)}, u32[]{:S(2)}, u32[]{:S(2)}) async-start(bf16[32,36,128]{2,1,0:T(8,128)(2,1)} %get-tuple-element.33), calls=%async_computation | async-start | bytes 655360 | tf_op jit(solution)/shard_map/all_to_all | solution.py:480
  35.6 0.0 collective-permute-done.2.low_ref
  35.6 0.0 collective-permute-done.3.high_ref
  35.6 2.0 %edges.1 = bf16[12,384,128]{2,1,0:T(8,128)(2,1)} custom-call(s32[1,16]{1,0:T(1,128)} %rates_ref.5, bf16[2,384,128]{2,1,0:T(8,128)(2,1)S(1)} %collective-permute-done.2.low_ref, bf16[2,384,128]{2,1,0:T(8,128)(2,1)S(1)} %collective-permute-done.3.high_ref, f32[4,384,128]{2,1,0:T(8,128)S(1)} %get-tuple-element.30.edge_ref, ...), custom_call_target="tpu_custom_call", output_to_operand_aliasing={{}: (6, {})} | custom-call | flops 20000000000 | tf_op jit(solution)/shard_map/edges/pallas_call | solution.py:482
  37.6 10.0 %all-to-all-done = bf16[32,36,128]{2,1,0:T(8,128)(2,1)S(1)} async-done(((bf16[32,36,128]{2,1,0:T(8,128)(2,1)}), bf16[32,36,128]{2,1,0:T(8,128)(2,1)S(1)}, u32[]{:S(2)}, u32[]{:S(2)}) %all-to-all-start) | async-done | bytes 294944 | tf_op jit(solution)/shard_map/all_to_all | solution.py:480
  47.6 0.7 %convert_reduce_fusion = f32[36,128]{1,0:T(8,128)} fusion(bf16[32,36,128]{2,1,0:T(8,128)(2,1)S(1)} %all-to-all-done), kind=kLoop, calls=%fused_computation | loop fusion | flops 290304 | bytes 313344 | tf_op jit(solution)/shard_map/reduce_sum | solution.py:496
Async XLA Ops:
  1.7 14.9 %collective-permute-start.1 = (bf16[2,384,128]{2,1,0:T(8,128)(2,1)S(1)}, bf16[2,384,128]{2,1,0:T(8,128)(2,1)S(1)}, u32[]{:S(2)}, u32[]{:S(2)}) collective-permute-start(bf16[2,384,128]{2,1,0:T(8,128)(2,1)S(1)} %get-tuple-element.34), channel_id=1, source_target_pairs={{2,0},{4,2},{6,4},{8,6},{10,8},{12,10},{14,12},{16,14},{18,16},{20... | collective-permute-start | bytes 589832 | tf_op jit(solution)/shard_map/ppermute | solution.py:373
  3.0 13.8 %collective-permute-start = (bf16[2,384,128]{2,1,0:T(8,128)(2,1)S(1)}, bf16[2,384,128]{2,1,0:T(8,128)(2,1)S(1)}, u32[]{:S(2)}, u32[]{:S(2)}) collective-permute-start(bf16[2,384,128]{2,1,0:T(8,128)(2,1)S(1)} %get-tuple-element.35), channel_id=1, source_target_pairs={{0,2},{2,4},{4,6},{6,8},{8,10},{10,12},{12,14},{14,16},{16,18},{18... | collective-permute-start | bytes 589832 | tf_op jit(solution)/shard_map/ppermute | solution.py:373
  18.2 17.4 %collective-permute-start.2 = (bf16[2,384,128]{2,1,0:T(8,128)(2,1)S(1)}, bf16[2,384,128]{2,1,0:T(8,128)(2,1)S(1)}, u32[]{:S(2)}, u32[]{:S(2)}) collective-permute-start(bf16[2,384,128]{2,1,0:T(8,128)(2,1)S(1)} %get-tuple-element.22.refs_2_), channel_id=1, source_target_pairs={{0,2},{2,4},{4,6},{6,8},{8,10},{10,12},{12,14},{14,16},{16,18},{18... | collective-permute-start | bytes 589832 | tf_op jit(solution)/shard_map/ppermute | solution.py:373
  22.6 13.0 %collective-permute-start.3 = (bf16[2,384,128]{2,1,0:T(8,128)(2,1)S(1)}, bf16[2,384,128]{2,1,0:T(8,128)(2,1)S(1)}, u32[]{:S(2)}, u32[]{:S(2)}) collective-permute-start(bf16[2,384,128]{2,1,0:T(8,128)(2,1)S(1)} %get-tuple-element.23.refs_1_), channel_id=1, source_target_pairs={{2,0},{4,2},{6,4},{8,6},{10,8},{12,10},{14,12},{16,14},{18,16},{20... | collective-permute-start | bytes 589832 | tf_op jit(solution)/shard_map/ppermute | solution.py:373
  28.3 19.2 %all-to-all-start = ((bf16[32,36,128]{2,1,0:T(8,128)(2,1)}), bf16[32,36,128]{2,1,0:T(8,128)(2,1)S(1)}, u32[]{:S(2)}, u32[]{:S(2)}) async-start(bf16[32,36,128]{2,1,0:T(8,128)(2,1)} %get-tuple-element.33), calls=%async_computation | async-start | bytes 655360 | tf_op jit(solution)/shard_map/all_to_all | solution.py:480

commit v3 on v2

--- a/solution.py
+++ b/solution.py
@@ -242,11 +242,50 @@
     by_rate(rates_ref[0, lax.axis_index("tile")], body)
 
 
-def second_kernel(
+def taps_kernel(
     rates_ref, grad_low_ref, grad_high_ref, xt_own_ref, xt_halo_ref, total_ref,
-    gcat_ref, cot_hbm, mask_ref, back_ref, held_hbm,
-    out_hbm, edge_ref, tap_ref,
-    cbuf, obuf, pad, gedge, flat, sems, *, scale,
+    keep_ref, send_ref, gedge_ref,
+    pad, flat, *, scale, paired,
+):
+    _, columns, channels = grad_low_ref.shape
+    rows = xt_own_ref.shape[0]
+    clear_ends(pad, 2 * HALO, columns)
+
+    def flipped(row):
+        if row < 0:
+            return xt_halo_ref[row + HALO]
+        return xt_own_ref[row] if row < rows else xt_halo_ref[row - rows + HALO]
+
+    def body(rate):
+        edges = []
+        for side, ref in enumerate((grad_low_ref, grad_high_ref)):
+            for k in range(HALO):
+                slot = side * HALO + k
+                spread(ref[k], pad, slot, gedge_ref.at[slot], -rate)
+                edges.append((k + side * (rows - HALO), gedge_ref.at[slot]))
+        total = (total_ref[...] + tap_sums(edges, flipped, rate)) * scale
+        for a in range(3):
+            for b in range(3):
+                start = (a * 3 + b) * channels
+                flat[start : start + channels] = total[
+                    a * channels : (a + 1) * channels, b * channels : (b + 1) * channels
+                ]
+
+    by_rate(rates_ref[0, lax.axis_index("tile")], body)
+    if not paired:
+        keep_ref[0] = flat[...]
+        return
+    parts, share, _ = keep_ref.shape
+    here = lax.axis_index("dp")
+    for part in range(parts):
+        keep_ref[part] = flat[pl.ds((2 * part + here) * share, share)]
+        send_ref[part] = flat[pl.ds((2 * part + 1 - here) * share, share)].astype(BF16)
+
+
+def inputs_kernel(
+    rates_ref, gcat_ref, gedge_ref, cot_hbm, mask_ref, back_ref, held_hbm,
+    out_hbm, edge_ref,
+    cbuf, obuf, sems,
 ):
     del held_hbm
     rows, columns, channels = cot_hbm.shape
@@ -269,33 +308,23 @@
     ]
     for load in loads:
         load.start()
-    clear_ends(pad, 2 * HALO, columns)
-    for load in loads:
-        load.wait()
-
-    def flipped(row):
-        if row < 0:
-            return xt_halo_ref[row + HALO]
-        return xt_own_ref[row] if row < rows else xt_halo_ref[row - rows + HALO]
 
     def grads(row):
         if row < HALO:
-            return gedge.at[row]
+            return gedge_ref.at[row]
         if row < rows - HALO:
             return gcat_ref.at[row - HALO]
-        return gedge.at[row - (rows - 2 * HALO)]
+        return gedge_ref.at[row - (rows - 2 * HALO)]
 
     def body(rate):
-        edges = []
-        for side, ref in enumerate((grad_low_ref, grad_high_ref)):
-            for k in range(HALO):
-                slot = side * HALO + k
-                spread(ref[k], pad, slot, gedge.at[slot], -rate)
-                edges.append((k + side * (rows - HALO), gedge.at[slot]))
         for side in range(2):
             start = side * (rows - around)
-            for pair in row_pairs(rate, range(start, start + around)):
-                sums = input_sums(pair, rate, rows, grads, back_ref)
+            results = [
+                (pair, input_sums(pair, rate, rows, grads, back_ref))
+                for pair in row_pairs(rate, range(start, start + around))
+            ]
+            loads[side].wait()
+            for pair, sums in results:
                 for row, value in zip(pair, sums):
                     value = value + cbuf[row - start + side * around].astype(F32)
                     if HALO <= row < rows - HALO:
@@ -305,18 +334,8 @@
                         here = row if side == 0 else row - (rows - around)
                         edge_ref[here] = value
             stores[side].start()
-        total = (total_ref[...] + tap_sums(edges, flipped, rate)) * scale
-        for a in range(3):
-            for b in range(3):
-                start = (a * 3 + b) * channels
-                flat[start : start + channels] = total[
-                    a * channels : (a + 1) * channels, b * channels : (b + 1) * channels
-                ]
 
     by_rate(rates_ref[0, lax.axis_index("tile")], body)
-    share = tap_ref.shape[1]
-    for part in range(tap_ref.shape[0]):
-        tap_ref[part] = flat[part * share : (part + 1) * share].astype(BF16)
     for store in stores:
         store.wait()
 
@@ -456,28 +475,43 @@
     from_low, from_high = exchange(grad_high, grad_low, "tile")
 
     tap_rows = 9 * channels
-    direct = tap_rows % devices == 0
-    share = (devices, tap_rows // devices) if direct else (1, tap_rows)
+    cores = lax.axis_size("dp")
+    paired = cores == 2 and tap_rows % devices == 0
+    share = (devices // 2, tap_rows // devices) if paired else (1, tap_rows)
     scale = 1.0 / math.sqrt(devices * lists.shape[1] * TILE * TILE)
-    held, edge, taps = call(
-        lambda *refs: second_kernel(*refs, scale=scale),
-        "second",
-        [whole, ((2 * HALO, columns, channels), F32), (share + (channels,), BF16)],
-        "svvvvvvhvvh>hvv",
+    keep, send, gedge = call(
+        lambda *refs: taps_kernel(*refs, scale=scale, paired=paired),
+        "taps",
+        [
+            (share + (channels,), F32),
+            (share + (channels,), BF16),
+            ((2 * HALO, columns, wide_row), BF16),
+        ],
+        "svvvvv>vvv",
+        [pads(2 * HALO), pltpu.VMEM((tap_rows, channels), F32)],
+    )(dilations, grad_low, grad_high, xt, xt_halo, total)
+    if paired:
+        other = lax.ppermute(send, "dp", [(0, 1), (1, 0)])
+        both = (keep + other.astype(F32)).astype(BF16)
+        received = lax.all_to_all(both, "tile", 0, 0, tiled=True)
+    else:
+        received = lax.all_to_all(
+            keep.astype(BF16).reshape(devices, -1), axes, 0, 0, tiled=True
+        )
+
+    held, edge = call(
+        inputs_kernel,
+        "inputs",
+        [whole, ((2 * HALO, columns, channels), F32)],
+        "svvhvvh>hv",
         [
             pltpu.VMEM((4 * HALO, columns, channels), BF16),
             pltpu.VMEM((2 * HALO, columns, channels), BF16),
-            pads(2 * HALO),
-            pltpu.VMEM((2 * HALO, columns, wide_row), BF16),
-            pltpu.VMEM((tap_rows, channels), F32),
             pltpu.SemaphoreType.DMA((4,)),
         ],
-        {10: 0},
+        {6: 0},
         flops=BUSY,
-    )(dilations, grad_low, grad_high, xt, xt_halo, total, gcat, cot, mask, back, held)
-    if not direct:
-        taps = taps.reshape(devices, -1)
-    received = lax.all_to_all(taps, axes, 0, 0, tiled=True)
+    )(dilations, gcat, gedge, cot, mask, back, held)
 
     (input_grad,) = call(
         edges_kernel,

time: 48.6 us -> 47 us (0.967)
  waiting for transfers between devices: 10.1 us -> 6.67 us
  starting transfers between devices: 19.7 us -> 20.6 us
  other arithmetic: 0.67 us -> 1.33 us
    all_to_all x1, waiting for transfers between devices: 9.96 us -> 6.39 us  [shards(): received = lax.all_to_all(both, 'tile', 0, 0, tiled=True)]
    convert_element_type x0 -> x1, other arithmetic: none -> 0.69 us  [shards(): both = (keep + other.astype(F32)).astype(BF16)]
    ppermute x2, starting transfers between devices: 9.86 us -> 10.4 us  [exchange(): lax.ppermute(to_next, axis, forward)]
    pallas_call x1 -> x2, Pallas kernels: 4.47 us -> 4.87 us  [the longest x1 3.23 us: shards(): call(inputs_kernel, 'inputs', [whole, ((2 * HALO, columns, channels), F32...]
  transfers between devices with their start and end apart: 5 -> 6, of which waited for: 2 -> 2; matrix products, arithmetic and copies ran while one was open for 0% -> 1% of each run, Pallas kernels for 30% -> 32%
where the time goes in v3:
time: 47 us; the launch traced here: 46.5 us
  starting transfers between devices  20.6 us (44%)
  Pallas kernels  16.1 us (34%)
  waiting for transfers between devices  6.67 us (14%)
  other arithmetic  1.33 us (3%)
  local copies, waits for them, and re-layouts  1.05 us (2%)
  between operations  0.75 us (2%)
    ppermute x2, starting transfers between devices, exchange(): lax.ppermute(to_next, axis, forward)  10.4 us
    pallas_call x1, Pallas kernels, shards(): call(first_kernel, 'first', [whole, ((2 * HALO, columns, channels), F32),...  7.98 us
    all_to_all x1, starting transfers between devices, shards(): received = lax.all_to_all(both, 'tile', 0, 0, tiled=True)  7.54 us
    all_to_all x1, waiting for transfers between devices, shards(): received = lax.all_to_all(both, 'tile', 0, 0, tiled=True)  6.39 us
    pallas_call x1, Pallas kernels, shards(): call(inputs_kernel, 'inputs', [whole, ((2 * HALO, columns, channels), F32...  3.23 us
    ppermute x2, starting transfers between devices, exchange(): lax.ppermute(to_previous, axis, backward)  2.58 us
    pallas_call x1, Pallas kernels, shards(): call(edges_kernel, 'edges', [whole], 'svvvvvh>h', [pltpu.VMEM((2 * HALO,...  2.01 us
    pallas_call x1, Pallas kernels, shards(): call(lambda *refs: taps_kernel(*refs, scale=scale, paired=paired), 'taps'...  1.64 us
  transfers between devices with their start and end apart: 6, of which 2 were waited for; matrix products, arithmetic and copies ran while one was open for 1% of the time, Pallas kernels for 32%

profile of v3, /device:TPU:0, one launch (start us, length us, event | category | flops | bytes accessed | tf_op | source)
XLA Modules:
  0.0 46.5 jit_solution(12640486631648370749)
XLA Ops:
  0.6 1.1 %slice_bitcast_fusion = (bf16[2,384,128]{2,1,0:T(8,128)(2,1)S(1)}, bf16[2,384,128]{2,1,0:T(8,128)(2,1)S(1)}) fusion(bf16[1,12,384,128]{3,2,1,0:T(8,128)(2,1)} %param.7), kind=kLoop, calls=%fused_computation.2 | loop fusion | bytes 786432 | tf_op jit(solution)/shard_map/slice | solution.py:432
  1.7 1.3 %collective-permute-start.1 = (bf16[2,384,128]{2,1,0:T(8,128)(2,1)S(1)}, bf16[2,384,128]{2,1,0:T(8,128)(2,1)S(1)}, u32[]{:S(2)}, u32[]{:S(2)}) collective-permute-start(bf16[2,384,128]{2,1,0:T(8,128)(2,1)S(1)} %get-tuple-element.38), channel_id=1, source_target_pairs={{2,0},{4,2},{6,4},{8,6},{10,8},{12,10},{14,12},{16,14},{18,16},{20... | collective-permute-start | bytes 589832 | tf_op jit(solution)/shard_map/ppermute | solution.py:392
  3.0 5.5 %collective-permute-start = (bf16[2,384,128]{2,1,0:T(8,128)(2,1)S(1)}, bf16[2,384,128]{2,1,0:T(8,128)(2,1)S(1)}, u32[]{:S(2)}, u32[]{:S(2)}) collective-permute-start(bf16[2,384,128]{2,1,0:T(8,128)(2,1)S(1)} %get-tuple-element.39), channel_id=1, source_target_pairs={{0,2},{2,4},{4,6},{6,8},{8,10},{10,12},{12,14},{14,16},{16,18},{18... | collective-permute-start | bytes 589832 | tf_op jit(solution)/shard_map/ppermute | solution.py:392
  8.5 8.0 %first.1 = (bf16[12,384,128]{2,1,0:T(8,128)(2,1)}, f32[4,384,128]{2,1,0:T(8,128)S(1)}, bf16[8,384,384]{2,1,0:T(8,128)(2,1)S(1)}, bf16[12,128,384]{2,1,0:T(8,128)...) custom-call(s32[1,16]{1,0:T(1,128)} %rates_ref.7, ...), custom_call_target="tpu_custom_call" | custom-call | flops 20000000000 | tf_op jit(solution)/shard_map/first/pallas_call | solution.py:434
  16.5 0.0 collective-permute-done.1.high_ref
  16.5 0.3 collective-permute-done.low_ref
  16.7 1.2 %rims.1 = (bf16[2,384,128]{2,1,0:T(8,128)(2,1)S(1)}, bf16[2,384,128]{2,1,0:T(8,128)(2,1)S(1)}, bf16[4,128,384]{2,1,0:T(8,128)(2,1)S(1)}) custom-call(s32[1,16]{1,0:T(1,128)} %rates_ref.7, bf16[2,384,128]{2,1,0:T(8,128)(2,1)S(1)} %collective-permute-done.low_ref, bf16[2,384,128]{2,1,0:T(8,128)(2,1)S(1)} %collective-permute-done.1.high_ref, ...), custom_call_target="tpu_custom_call" | custom-call | tf_op jit(solution)/shard_map/rims/pallas_call | solution.py:463
  18.0 4.9 %collective-permute-start.2 = (bf16[2,384,128]{2,1,0:T(8,128)(2,1)S(1)}, bf16[2,384,128]{2,1,0:T(8,128)(2,1)S(1)}, u32[]{:S(2)}, u32[]{:S(2)}) collective-permute-start(bf16[2,384,128]{2,1,0:T(8,128)(2,1)S(1)} %get-tuple-element.24.refs_2_), channel_id=1, source_target_pairs={{0,2},{2,4},{4,6},{6,8},{8,10},{10,12},{12,14},{14,16},{16,18},{18... | collective-permute-start | bytes 589832 | tf_op jit(solution)/shard_map/ppermute | solution.py:392
  22.9 1.3 %collective-permute-start.3 = (bf16[2,384,128]{2,1,0:T(8,128)(2,1)S(1)}, bf16[2,384,128]{2,1,0:T(8,128)(2,1)S(1)}, u32[]{:S(2)}, u32[]{:S(2)}) collective-permute-start(bf16[2,384,128]{2,1,0:T(8,128)(2,1)S(1)} %get-tuple-element.25.refs_1_), channel_id=1, source_target_pairs={{2,0},{4,2},{6,4},{8,6},{10,8},{12,10},{14,12},{16,14},{18,16},{20... | collective-permute-start | bytes 589832 | tf_op jit(solution)/shard_map/ppermute | solution.py:392
  24.2 1.6 %taps.1 = (f32[16,36,128]{2,1,0:T(8,128)S(1)}, bf16[16,36,128]{2,1,0:T(8,128)(2,1)S(1)}, bf16[4,384,384]{2,1,0:T(8,128)(2,1)S(1)}) custom-call(s32[1,16]{1,0:T(1,128)} %rates_ref.7, bf16[2,384,128]{2,1,0:T(8,128)(2,1)S(1)} %get-tuple-element.25.refs_1_, bf16[2,384,128]{2,1,0:T(8,128)(2,1)S(1)} %get-tuple-element.24.refs_2_, ...), custom_call_target="tpu_custom_call" | custom-call | tf_op jit(solution)/shard_map/taps/pallas_call | solution.py:482
  25.9 0.1 collective-permute-start.4
  25.9 3.2 %inputs.1 = (bf16[12,384,128]{2,1,0:T(8,128)(2,1)}, f32[4,384,128]{2,1,0:T(8,128)S(1)}) custom-call(s32[1,16]{1,0:T(1,128)} %rates_ref.7, bf16[8,384,384]{2,1,0:T(8,128)(2,1)S(1)} %get-tuple-element.26.gcat_ref, bf16[4,384,384]{2,1,0:T(8,128)(2,1)S(1)} %get-tuple-element.30.gedge_ref, ...), custom_call_target="tpu_custom_call", output_to_operand_aliasing={{0}: (6, {})} | custom-call | flops 20000000000 | tf_op jit(solution)/shard_map/inputs/pallas_call | solution.py:502
  29.2 0.0 collective-permute-done.4
  29.2 0.7 %add_convert_fusion = bf16[16,36,128]{2,1,0:T(8,128)(2,1)} fusion(f32[16,36,128]{2,1,0:T(8,128)S(1)} %get-tuple-element.36, bf16[16,36,128]{2,1,0:T(8,128)(2,1)S(1)} %collective-permute-done.4), kind=kLoop, calls=%fused_computation.1 | loop fusion | flops 221184 | bytes 589824 | tf_op jit(solution)/shard_map/convert_element_type | solution.py:495
  29.9 7.5 %all-to-all-start = ((bf16[16,36,128]{2,1,0:T(8,128)(2,1)}), bf16[16,36,128]{2,1,0:T(8,128)(2,1)S(1)}, u32[]{:S(2)}, u32[]{:S(2)}) async-start(bf16[16,36,128]{2,1,0:T(8,128)(2,1)} %add_convert_fusion), calls=%async_computation | async-start | bytes 327680 | tf_op jit(solution)/shard_map/all_to_all | solution.py:496
  37.4 0.0 collective-permute-done.2.low_ref
  37.4 0.0 collective-permute-done.3.high_ref
  37.4 2.0 %edges.1 = bf16[12,384,128]{2,1,0:T(8,128)(2,1)} custom-call(s32[1,16]{1,0:T(1,128)} %rates_ref.7, bf16[2,384,128]{2,1,0:T(8,128)(2,1)S(1)} %collective-permute-done.2.low_ref, bf16[2,384,128]{2,1,0:T(8,128)(2,1)S(1)} %collective-permute-done.3.high_ref, f32[4,384,128]{2,1,0:T(8,128)S(1)} %get-tuple-element.33.edge_ref, ...), custom_call_target="tpu_custom_call", output_to_operand_aliasing={{}: (6, {})} | custom-call | flops 20000000000 | tf_op jit(solution)/shard_map/edges/pallas_call | solution.py:516
  39.5 6.4 %all-to-all-done = bf16[16,36,128]{2,1,0:T(8,128)(2,1)S(1)} async-done(((bf16[16,36,128]{2,1,0:T(8,128)(2,1)}), bf16[16,36,128]{2,1,0:T(8,128)(2,1)S(1)}, u32[]{:S(2)}, u32[]{:S(2)}) %all-to-all-start) | async-done | bytes 147488 | tf_op jit(solution)/shard_map/all_to_all | solution.py:496
  45.9 0.6 %convert_reduce_fusion = f32[36,128]{1,0:T(8,128)} fusion(bf16[16,36,128]{2,1,0:T(8,128)(2,1)S(1)} %all-to-all-done), kind=kLoop, calls=%fused_computation | loop fusion | flops 142848 | bytes 165888 | tf_op jit(solution)/shard_map/reduce_sum | solution.py:530
Async XLA Ops:
  1.7 14.8 %collective-permute-start.1 = (bf16[2,384,128]{2,1,0:T(8,128)(2,1)S(1)}, bf16[2,384,128]{2,1,0:T(8,128)(2,1)S(1)}, u32[]{:S(2)}, u32[]{:S(2)}) collective-permute-start(bf16[2,384,128]{2,1,0:T(8,128)(2,1)S(1)} %get-tuple-element.38), channel_id=1, source_target_pairs={{2,0},{4,2},{6,4},{8,6},{10,8},{12,10},{14,12},{16,14},{18,16},{20... | collective-permute-start | bytes 589832 | tf_op jit(solution)/shard_map/ppermute | solution.py:392
  3.0 13.8 %collective-permute-start = (bf16[2,384,128]{2,1,0:T(8,128)(2,1)S(1)}, bf16[2,384,128]{2,1,0:T(8,128)(2,1)S(1)}, u32[]{:S(2)}, u32[]{:S(2)}) collective-permute-start(bf16[2,384,128]{2,1,0:T(8,128)(2,1)S(1)} %get-tuple-element.39), channel_id=1, source_target_pairs={{0,2},{2,4},{4,6},{6,8},{8,10},{10,12},{12,14},{14,16},{16,18},{18... | collective-permute-start | bytes 589832 | tf_op jit(solution)/shard_map/ppermute | solution.py:392
  18.0 19.4 %collective-permute-start.2 = (bf16[2,384,128]{2,1,0:T(8,128)(2,1)S(1)}, bf16[2,384,128]{2,1,0:T(8,128)(2,1)S(1)}, u32[]{:S(2)}, u32[]{:S(2)}) collective-permute-start(bf16[2,384,128]{2,1,0:T(8,128)(2,1)S(1)} %get-tuple-element.24.refs_2_), channel_id=1, source_target_pairs={{0,2},{2,4},{4,6},{6,8},{8,10},{10,12},{12,14},{14,16},{16,18},{18... | collective-permute-start | bytes 589832 | tf_op jit(solution)/shard_map/ppermute | solution.py:392
  22.9 14.5 %collective-permute-start.3 = (bf16[2,384,128]{2,1,0:T(8,128)(2,1)S(1)}, bf16[2,384,128]{2,1,0:T(8,128)(2,1)S(1)}, u32[]{:S(2)}, u32[]{:S(2)}) collective-permute-start(bf16[2,384,128]{2,1,0:T(8,128)(2,1)S(1)} %get-tuple-element.25.refs_1_), channel_id=1, source_target_pairs={{2,0},{4,2},{6,4},{8,6},{10,8},{12,10},{14,12},{16,14},{18,16},{20... | collective-permute-start | bytes 589832 | tf_op jit(solution)/shard_map/ppermute | solution.py:392
  25.9 3.3 %collective-permute-start.4 = (bf16[16,36,128]{2,1,0:T(8,128)(2,1)S(1)}, bf16[16,36,128]{2,1,0:T(8,128)(2,1)S(1)}, u32[]{:S(2)}, u32[]{:S(2)}) collective-permute-start(bf16[16,36,128]{2,1,0:T(8,128)(2,1)S(1)} %get-tuple-element.37), channel_id=1, source_target_pairs={{0,1},{1,0},{2,3},{3,2},{4,5},{5,4},{6,7},{7,6},{8,9},{9,8},{10,11... | collective-permute-start | bytes 442376 | tf_op jit(solution)/shard_map/ppermute | solution.py:494
  29.9 16.0 %all-to-all-start = ((bf16[16,36,128]{2,1,0:T(8,128)(2,1)}), bf16[16,36,128]{2,1,0:T(8,128)(2,1)S(1)}, u32[]{:S(2)}, u32[]{:S(2)}) async-start(bf16[16,36,128]{2,1,0:T(8,128)(2,1)} %add_convert_fusion), calls=%async_computation | async-start | bytes 327680 | tf_op jit(solution)/shard_map/all_to_all | solution.py:496

commit v4 on v3

--- a/solution.py
+++ b/solution.py
@@ -109,16 +109,26 @@
 
 def first_kernel(
     rates_ref, lists_ref, x_hbm, cot_hbm, w_hbm, bias_ref,
-    out_hbm, pre_ref, gcat_ref, xt_ref, total_ref, mask_ref, cot_ref, back_ref, near_ref, far_ref,
-    xbuf, cbuf, wbuf, obuf, pad, xcat, wide, sems,
+    gcat_hbm, pre_ref, xt_ref, total_ref, mask_ref, cot_ref, back_ref, near_ref, far_ref,
+    xbuf, cbuf, wbuf, pad, xcat, gcat_ref, wide, sems,
 ):
     rows, columns, channels = x_hbm.shape
     tiles_row = columns // TILE
     mine = lax.axis_index("tile")
-    loads = [
-        pltpu.make_async_copy(w_hbm, wbuf, sems.at[0]),
-        pltpu.make_async_copy(x_hbm, xbuf, sems.at[1]),
-        pltpu.make_async_copy(cot_hbm, cbuf, sems.at[2]),
+    step = rows // 4
+    loads = [pltpu.make_async_copy(w_hbm, wbuf, sems.at[0])]
+    for source, target, base in ((x_hbm, xbuf, 1), (cot_hbm, cbuf, 5)):
+        for k in range(4):
+            part = pl.ds(k * step, step)
+            loads.append(
+                pltpu.make_async_copy(source.at[part], target.at[part], sems.at[base + k])
+            )
+    inner = rows - 2 * HALO
+    stores = [
+        pltpu.make_async_copy(
+            gcat_ref.at[pl.ds(k, 2)], gcat_hbm.at[pl.ds(k, 2)], sems.at[9 + k // 2]
+        )
+        for k in range(0, inner, 2)
     ]
     for load in loads:
         load.start()
@@ -142,13 +152,9 @@
                 wide[here, there] = wbuf[tap * 3 + col] if 0 <= tap < 3 else none
                 tap = out + 2 - row
                 back_ref[here, there] = turned[tap] if 0 <= tap < 3 else none
-    loads[1].wait()
-    loads[2].wait()
+    for load in loads[1:]:
+        load.wait()
     half_bias = 0.5 * bias_ref[...]
-    middle = range(2 * HALO, rows - 2 * HALO)
-    store = pltpu.make_async_copy(
-        obuf, out_hbm.at[pl.ds(middle.start, len(middle))], sems.at[3]
-    )
 
     def body(rate):
         done = set()
@@ -180,12 +186,17 @@
                     grad = silu_grad(half_cot.astype(F32), half_pre)
                     spread(grad, pad, row, gcat_ref.at[row - HALO], -rate)
                     ready.append(row)
+                    there.add(row)
+                    mate = row ^ 1
+                    if mate in there:
+                        stores[(row - HALO) // 2].start()
                 else:
                     here = row if row < HALO else row - (rows - 2 * HALO)
                     pre_ref[here] = half_pre
                     cot_ref[here] = half_cot
 
         ready = []
+        there = set()
         summed = []
         waiting = None
         for pair in row_pairs(rate, range(rows)) + [None]:
@@ -199,15 +210,10 @@
                 total_ref[...] = total_ref[...] + part if summed else part
                 summed.extend(ready[:2])
                 del ready[:2]
-        for pair in row_pairs(rate, middle):
-            sums = input_sums(pair, rate, rows, lambda row: gcat_ref.at[row - HALO], back_ref)
-            for row, value in zip(pair, sums):
-                value = (value + cbuf[row].astype(F32)).astype(BF16)
-                obuf[row - middle.start] = value * mask_ref[1]
 
     by_rate(rates_ref[0, mine], body)
-    store.start()
-    store.wait()
+    for store in stores:
+        store.wait()
 
 
 def rims_kernel(
@@ -244,8 +250,8 @@
 
 def taps_kernel(
     rates_ref, grad_low_ref, grad_high_ref, xt_own_ref, xt_halo_ref, total_ref,
-    keep_ref, send_ref, gedge_ref,
-    pad, flat, *, scale, paired,
+    keep_ref, send_ref,
+    pad, gedge_ref, flat, *, scale, paired,
 ):
     _, columns, channels = grad_low_ref.shape
     rows = xt_own_ref.shape[0]
@@ -282,107 +288,94 @@
         send_ref[part] = flat[pl.ds((2 * part + 1 - here) * share, share)].astype(BF16)
 
 
-def inputs_kernel(
-    rates_ref, gcat_ref, gedge_ref, cot_hbm, mask_ref, back_ref, held_hbm,
-    out_hbm, edge_ref,
-    cbuf, obuf, sems,
+def last_kernel(
+    rates_ref, from_low_ref, from_high_ref, grad_low_ref, grad_high_ref,
+    gcat_hbm, cot_hbm, mask_ref, back_ref, far_ref,
+    out_hbm,
+    cbuf, obuf, pad, gcat, spare, terms, sems,
 ):
-    del held_hbm
     rows, columns, channels = cot_hbm.shape
+    inner = rows - 2 * HALO
+    mine = lax.axis_index("tile")
+    last = rates_ref.shape[1] - 1
     around = 2 * HALO
+    chunks = rows // around
     loads = [
         pltpu.make_async_copy(
-            cot_hbm.at[pl.ds(side * (rows - around), around)],
-            cbuf.at[pl.ds(side * around, around)],
-            sems.at[side],
+            gcat_hbm.at[pl.ds(k, 2)], gcat.at[pl.ds(HALO + k, 2)], sems.at[k // 2]
         )
-        for side in range(2)
+        for k in range(0, inner, 2)
     ]
-    stores = [
-        pltpu.make_async_copy(
-            obuf.at[pl.ds(side * HALO, HALO)],
-            out_hbm.at[pl.ds(HALO + side * (rows - 3 * HALO), HALO)],
-            sems.at[2 + side],
+    cots, stores = [], []
+    for k in range(chunks):
+        part = pl.ds(k * around, around)
+        cots.append(
+            pltpu.make_async_copy(cot_hbm.at[part], cbuf.at[part], sems.at[inner // 2 + k])
         )
-        for side in range(2)
-    ]
-    for load in loads:
+        stores.append(
+            pltpu.make_async_copy(obuf.at[part], out_hbm.at[part], sems.at[inner // 2 + chunks + k])
+        )
+    for load in loads + cots:
         load.start()
-
-    def grads(row):
-        if row < HALO:
-            return gedge_ref.at[row]
-        if row < rows - HALO:
-            return gcat_ref.at[row - HALO]
-        return gedge_ref.at[row - (rows - 2 * HALO)]
-
-    def body(rate):
-        for side in range(2):
-            start = side * (rows - around)
-            results = [
-                (pair, input_sums(pair, rate, rows, grads, back_ref))
-                for pair in row_pairs(rate, range(start, start + around))
-            ]
-            loads[side].wait()
-            for pair, sums in results:
-                for row, value in zip(pair, sums):
-                    value = value + cbuf[row - start + side * around].astype(F32)
-                    if HALO <= row < rows - HALO:
-                        here = row - HALO if side == 0 else row - (rows - around) + HALO
-                        obuf[here] = value.astype(BF16) * mask_ref[1]
-                    else:
-                        here = row if side == 0 else row - (rows - around)
-                        edge_ref[here] = value
-            stores[side].start()
-
-    by_rate(rates_ref[0, lax.axis_index("tile")], body)
-    for store in stores:
-        store.wait()
-
-
-def edges_kernel(
-    rates_ref, low_ref, high_ref, edge_ref, mask_ref, far_ref, held_hbm,
-    out_hbm,
-    obuf, pad, gcat, sems,
-):
-    del held_hbm
-    _, columns, channels = low_ref.shape
-    rows = out_hbm.shape[0]
-    mine = lax.axis_index("tile")
-    last = rates_ref.shape[1] - 1
-    clear_ends(pad, 2 * HALO, columns)
-    stores = [
-        pltpu.make_async_copy(
-            obuf.at[pl.ds(HALO * side, HALO)],
-            out_hbm.at[pl.ds((rows - HALO) * side, HALO)],
-            sems.at[side],
-        )
-        for side in range(2)
-    ]
-
-    def one_side(side, rate):
-        ref = high_ref if side else low_ref
+    clear_ends(pad, 4 * HALO, columns)
+
+    def neighbour(side, rate):
+        ref = from_high_ref if side else from_low_ref
         used = range(rate) if side else range(HALO - rate, HALO)
         for place, k in enumerate(used):
             spread(
-                ref[k], pad, side * HALO + k, gcat.at[side, pl.ds(place * columns, columns)], -rate
+                ref[k], pad, side * HALO + k, spare.at[side, pl.ds(place * columns, columns)], -rate
             )
         sums = jnp.dot(
-            gcat[side, : rate * columns], far_ref[side], preferred_element_type=F32
+            spare[side, : rate * columns], far_ref[side], preferred_element_type=F32
         )
         for k in range(HALO):
-            value = edge_ref[side * HALO + k]
             place = k - (HALO - rate) if side else k
             if 0 <= place < rate:
-                value = value + sums[place * columns : (place + 1) * columns]
-            obuf[side * HALO + k] = value.astype(BF16) * mask_ref[1]
+                terms[side * HALO + k] = sums[place * columns : (place + 1) * columns]
+            else:
+                terms[side * HALO + k] = jnp.zeros((columns, channels), F32)
 
     near = (jnp.maximum(mine - 1, 0), jnp.minimum(mine + 1, last))
     for side in range(2):
-        by_rate(rates_ref[0, near[side]], lambda rate, side=side: one_side(side, rate))
-        stores[side].start()
+        by_rate(rates_ref[0, near[side]], lambda rate, side=side: neighbour(side, rate))
+
+    def body(rate):
+        for side, ref in enumerate((grad_low_ref, grad_high_ref)):
+            for k in range(HALO):
+                slot = side * HALO + k
+                spread(ref[k], pad, 2 * HALO + slot, gcat.at[k + side * (rows - HALO)], -rate)
+        for load in loads + cots:
+            load.wait()
+        for chunk in range(chunks):
+            start = chunk * around
+            for pair in row_pairs(rate, range(start, start + around)):
+                sums = input_sums(pair, rate, rows, lambda row: gcat.at[row], back_ref)
+                for row, value in zip(pair, sums):
+                    value = value + cbuf[row].astype(F32)
+                    if row < HALO:
+                        value = value + terms[row]
+                    elif row >= rows - HALO:
+                        value = value + terms[row - inner]
+                    obuf[row] = value.astype(BF16) * mask_ref[1]
+            stores[chunk].start()
+
+    by_rate(rates_ref[0, mine], body)
     for store in stores:
         store.wait()
+
+
+def cut_kernel(x_hbm, low_ref, high_ref, sems):
+    rows = x_hbm.shape[0]
+    copies = [
+        pltpu.make_async_copy(x_hbm.at[row], ref.at[k], sems.at[side, k])
+        for side, ref in enumerate((low_ref, high_ref))
+        for k, row in enumerate(range(side * (rows - HALO), side * (rows - HALO) + HALO))
+    ]
+    for copy in copies:
+        copy.start()
+    for copy in copies:
+        copy.wait()
 
 
 def exchange(to_next, to_previous, axis):
@@ -400,7 +393,10 @@
     return pl.pallas_call(
         kernel,
         name=name,
-        out_shape=tuple(jax.ShapeDtypeStruct(shape, dtype) for shape, dtype in outs),
+        out_shape=tuple(
+            pltpu.HBM(shape, dtype) if letter == "h" else jax.ShapeDtypeStruct(shape, dtype)
+            for (shape, dtype), letter in zip(outs, specs.split(">")[1])
+        ),
         in_specs=ins,
         out_specs=tuple(results),
         scratch_shapes=scratch,
@@ -429,15 +425,22 @@
     def pads(count):
         return pltpu.VMEM((count, columns + 2 * EDGE, channels), F32)
 
-    low, high = exchange(x[rows - HALO :], x[:HALO], "tile")
-
-    held, pre, gcat, xt, total, mask, cot_edge, back, near, far = call(
+    rim = ((HALO, columns, channels), BF16)
+    first_rows, last_rows = call(
+        cut_kernel,
+        "cut",
+        [rim, rim],
+        "h>vv",
+        [pltpu.SemaphoreType.DMA((2, HALO))],
+    )(in_hbm(x))
+    low, high = exchange(last_rows, first_rows, "tile")
+
+    gcat, pre, xt, total, mask, cot_edge, back, near, far = call(
         first_kernel,
         "first",
         [
-            whole,
+            ((inner, columns, wide_row), BF16),
             ((2 * HALO, columns, channels), F32),
-            ((inner, columns, wide_row), BF16),
             ((rows, channels, columns), BF16),
             ((wide_row, wide_row), F32),
             ((3, columns, channels), BF16),
@@ -446,16 +449,16 @@
             ((2, wide_row, channels), BF16),
             ((2, wide_row, channels), BF16),
         ],
-        "svhhhv>hvvvvvvvvv",
+        "svhhhv>hvvvvvvvv",
         [
             pltpu.VMEM((rows, columns, channels), BF16),
             pltpu.VMEM((rows, columns, channels), BF16),
             pltpu.VMEM((9, channels, channels), BF16),
-            pltpu.VMEM((rows - 4 * HALO, columns, channels), BF16),
             pads(rows),
             pltpu.VMEM((rows, columns, wide_row), BF16),
+            pltpu.VMEM((inner, columns, wide_row), BF16),
             pltpu.VMEM((4 * wide_row, 2 * channels), BF16),
-            pltpu.SemaphoreType.DMA((4,)),
+            pltpu.SemaphoreType.DMA((9 + inner // 2,)),
         ],
         flops=BUSY,
     )(dilations, lists, in_hbm(x), cot, weight, bias)
@@ -464,8 +467,8 @@
         rims_kernel,
         "rims",
         [
-            ((HALO, columns, channels), BF16),
-            ((HALO, columns, channels), BF16),
+            rim,
+            rim,
             ((2 * HALO, channels, columns), BF16),
         ],
         "svvvvvv>vvv",
@@ -479,16 +482,19 @@
     paired = cores == 2 and tap_rows % devices == 0
     share = (devices // 2, tap_rows // devices) if paired else (1, tap_rows)
     scale = 1.0 / math.sqrt(devices * lists.shape[1] * TILE * TILE)
-    keep, send, gedge = call(
+    keep, send = call(
         lambda *refs: taps_kernel(*refs, scale=scale, paired=paired),
         "taps",
         [
             (share + (channels,), F32),
             (share + (channels,), BF16),
-            ((2 * HALO, columns, wide_row), BF16),
-        ],
-        "svvvvv>vvv",
-        [pads(2 * HALO), pltpu.VMEM((tap_rows, channels), F32)],
+        ],
+        "svvvvv>vv",
+        [
+            pads(2 * HALO),
+            pltpu.VMEM((2 * HALO, columns, wide_row), BF16),
+            pltpu.VMEM((tap_rows, channels), F32),
+        ],
     )(dilations, grad_low, grad_high, xt, xt_halo, total)
     if paired:
         other = lax.ppermute(send, "dp", [(0, 1), (1, 0)])
@@ -499,34 +505,25 @@
             keep.astype(BF16).reshape(devices, -1), axes, 0, 0, tiled=True
         )
 
-    held, edge = call(
-        inputs_kernel,
-        "inputs",
-        [whole, ((2 * HALO, columns, channels), F32)],
-        "svvhvvh>hv",
-        [
-            pltpu.VMEM((4 * HALO, columns, channels), BF16),
-            pltpu.VMEM((2 * HALO, columns, channels), BF16),
-            pltpu.SemaphoreType.DMA((4,)),
-        ],
-        {6: 0},
+    (input_grad,) = call(
+        last_kernel,
+        "last",
+        [whole],
+        "svvvvhhvvv>h",
+        [
+            pltpu.VMEM((rows, columns, channels), BF16),
+            pltpu.VMEM((rows, columns, channels), BF16),
+            pads(4 * HALO),
+            pltpu.VMEM((rows, columns, wide_row), BF16),
+            pltpu.VMEM((2, HALO * columns, wide_row), BF16),
+            pltpu.VMEM((2 * HALO, columns, channels), F32),
+            pltpu.SemaphoreType.DMA((inner // 2 + 2 * (rows // (2 * HALO)),)),
+        ],
         flops=BUSY,
-    )(dilations, gcat, gedge, cot, mask, back, held)
-
-    (input_grad,) = call(
-        edges_kernel,
-        "edges",
-        [whole],
-        "svvvvvh>h",
-        [
-            pltpu.VMEM((2 * HALO, columns, channels), BF16),
-            pads(2 * HALO),
-            pltpu.VMEM((2, HALO * columns, wide_row), BF16),
-            pltpu.SemaphoreType.DMA((2,)),
-        ],
-        {6: 0},
-        flops=BUSY,
-    )(dilations, from_low, from_high, edge, mask, far, held)
+    )(
+        dilations, from_low, from_high, grad_low, grad_high,
+        in_hbm(gcat), cot, mask, back, far,
+    )
     summed = jnp.sum(received.astype(F32), axis=0)
     return (input_grad[None], summed.reshape(-1))
 

time: 47 us -> 42.9 us (0.913)
  waiting for transfers between devices: 6.67 us -> 4.83 us
  local copies, waits for them, and re-layouts: 1.05 us -> 0 us
  starting transfers between devices: 20.6 us -> 19.6 us
    all_to_all x1, waiting for transfers between devices: 6.39 us -> 2.48 us  [shards(): received = lax.all_to_all(both, 'tile', 0, 0, tiled=True)]
    ppermute x2, waiting for transfers between devices: 0.01 us -> 2.34 us  [exchange(): lax.ppermute(to_previous, axis, backward)]
    ppermute x2, starting transfers between devices: 10.4 us -> 8.45 us  [exchange(): lax.ppermute(to_next, axis, forward)]
    slice x1 -> x0, local copies, waits for them, and re-layouts: 1.05 us -> none  [shards(): low, high = exchange(x[rows - HALO:], x[:HALO], 'tile')]
    all_to_all x1, starting transfers between devices: 7.54 us -> 8.45 us  [shards(): received = lax.all_to_all(both, 'tile', 0, 0, tiled=True)]
  transfers between devices with their start and end apart: 6 -> 6, of which waited for: 2 -> 3; matrix products, arithmetic and copies ran while one was open for 1% -> 2% of each run, Pallas kernels for 32% -> 28%
where the time goes in v4:
time: 42.9 us; the launch traced here: 42.5 us
  starting transfers between devices  19.6 us (46%)
  Pallas kernels  16 us (37%)
  waiting for transfers between devices  4.83 us (11%)
  other arithmetic  1.34 us (3%)
  between operations  0.74 us (2%)
    all_to_all x1, starting transfers between devices, shards(): received = lax.all_to_all(both, 'tile', 0, 0, tiled=True)  8.45 us
    ppermute x2, starting transfers between devices, exchange(): lax.ppermute(to_next, axis, forward)  8.45 us
    pallas_call x1, Pallas kernels, shards(): call(first_kernel, 'first', [((inner, columns, wide_row), BF16), ((2 * HA...  6.73 us
    pallas_call x1, Pallas kernels, shards(): call(last_kernel, 'last', [whole], 'svvvvhhvvv>h', [pltpu.VMEM((rows, col...  5.34 us
    ppermute x2, starting transfers between devices, exchange(): lax.ppermute(to_previous, axis, backward)  2.58 us
    all_to_all x1, waiting for transfers between devices, shards(): received = lax.all_to_all(both, 'tile', 0, 0, tiled=True)  2.48 us
    ppermute x2, waiting for transfers between devices, exchange(): lax.ppermute(to_previous, axis, backward)  2.34 us
    pallas_call x1, Pallas kernels, shards(): call(lambda *refs: taps_kernel(*refs, scale=scale, paired=paired), 'taps'...  1.64 us
  transfers between devices with their start and end apart: 6, of which 3 were waited for; matrix products, arithmetic and copies ran while one was open for 2% of the time, Pallas kernels for 28%

profile of v4, /device:TPU:0, one launch (start us, length us, event | category | flops | bytes accessed | tf_op | source)
XLA Modules:
  0.0 42.5 jit_solution(17573768444933033123)
XLA Ops:
  0.6 1.1 %cut.1 = (bf16[2,384,128]{2,1,0:T(8,128)(2,1)S(1)}, bf16[2,384,128]{2,1,0:T(8,128)(2,1)S(1)}) custom-call(bf16[12,384,128]{2,1,0:T(8,128)(2,1)} %bitcast.7), custom_call_target="tpu_custom_call" | custom-call | tf_op jit(solution)/shard_map/cut/pallas_call | solution.py:429
  1.7 4.9 %collective-permute-start = (bf16[2,384,128]{2,1,0:T(8,128)(2,1)S(1)}, bf16[2,384,128]{2,1,0:T(8,128)(2,1)S(1)}, u32[]{:S(2)}, u32[]{:S(2)}) collective-permute-start(bf16[2,384,128]{2,1,0:T(8,128)(2,1)S(1)} %get-tuple-element.18), channel_id=1, source_target_pairs={{0,2},{2,4},{4,6},{6,8},{8,10},{10,12},{12,14},{14,16},{16,18},{18... | collective-permute-start | bytes 589832 | tf_op jit(solution)/shard_map/ppermute | solution.py:385
  6.6 1.3 %collective-permute-start.1 = (bf16[2,384,128]{2,1,0:T(8,128)(2,1)S(1)}, bf16[2,384,128]{2,1,0:T(8,128)(2,1)S(1)}, u32[]{:S(2)}, u32[]{:S(2)}) collective-permute-start(bf16[2,384,128]{2,1,0:T(8,128)(2,1)S(1)} %get-tuple-element.19), channel_id=1, source_target_pairs={{2,0},{4,2},{6,4},{8,6},{10,8},{12,10},{14,12},{16,14},{18,16},{20... | collective-permute-start | bytes 589832 | tf_op jit(solution)/shard_map/ppermute | solution.py:385
  7.9 6.7 %first.1 = (bf16[8,384,384]{2,1,0:T(8,128)(2,1)}, f32[4,384,128]{2,1,0:T(8,128)S(1)}, bf16[12,128,384]{2,1,0:T(8,128)(2,1)S(1)}, f32[384,384]{1,0:T(8,128)S(1)},...) custom-call(s32[1,16]{1,0:T(1,128)} %refs_0_.1, ...), custom_call_target="tpu_custom_call" | custom-call | flops 20000000000 | tf_op jit(solution)/shard_map/first/pallas_call | solution.py:438
  14.6 0.0 collective-permute-done.low_ref
  14.6 2.2 %collective-permute-done.1.high_ref = bf16[2,384,128]{2,1,0:T(8,128)(2,1)S(1)} collective-permute-done((bf16[2,384,128]{2,1,0:T(8,128)(2,1)S(1)}, bf16[2,384,128]{2,1,0:T(8,128)(2,1)S(1)}, u32[]{:S(2)}, u32[]{:S(2)}) %collective-permute-start.1) | collective-permute-done | bytes 196640 | tf_op jit(solution)/shard_map/ppermute | solution.py:385
  16.9 1.2 %rims.1 = (bf16[2,384,128]{2,1,0:T(8,128)(2,1)S(1)}, bf16[2,384,128]{2,1,0:T(8,128)(2,1)S(1)}, bf16[4,128,384]{2,1,0:T(8,128)(2,1)S(1)}) custom-call(s32[1,16]{1,0:T(1,128)} %refs_0_.1, bf16[2,384,128]{2,1,0:T(8,128)(2,1)S(1)} %collective-permute-done.low_ref, bf16[2,384,128]{2,1,0:T(8,128)(2,1)S(1)} %collective-permute-done.1.high_ref, ...), custom_call_target="tpu_custom_call" | custom-call | tf_op jit(solution)/shard_map/rims/pallas_call | solution.py:466
  18.1 1.6 %taps.1 = (f32[16,36,128]{2,1,0:T(8,128)S(1)}, bf16[16,36,128]{2,1,0:T(8,128)(2,1)S(1)}) custom-call(s32[1,16]{1,0:T(1,128)} %refs_0_.1, bf16[2,384,128]{2,1,0:T(8,128)(2,1)S(1)} %get-tuple-element.25.grad_low_ref.refs_1_, bf16[2,384,128]{2,1,0:T(8,128)(2,1)S(1)} %get-tuple-element.24.grad_high_ref.refs_2_, ...), custom_call_target="tpu_custom_call" | custom-call | tf_op jit(solution)/shard_map/taps/pallas_call | solution.py:485
  19.7 0.1 collective-permute-start.4
  19.8 3.6 %collective-permute-start.2 = (bf16[2,384,128]{2,1,0:T(8,128)(2,1)S(1)}, bf16[2,384,128]{2,1,0:T(8,128)(2,1)S(1)}, u32[]{:S(2)}, u32[]{:S(2)}) collective-permute-start(bf16[2,384,128]{2,1,0:T(8,128)(2,1)S(1)} %get-tuple-element.24.grad_high_ref.refs_2_), channel_id=1, source_target_pairs={{0,2},{2,4},{4,6},{6,8},{8,10},{10,12},{12,14},{14,16},{16,18},{18... | collective-permute-start | bytes 589832 | tf_op jit(solution)/shard_map/ppermute | solution.py:385
  23.4 1.3 %collective-permute-start.3 = (bf16[2,384,128]{2,1,0:T(8,128)(2,1)S(1)}, bf16[2,384,128]{2,1,0:T(8,128)(2,1)S(1)}, u32[]{:S(2)}, u32[]{:S(2)}) collective-permute-start(bf16[2,384,128]{2,1,0:T(8,128)(2,1)S(1)} %get-tuple-element.25.grad_low_ref.refs_1_), channel_id=1, source_target_pairs={{2,0},{4,2},{6,4},{8,6},{10,8},{12,10},{14,12},{16,14},{18,16},{20... | collective-permute-start | bytes 589832 | tf_op jit(solution)/shard_map/ppermute | solution.py:385
  24.7 0.0 collective-permute-done.4
  24.7 0.7 %add_convert_fusion = bf16[16,36,128]{2,1,0:T(8,128)(2,1)} fusion(f32[16,36,128]{2,1,0:T(8,128)S(1)} %get-tuple-element.32, bf16[16,36,128]{2,1,0:T(8,128)(2,1)S(1)} %collective-permute-done.4), kind=kLoop, calls=%fused_computation.1 | loop fusion | flops 221184 | bytes 589824 | tf_op jit(solution)/shard_map/convert_element_type | solution.py:501
  25.4 8.4 %all-to-all-start = ((bf16[16,36,128]{2,1,0:T(8,128)(2,1)}), bf16[16,36,128]{2,1,0:T(8,128)(2,1)S(1)}, u32[]{:S(2)}, u32[]{:S(2)}) async-start(bf16[16,36,128]{2,1,0:T(8,128)(2,1)} %add_convert_fusion), calls=%async_computation | async-start | bytes 327680 | tf_op jit(solution)/shard_map/all_to_all | solution.py:502
  33.9 0.0 collective-permute-done.2.from_low_ref
  33.9 0.1 collective-permute-done.3.from_high_ref
  34.0 5.3 %last.1 = bf16[12,384,128]{2,1,0:T(8,128)(2,1)} custom-call(s32[1,16]{1,0:T(1,128)} %refs_0_.1, bf16[2,384,128]{2,1,0:T(8,128)(2,1)S(1)} %collective-permute-done.2.from_low_ref, bf16[2,384,128]{2,1,0:T(8,128)(2,1)S(1)} %collective-permute-done.3.from_high_ref, bf16[2,384,128]{2,1,0:T(8,128)(2,1)S(1)} %get-tuple-element.25.grad_low_ref.refs_1_, ...), custom_call_target="tpu_custom_call" | custom-call | flops 20000000000 | tf_op jit(solution)/shard_map/last/pallas_call | solution.py:508
  39.3 2.5 %all-to-all-done = bf16[16,36,128]{2,1,0:T(8,128)(2,1)S(1)} async-done(((bf16[16,36,128]{2,1,0:T(8,128)(2,1)}), bf16[16,36,128]{2,1,0:T(8,128)(2,1)S(1)}, u32[]{:S(2)}, u32[]{:S(2)}) %all-to-all-start) | async-done | bytes 147488 | tf_op jit(solution)/shard_map/all_to_all | solution.py:502
  41.8 0.6 %convert_reduce_fusion = f32[36,128]{1,0:T(8,128)} fusion(bf16[16,36,128]{2,1,0:T(8,128)(2,1)S(1)} %all-to-all-done), kind=kLoop, calls=%fused_computation | loop fusion | flops 142848 | bytes 165888 | tf_op jit(solution)/shard_map/reduce_sum | solution.py:527
Async XLA Ops:
  1.7 12.9 %collective-permute-start = (bf16[2,384,128]{2,1,0:T(8,128)(2,1)S(1)}, bf16[2,384,128]{2,1,0:T(8,128)(2,1)S(1)}, u32[]{:S(2)}, u32[]{:S(2)}) collective-permute-start(bf16[2,384,128]{2,1,0:T(8,128)(2,1)S(1)} %get-tuple-element.18), channel_id=1, source_target_pairs={{0,2},{2,4},{4,6},{6,8},{8,10},{10,12},{12,14},{14,16},{16,18},{18... | collective-permute-start | bytes 589832 | tf_op jit(solution)/shard_map/ppermute | solution.py:385
  6.6 10.3 %collective-permute-start.1 = (bf16[2,384,128]{2,1,0:T(8,128)(2,1)S(1)}, bf16[2,384,128]{2,1,0:T(8,128)(2,1)S(1)}, u32[]{:S(2)}, u32[]{:S(2)}) collective-permute-start(bf16[2,384,128]{2,1,0:T(8,128)(2,1)S(1)} %get-tuple-element.19), channel_id=1, source_target_pairs={{2,0},{4,2},{6,4},{8,6},{10,8},{12,10},{14,12},{16,14},{18,16},{20... | collective-permute-start | bytes 589832 | tf_op jit(solution)/shard_map/ppermute | solution.py:385
  19.7 5.0 %collective-permute-start.4 = (bf16[16,36,128]{2,1,0:T(8,128)(2,1)S(1)}, bf16[16,36,128]{2,1,0:T(8,128)(2,1)S(1)}, u32[]{:S(2)}, u32[]{:S(2)}) collective-permute-start(bf16[16,36,128]{2,1,0:T(8,128)(2,1)S(1)} %get-tuple-element.33), channel_id=1, source_target_pairs={{0,1},{1,0},{2,3},{3,2},{4,5},{5,4},{6,7},{7,6},{8,9},{9,8},{10,11... | collective-permute-start | bytes 442376 | tf_op jit(solution)/shard_map/ppermute | solution.py:500
  19.8 14.1 %collective-permute-start.2 = (bf16[2,384,128]{2,1,0:T(8,128)(2,1)S(1)}, bf16[2,384,128]{2,1,0:T(8,128)(2,1)S(1)}, u32[]{:S(2)}, u32[]{:S(2)}) collective-permute-start(bf16[2,384,128]{2,1,0:T(8,128)(2,1)S(1)} %get-tuple-element.24.grad_high_ref.refs_2_), channel_id=1, source_target_pairs={{0,2},{2,4},{4,6},{6,8},{8,10},{10,12},{12,14},{14,16},{16,18},{18... | collective-permute-start | bytes 589832 | tf_op jit(solution)/shard_map/ppermute | solution.py:385
  23.4 10.6 %collective-permute-start.3 = (bf16[2,384,128]{2,1,0:T(8,128)(2,1)S(1)}, bf16[2,384,128]{2,1,0:T(8,128)(2,1)S(1)}, u32[]{:S(2)}, u32[]{:S(2)}) collective-permute-start(bf16[2,384,128]{2,1,0:T(8,128)(2,1)S(1)} %get-tuple-element.25.grad_low_ref.refs_1_), channel_id=1, source_target_pairs={{2,0},{4,2},{6,4},{8,6},{10,8},{12,10},{14,12},{16,14},{18,16},{20... | collective-permute-start | bytes 589832 | tf_op jit(solution)/shard_map/ppermute | solution.py:385
  25.4 16.4 %all-to-all-start = ((bf16[16,36,128]{2,1,0:T(8,128)(2,1)}), bf16[16,36,128]{2,1,0:T(8,128)(2,1)S(1)}, u32[]{:S(2)}, u32[]{:S(2)}) async-start(bf16[16,36,128]{2,1,0:T(8,128)(2,1)} %add_convert_fusion), calls=%async_computation | async-start | bytes 327680 | tf_op jit(solution)/shard_map/all_to_all | solution.py:502

commit v5 on v4

--- a/solution.py
+++ b/solution.py
@@ -109,7 +109,7 @@
 
 def first_kernel(
     rates_ref, lists_ref, x_hbm, cot_hbm, w_hbm, bias_ref,
-    gcat_hbm, pre_ref, xt_ref, total_ref, mask_ref, cot_ref, back_ref, near_ref, far_ref,
+    grad_ref, pre_ref, xt_ref, total_ref, mask_ref, cot_ref, back_ref, near_ref, far_ref,
     xbuf, cbuf, wbuf, pad, xcat, gcat_ref, wide, sems,
 ):
     rows, columns, channels = x_hbm.shape
@@ -123,13 +123,6 @@
             loads.append(
                 pltpu.make_async_copy(source.at[part], target.at[part], sems.at[base + k])
             )
-    inner = rows - 2 * HALO
-    stores = [
-        pltpu.make_async_copy(
-            gcat_ref.at[pl.ds(k, 2)], gcat_hbm.at[pl.ds(k, 2)], sems.at[9 + k // 2]
-        )
-        for k in range(0, inner, 2)
-    ]
     for load in loads:
         load.start()
     for k, value in enumerate(cell_masks(lists_ref, mine, tiles_row, columns)):
@@ -185,18 +178,14 @@
                 if HALO <= row < rows - HALO:
                     grad = silu_grad(half_cot.astype(F32), half_pre)
                     spread(grad, pad, row, gcat_ref.at[row - HALO], -rate)
+                    grad_ref[row - HALO] = grad.astype(BF16)
                     ready.append(row)
-                    there.add(row)
-                    mate = row ^ 1
-                    if mate in there:
-                        stores[(row - HALO) // 2].start()
                 else:
                     here = row if row < HALO else row - (rows - 2 * HALO)
                     pre_ref[here] = half_pre
                     cot_ref[here] = half_cot
 
         ready = []
-        there = set()
         summed = []
         waiting = None
         for pair in row_pairs(rate, range(rows)) + [None]:
@@ -212,8 +201,6 @@
                 del ready[:2]
 
     by_rate(rates_ref[0, mine], body)
-    for store in stores:
-        store.wait()
 
 
 def rims_kernel(
@@ -290,7 +277,7 @@
 
 def last_kernel(
     rates_ref, from_low_ref, from_high_ref, grad_low_ref, grad_high_ref,
-    gcat_hbm, cot_hbm, mask_ref, back_ref, far_ref,
+    grad_ref, cot_hbm, mask_ref, back_ref, far_ref,
     out_hbm,
     cbuf, obuf, pad, gcat, spare, terms, sems,
 ):
@@ -300,24 +287,18 @@
     last = rates_ref.shape[1] - 1
     around = 2 * HALO
     chunks = rows // around
-    loads = [
-        pltpu.make_async_copy(
-            gcat_hbm.at[pl.ds(k, 2)], gcat.at[pl.ds(HALO + k, 2)], sems.at[k // 2]
-        )
-        for k in range(0, inner, 2)
-    ]
     cots, stores = [], []
     for k in range(chunks):
         part = pl.ds(k * around, around)
         cots.append(
-            pltpu.make_async_copy(cot_hbm.at[part], cbuf.at[part], sems.at[inner // 2 + k])
+            pltpu.make_async_copy(cot_hbm.at[part], cbuf.at[part], sems.at[k])
         )
         stores.append(
-            pltpu.make_async_copy(obuf.at[part], out_hbm.at[part], sems.at[inner // 2 + chunks + k])
+            pltpu.make_async_copy(obuf.at[part], out_hbm.at[part], sems.at[chunks + k])
         )
-    for load in loads + cots:
+    for load in cots:
         load.start()
-    clear_ends(pad, 4 * HALO, columns)
+    clear_ends(pad, rows, columns)
 
     def neighbour(side, rate):
         ref = from_high_ref if side else from_low_ref
@@ -341,16 +322,28 @@
         by_rate(rates_ref[0, near[side]], lambda rate, side=side: neighbour(side, rate))
 
     def body(rate):
-        for side, ref in enumerate((grad_low_ref, grad_high_ref)):
-            for k in range(HALO):
-                slot = side * HALO + k
-                spread(ref[k], pad, 2 * HALO + slot, gcat.at[k + side * (rows - HALO)], -rate)
-        for load in loads + cots:
-            load.wait()
+        done = set()
+
+        def shifted(row):
+            if row not in done:
+                done.add(row)
+                if row < HALO:
+                    value = grad_low_ref[row]
+                elif row < rows - HALO:
+                    value = grad_ref[row - HALO]
+                else:
+                    value = grad_high_ref[row - (rows - HALO)]
+                spread(value, pad, row, gcat.at[row], -rate)
+            return gcat.at[row]
+
         for chunk in range(chunks):
             start = chunk * around
-            for pair in row_pairs(rate, range(start, start + around)):
-                sums = input_sums(pair, rate, rows, lambda row: gcat.at[row], back_ref)
+            results = [
+                (pair, input_sums(pair, rate, rows, shifted, back_ref))
+                for pair in row_pairs(rate, range(start, start + around))
+            ]
+            cots[chunk].wait()
+            for pair, sums in results:
                 for row, value in zip(pair, sums):
                     value = value + cbuf[row].astype(F32)
                     if row < HALO:
@@ -376,6 +369,10 @@
         copy.start()
     for copy in copies:
         copy.wait()
+
+
+def add_kernel(keep_ref, other_ref, sum_ref):
+    sum_ref[...] = (keep_ref[...] + other_ref[...].astype(F32)).astype(BF16)
 
 
 def exchange(to_next, to_previous, axis):
@@ -435,11 +432,11 @@
     )(in_hbm(x))
     low, high = exchange(last_rows, first_rows, "tile")
 
-    gcat, pre, xt, total, mask, cot_edge, back, near, far = call(
+    grad, pre, xt, total, mask, cot_edge, back, near, far = call(
         first_kernel,
         "first",
         [
-            ((inner, columns, wide_row), BF16),
+            ((inner, columns, channels), BF16),
             ((2 * HALO, columns, channels), F32),
             ((rows, channels, columns), BF16),
             ((wide_row, wide_row), F32),
@@ -449,7 +446,7 @@
             ((2, wide_row, channels), BF16),
             ((2, wide_row, channels), BF16),
         ],
-        "svhhhv>hvvvvvvvv",
+        "svhhhv>vvvvvvvvv",
         [
             pltpu.VMEM((rows, columns, channels), BF16),
             pltpu.VMEM((rows, columns, channels), BF16),
@@ -458,7 +455,7 @@
             pltpu.VMEM((rows, columns, wide_row), BF16),
             pltpu.VMEM((inner, columns, wide_row), BF16),
             pltpu.VMEM((4 * wide_row, 2 * channels), BF16),
-            pltpu.SemaphoreType.DMA((9 + inner // 2,)),
+            pltpu.SemaphoreType.DMA((9,)),
         ],
         flops=BUSY,
     )(dilations, lists, in_hbm(x), cot, weight, bias)
@@ -498,7 +495,7 @@
     )(dilations, grad_low, grad_high, xt, xt_halo, total)
     if paired:
         other = lax.ppermute(send, "dp", [(0, 1), (1, 0)])
-        both = (keep + other.astype(F32)).astype(BF16)
+        (both,) = call(add_kernel, "add", [(share + (channels,), BF16)], "vv>v", [])(keep, other)
         received = lax.all_to_all(both, "tile", 0, 0, tiled=True)
     else:
         received = lax.all_to_all(
@@ -509,20 +506,20 @@
         last_kernel,
         "last",
         [whole],
-        "svvvvhhvvv>h",
+        "svvvvvhvvv>h",
         [
             pltpu.VMEM((rows, columns, channels), BF16),
             pltpu.VMEM((rows, columns, channels), BF16),
-            pads(4 * HALO),
+            pads(rows),
             pltpu.VMEM((rows, columns, wide_row), BF16),
             pltpu.VMEM((2, HALO * columns, wide_row), BF16),
             pltpu.VMEM((2 * HALO, columns, channels), F32),
-            pltpu.SemaphoreType.DMA((inner // 2 + 2 * (rows // (2 * HALO)),)),
+            pltpu.SemaphoreType.DMA((2 * (rows // (2 * HALO)),)),
         ],
         flops=BUSY,
     )(
         dilations, from_low, from_high, grad_low, grad_high,
-        in_hbm(gcat), cot, mask, back, far,
+        grad, cot, mask, back, far,
     )
     summed = jnp.sum(received.astype(F32), axis=0)
     return (input_grad[None], summed.reshape(-1))

time: 42.9 us -> 44.7 us (1.042)
  waiting for transfers between devices: 4.83 us -> 6.68 us
  other arithmetic: 1.34 us -> 0.64 us
  Pallas kernels: 16 us -> 16.6 us
    ppermute x1, waiting for transfers between devices: 0.01 us -> 1.38 us  [shards(): other = lax.ppermute(send, 'dp', [(0, 1), (1, 0)])]
    convert_element_type x1 -> x0, other arithmetic: 0.7 us -> none  [shards(): both = (keep + other.astype(F32)).astype(BF16)]
    all_to_all x1, waiting for transfers between devices: 2.48 us -> 3.12 us  [shards(): received = lax.all_to_all(both, 'tile', 0, 0, tiled=True)]
    all_to_all x1, starting transfers between devices: 8.45 us -> 8.9 us  [shards(): received = lax.all_to_all(both, 'tile', 0, 0, tiled=True)]
    pallas_call x2 -> x3, Pallas kernels: 12.1 us -> 12.5 us  [the longest x1 6.8 us: shards(): call(first_kernel, 'first', [((inner, columns, channels), BF16), ((2 * HA...]
  transfers between devices with their start and end apart: 6 -> 6, of which waited for: 3 -> 3; matrix products, arithmetic and copies ran while one was open for 2% -> 0% of each run, Pallas kernels for 28% -> 32%
where the time goes in v5:
time: 44.7 us; the launch traced here: 44.3 us
  starting transfers between devices  19.6 us (44%)
  Pallas kernels  16.6 us (37%)
  waiting for transfers between devices  6.68 us (15%)
  between operations  0.74 us (2%)
  other arithmetic  0.64 us (1%)
    all_to_all x1, starting transfers between devices, shards(): received = lax.all_to_all(both, 'tile', 0, 0, tiled=True)  8.9 us
    ppermute x2, starting transfers between devices, exchange(): lax.ppermute(to_next, axis, forward)  8.08 us
    pallas_call x1, Pallas kernels, shards(): call(first_kernel, 'first', [((inner, columns, channels), BF16), ((2 * HA...  6.8 us
    pallas_call x1, Pallas kernels, shards(): call(last_kernel, 'last', [whole], 'svvvvvhvvv>h', [pltpu.VMEM((rows, col...  4.99 us
    all_to_all x1, waiting for transfers between devices, shards(): received = lax.all_to_all(both, 'tile', 0, 0, tiled=True)  3.12 us
    ppermute x2, starting transfers between devices, exchange(): lax.ppermute(to_previous, axis, backward)  2.58 us
    ppermute x2, waiting for transfers between devices, exchange(): lax.ppermute(to_previous, axis, backward)  2.17 us
    pallas_call x1, Pallas kernels, shards(): call(lambda *refs: taps_kernel(*refs, scale=scale, paired=paired), 'taps'...  1.64 us
  transfers between devices with their start and end apart: 6, of which 3 were waited for; matrix products, arithmetic and copies ran while one was open for 0% of the time, Pallas kernels for 32%

profile of v5, /device:TPU:0, one launch (start us, length us, event | category | flops | bytes accessed | tf_op | source)
XLA Modules:
  0.0 44.3 jit_solution(10169956050959363069)
XLA Ops:
  0.6 1.1 %cut.1 = (bf16[2,384,128]{2,1,0:T(8,128)(2,1)S(1)}, bf16[2,384,128]{2,1,0:T(8,128)(2,1)S(1)}) custom-call(bf16[12,384,128]{2,1,0:T(8,128)(2,1)} %bitcast.7), custom_call_target="tpu_custom_call" | custom-call | tf_op jit(solution)/shard_map/cut/pallas_call | solution.py:426
  1.7 4.9 %collective-permute-start = (bf16[2,384,128]{2,1,0:T(8,128)(2,1)S(1)}, bf16[2,384,128]{2,1,0:T(8,128)(2,1)S(1)}, u32[]{:S(2)}, u32[]{:S(2)}) collective-permute-start(bf16[2,384,128]{2,1,0:T(8,128)(2,1)S(1)} %get-tuple-element.18), channel_id=1, source_target_pairs={{0,2},{2,4},{4,6},{6,8},{8,10},{10,12},{12,14},{14,16},{16,18},{18... | collective-permute-start | bytes 589832 | tf_op jit(solution)/shard_map/ppermute | solution.py:382
  6.6 1.3 %collective-permute-start.1 = (bf16[2,384,128]{2,1,0:T(8,128)(2,1)S(1)}, bf16[2,384,128]{2,1,0:T(8,128)(2,1)S(1)}, u32[]{:S(2)}, u32[]{:S(2)}) collective-permute-start(bf16[2,384,128]{2,1,0:T(8,128)(2,1)S(1)} %get-tuple-element.19), channel_id=1, source_target_pairs={{2,0},{4,2},{6,4},{8,6},{10,8},{12,10},{14,12},{16,14},{18,16},{20... | collective-permute-start | bytes 589832 | tf_op jit(solution)/shard_map/ppermute | solution.py:382
  7.9 6.8 %first.1 = (bf16[8,384,128]{2,1,0:T(8,128)(2,1)S(1)}, f32[4,384,128]{2,1,0:T(8,128)S(1)}, bf16[12,128,384]{2,1,0:T(8,128)(2,1)S(1)}, f32[384,384]{1,0:T(8,128)S(...) custom-call(s32[1,16]{1,0:T(1,128)} %refs_0_.1, ...), custom_call_target="tpu_custom_call" | custom-call | flops 20000000000 | tf_op jit(solution)/shard_map/first/pallas_call | solution.py:435
  14.7 0.0 collective-permute-done.low_ref
  14.7 2.2 %collective-permute-done.1.high_ref = bf16[2,384,128]{2,1,0:T(8,128)(2,1)S(1)} collective-permute-done((bf16[2,384,128]{2,1,0:T(8,128)(2,1)S(1)}, bf16[2,384,128]{2,1,0:T(8,128)(2,1)S(1)}, u32[]{:S(2)}, u32[]{:S(2)}) %collective-permute-start.1) | collective-permute-done | bytes 196640 | tf_op jit(solution)/shard_map/ppermute | solution.py:382
  16.9 1.4 %rims.1 = (bf16[2,384,128]{2,1,0:T(8,128)(2,1)S(1)}, bf16[2,384,128]{2,1,0:T(8,128)(2,1)S(1)}, bf16[4,128,384]{2,1,0:T(8,128)(2,1)S(1)}) custom-call(s32[1,16]{1,0:T(1,128)} %refs_0_.1, bf16[2,384,128]{2,1,0:T(8,128)(2,1)S(1)} %collective-permute-done.low_ref, bf16[2,384,128]{2,1,0:T(8,128)(2,1)S(1)} %collective-permute-done.1.high_ref, ...), custom_call_target="tpu_custom_call" | custom-call | tf_op jit(solution)/shard_map/rims/pallas_call | solution.py:463
  18.3 3.2 %collective-permute-start.2 = (bf16[2,384,128]{2,1,0:T(8,128)(2,1)S(1)}, bf16[2,384,128]{2,1,0:T(8,128)(2,1)S(1)}, u32[]{:S(2)}, u32[]{:S(2)}) collective-permute-start(bf16[2,384,128]{2,1,0:T(8,128)(2,1)S(1)} %get-tuple-element.24.grad_high_ref.refs_2_), channel_id=1, source_target_pairs={{0,2},{2,4},{4,6},{6,8},{8,10},{10,12},{12,14},{14,16},{16,18},{18... | collective-permute-start | bytes 589832 | tf_op jit(solution)/shard_map/ppermute | solution.py:382
  21.5 1.3 %collective-permute-start.3 = (bf16[2,384,128]{2,1,0:T(8,128)(2,1)S(1)}, bf16[2,384,128]{2,1,0:T(8,128)(2,1)S(1)}, u32[]{:S(2)}, u32[]{:S(2)}) collective-permute-start(bf16[2,384,128]{2,1,0:T(8,128)(2,1)S(1)} %get-tuple-element.25.grad_low_ref.refs_1_), channel_id=1, source_target_pairs={{2,0},{4,2},{6,4},{8,6},{10,8},{12,10},{14,12},{16,14},{18,16},{20... | collective-permute-start | bytes 589832 | tf_op jit(solution)/shard_map/ppermute | solution.py:382
  22.8 1.6 %taps.1 = (f32[16,36,128]{2,1,0:T(8,128)S(1)}, bf16[16,36,128]{2,1,0:T(8,128)(2,1)S(1)}) custom-call(s32[1,16]{1,0:T(1,128)} %refs_0_.1, bf16[2,384,128]{2,1,0:T(8,128)(2,1)S(1)} %get-tuple-element.25.grad_low_ref.refs_1_, bf16[2,384,128]{2,1,0:T(8,128)(2,1)S(1)} %get-tuple-element.24.grad_high_ref.refs_2_, ...), custom_call_target="tpu_custom_call" | custom-call | tf_op jit(solution)/shard_map/taps/pallas_call | solution.py:482
  24.5 0.1 collective-permute-start.4
  24.5 1.4 %collective-permute-done.4.other_ref = bf16[16,36,128]{2,1,0:T(8,128)(2,1)S(1)} collective-permute-done((bf16[16,36,128]{2,1,0:T(8,128)(2,1)S(1)}, bf16[16,36,128]{2,1,0:T(8,128)(2,1)S(1)}, u32[]{:S(2)}, u32[]{:S(2)}) %collective-permute-start.4) | collective-permute-done | bytes 147488 | tf_op jit(solution)/shard_map/ppermute | solution.py:497
  25.9 0.7 %add.1 = bf16[16,36,128]{2,1,0:T(8,128)(2,1)} custom-call(f32[16,36,128]{2,1,0:T(8,128)S(1)} %get-tuple-element.32.keep_ref, bf16[16,36,128]{2,1,0:T(8,128)(2,1)S(1)} %collective-permute-done.4.other_ref), custom_call_target="tpu_custom_call" | custom-call | tf_op jit(solution)/shard_map/add/pallas_call | solution.py:498
  26.6 8.9 %all-to-all-start = ((bf16[16,36,128]{2,1,0:T(8,128)(2,1)}), bf16[16,36,128]{2,1,0:T(8,128)(2,1)S(1)}, u32[]{:S(2)}, u32[]{:S(2)}) async-start(bf16[16,36,128]{2,1,0:T(8,128)(2,1)} %add.1), calls=%async_computation | async-start | bytes 327680 | tf_op jit(solution)/shard_map/all_to_all | solution.py:499
  35.5 0.0 collective-permute-done.2.from_low_ref
  35.5 0.0 collective-permute-done.3.from_high_ref
  35.5 5.0 %last.1 = bf16[12,384,128]{2,1,0:T(8,128)(2,1)} custom-call(s32[1,16]{1,0:T(1,128)} %refs_0_.1, bf16[2,384,128]{2,1,0:T(8,128)(2,1)S(1)} %collective-permute-done.2.from_low_ref, bf16[2,384,128]{2,1,0:T(8,128)(2,1)S(1)} %collective-permute-done.3.from_high_ref, bf16[2,384,128]{2,1,0:T(8,128)(2,1)S(1)} %get-tuple-element.25.grad_low_ref.refs_1_, ...), custom_call_target="tpu_custom_call" | custom-call | flops 20000000000 | tf_op jit(solution)/shard_map/last/pallas_call | solution.py:505
  40.5 3.1 %all-to-all-done = bf16[16,36,128]{2,1,0:T(8,128)(2,1)S(1)} async-done(((bf16[16,36,128]{2,1,0:T(8,128)(2,1)}), bf16[16,36,128]{2,1,0:T(8,128)(2,1)S(1)}, u32[]{:S(2)}, u32[]{:S(2)}) %all-to-all-start) | async-done | bytes 147488 | tf_op jit(solution)/shard_map/all_to_all | solution.py:499
  43.6 0.6 %convert_reduce_fusion = f32[36,128]{1,0:T(8,128)} fusion(bf16[16,36,128]{2,1,0:T(8,128)(2,1)S(1)} %all-to-all-done), kind=kLoop, calls=%fused_computation | loop fusion | flops 142848 | bytes 165888 | tf_op jit(solution)/shard_map/reduce_sum | solution.py:524
Async XLA Ops:
  1.7 13.0 %collective-permute-start = (bf16[2,384,128]{2,1,0:T(8,128)(2,1)S(1)}, bf16[2,384,128]{2,1,0:T(8,128)(2,1)S(1)}, u32[]{:S(2)}, u32[]{:S(2)}) collective-permute-start(bf16[2,384,128]{2,1,0:T(8,128)(2,1)S(1)} %get-tuple-element.18), channel_id=1, source_target_pairs={{0,2},{2,4},{4,6},{6,8},{8,10},{10,12},{12,14},{14,16},{16,18},{18... | collective-permute-start | bytes 589832 | tf_op jit(solution)/shard_map/ppermute | solution.py:382
  6.6 10.3 %collective-permute-start.1 = (bf16[2,384,128]{2,1,0:T(8,128)(2,1)S(1)}, bf16[2,384,128]{2,1,0:T(8,128)(2,1)S(1)}, u32[]{:S(2)}, u32[]{:S(2)}) collective-permute-start(bf16[2,384,128]{2,1,0:T(8,128)(2,1)S(1)} %get-tuple-element.19), channel_id=1, source_target_pairs={{2,0},{4,2},{6,4},{8,6},{10,8},{12,10},{14,12},{16,14},{18,16},{20... | collective-permute-start | bytes 589832 | tf_op jit(solution)/shard_map/ppermute | solution.py:382
  18.3 17.2 %collective-permute-start.2 = (bf16[2,384,128]{2,1,0:T(8,128)(2,1)S(1)}, bf16[2,384,128]{2,1,0:T(8,128)(2,1)S(1)}, u32[]{:S(2)}, u32[]{:S(2)}) collective-permute-start(bf16[2,384,128]{2,1,0:T(8,128)(2,1)S(1)} %get-tuple-element.24.grad_high_ref.refs_2_), channel_id=1, source_target_pairs={{0,2},{2,4},{4,6},{6,8},{8,10},{10,12},{12,14},{14,16},{16,18},{18... | collective-permute-start | bytes 589832 | tf_op jit(solution)/shard_map/ppermute | solution.py:382
  21.5 14.0 %collective-permute-start.3 = (bf16[2,384,128]{2,1,0:T(8,128)(2,1)S(1)}, bf16[2,384,128]{2,1,0:T(8,128)(2,1)S(1)}, u32[]{:S(2)}, u32[]{:S(2)}) collective-permute-start(bf16[2,384,128]{2,1,0:T(8,128)(2,1)S(1)} %get-tuple-element.25.grad_low_ref.refs_1_), channel_id=1, source_target_pairs={{2,0},{4,2},{6,4},{8,6},{10,8},{12,10},{14,12},{16,14},{18,16},{20... | collective-permute-start | bytes 589832 | tf_op jit(solution)/shard_map/ppermute | solution.py:382
  24.5 1.5 %collective-permute-start.4 = (bf16[16,36,128]{2,1,0:T(8,128)(2,1)S(1)}, bf16[16,36,128]{2,1,0:T(8,128)(2,1)S(1)}, u32[]{:S(2)}, u32[]{:S(2)}) collective-permute-start(bf16[16,36,128]{2,1,0:T(8,128)(2,1)S(1)} %get-tuple-element.33), channel_id=1, source_target_pairs={{0,1},{1,0},{2,3},{3,2},{4,5},{5,4},{6,7},{7,6},{8,9},{9,8},{10,11... | collective-permute-start | bytes 442376 | tf_op jit(solution)/shard_map/ppermute | solution.py:497
  26.6 17.0 %all-to-all-start = ((bf16[16,36,128]{2,1,0:T(8,128)(2,1)}), bf16[16,36,128]{2,1,0:T(8,128)(2,1)S(1)}, u32[]{:S(2)}, u32[]{:S(2)}) async-start(bf16[16,36,128]{2,1,0:T(8,128)(2,1)} %add.1), calls=%async_computation | async-start | bytes 327680 | tf_op jit(solution)/shard_map/all_to_all | solution.py:499

commit v6 on v5

--- a/solution.py
+++ b/solution.py
@@ -70,6 +70,17 @@
     target_ref[:, :channels] = pad_ref[slot, pl.ds(EDGE - offset, columns)].astype(BF16)
     target_ref[:, channels : 2 * channels] = value.astype(BF16)
     target_ref[:, 2 * channels :] = pad_ref[slot, pl.ds(EDGE + offset, columns)].astype(BF16)
+
+
+def by_side(a_ref, b_ref, sides_ref):
+    odd = lax.axis_index("tile") % 2
+
+    def order(low, high):
+        sides_ref[0] = low[...]
+        sides_ref[1] = high[...]
+
+    pl.when(odd == 0)(lambda: order(b_ref, a_ref))
+    pl.when(odd == 1)(lambda: order(a_ref, b_ref))
 
 
 def silu_grad(half_cot, half_pre):
@@ -204,24 +215,24 @@
 
 
 def rims_kernel(
-    rates_ref, low_ref, high_ref, pre_ref, cot_ref, mask_ref, near_ref,
-    grad_low_ref, grad_high_ref, xt_ref,
-    pad, xcat,
+    rates_ref, a_ref, b_ref, pre_ref, cot_ref, mask_ref, near_ref,
+    grad_a_ref, grad_b_ref, xt_ref,
+    pad, xcat, halo, grads,
 ):
-    _, columns, channels = low_ref.shape
+    _, columns, channels = a_ref.shape
     clear_ends(pad, 2 * HALO, columns)
+    by_side(a_ref, b_ref, halo)
 
     def body(rate):
-        for side, ref in enumerate((low_ref, high_ref)):
+        for side in range(2):
             used = range(HALO - rate, HALO) if side == 0 else range(rate)
             for place, k in enumerate(used):
-                value = ref[k] * mask_ref[2 * side]
-                spread(
-                    value, pad, side * HALO + k, xcat.at[pl.ds(place * columns, columns)], rate
-                )
+                value = halo[side, k] * mask_ref[2 * side]
+                part = pl.ds(place * columns, columns)
+                spread(value, pad, side * HALO + k, xcat.at[side, part], rate)
                 xt_ref[side * HALO + k] = value.T
             sums = jnp.dot(
-                xcat[: rate * columns], near_ref[side], preferred_element_type=F32
+                xcat[side, : rate * columns], near_ref[side], preferred_element_type=F32
             )
             for k in range(HALO):
                 half_pre = pre_ref[side * HALO + k]
@@ -229,18 +240,21 @@
                 if 0 <= place < rate:
                     half_pre += 0.5 * sums[place * columns : (place + 1) * columns]
                 grad = silu_grad(cot_ref[side * HALO + k].astype(F32), half_pre)
-                target = grad_high_ref if side else grad_low_ref
-                target[k] = grad.astype(BF16)
+                grads[side, k] = grad.astype(BF16)
 
     by_rate(rates_ref[0, lax.axis_index("tile")], body)
+    odd = lax.axis_index("tile") % 2
+    grad_a_ref[...] = grads[1 - odd]
+    grad_b_ref[...] = grads[odd]
 
 
 def taps_kernel(
-    rates_ref, grad_low_ref, grad_high_ref, xt_own_ref, xt_halo_ref, total_ref,
+    rates_ref, grad_a_ref, grad_b_ref, xt_own_ref, xt_halo_ref, total_ref,
     keep_ref, send_ref,
-    pad, gedge_ref, flat, *, scale, paired,
+    pad, gedge_ref, flat, sides, *, scale, paired,
 ):
-    _, columns, channels = grad_low_ref.shape
+    _, columns, channels = grad_a_ref.shape
+    by_side(grad_a_ref, grad_b_ref, sides)
     rows = xt_own_ref.shape[0]
     clear_ends(pad, 2 * HALO, columns)
 
@@ -251,10 +265,10 @@
 
     def body(rate):
         edges = []
-        for side, ref in enumerate((grad_low_ref, grad_high_ref)):
+        for side in range(2):
             for k in range(HALO):
                 slot = side * HALO + k
-                spread(ref[k], pad, slot, gedge_ref.at[slot], -rate)
+                spread(sides[side, k], pad, slot, gedge_ref.at[slot], -rate)
                 edges.append((k + side * (rows - HALO), gedge_ref.at[slot]))
         total = (total_ref[...] + tap_sums(edges, flipped, rate)) * scale
         for a in range(3):
@@ -276,10 +290,10 @@
 
 
 def last_kernel(
-    rates_ref, from_low_ref, from_high_ref, grad_low_ref, grad_high_ref,
+    rates_ref, from_a_ref, from_b_ref, grad_a_ref, grad_b_ref,
     grad_ref, cot_hbm, mask_ref, back_ref, far_ref,
     out_hbm,
-    cbuf, obuf, pad, gcat, spare, terms, sems,
+    cbuf, obuf, pad, gcat, spare, theirs, ours, sems,
 ):
     rows, columns, channels = cot_hbm.shape
     inner = rows - 2 * HALO
@@ -298,28 +312,22 @@
         )
     for load in cots:
         load.start()
-    clear_ends(pad, rows, columns)
-
-    def neighbour(side, rate):
-        ref = from_high_ref if side else from_low_ref
-        used = range(rate) if side else range(HALO - rate, HALO)
-        for place, k in enumerate(used):
-            spread(
-                ref[k], pad, side * HALO + k, spare.at[side, pl.ds(place * columns, columns)], -rate
-            )
-        sums = jnp.dot(
-            spare[side, : rate * columns], far_ref[side], preferred_element_type=F32
-        )
+    clear_ends(pad, rows + 2 * HALO, columns)
+    by_side(from_a_ref, from_b_ref, theirs)
+    by_side(grad_a_ref, grad_b_ref, ours)
+
+    def neighbour(side):
+        rate = rates_ref[0, jnp.minimum(mine + 1, last) if side else jnp.maximum(mine - 1, 0)]
         for k in range(HALO):
-            place = k - (HALO - rate) if side else k
-            if 0 <= place < rate:
-                terms[side * HALO + k] = sums[place * columns : (place + 1) * columns]
-            else:
-                terms[side * HALO + k] = jnp.zeros((columns, channels), F32)
-
-    near = (jnp.maximum(mine - 1, 0), jnp.minimum(mine + 1, last))
-    for side in range(2):
-        by_rate(rates_ref[0, near[side]], lambda rate, side=side: neighbour(side, rate))
+            part = pl.ds(k * columns, columns)
+            spread(theirs[side, k], pad, rows + side * HALO + k, spare.at[side, part], -rate)
+        sums = jnp.dot(spare[side], far_ref[side], preferred_element_type=F32)
+        parts = [sums[k * columns : (k + 1) * columns] for k in range(HALO)]
+        none = jnp.zeros((columns, channels), F32)
+        one = rate == 1
+        if side:
+            return [jnp.where(one, none, parts[0]), jnp.where(one, parts[0], parts[1])]
+        return [jnp.where(one, parts[1], parts[0]), jnp.where(one, none, parts[1])]
 
     def body(rate):
         done = set()
@@ -328,11 +336,11 @@
             if row not in done:
                 done.add(row)
                 if row < HALO:
-                    value = grad_low_ref[row]
+                    value = ours[0, row]
                 elif row < rows - HALO:
                     value = grad_ref[row - HALO]
                 else:
-                    value = grad_high_ref[row - (rows - HALO)]
+                    value = ours[1, row - (rows - HALO)]
                 spread(value, pad, row, gcat.at[row], -rate)
             return gcat.at[row]
 
@@ -342,14 +350,16 @@
                 (pair, input_sums(pair, rate, rows, shifted, back_ref))
                 for pair in row_pairs(rate, range(start, start + around))
             ]
+            terms = {0: 0, chunks - 1: 1}
+            added = neighbour(terms[chunk]) if chunk in terms else None
             cots[chunk].wait()
             for pair, sums in results:
                 for row, value in zip(pair, sums):
                     value = value + cbuf[row].astype(F32)
                     if row < HALO:
-                        value = value + terms[row]
+                        value = value + added[row]
                     elif row >= rows - HALO:
-                        value = value + terms[row - inner]
+                        value = value + added[row - (rows - HALO)]
                     obuf[row] = value.astype(BF16) * mask_ref[1]
             stores[chunk].start()
 
@@ -358,28 +368,29 @@
         store.wait()
 
 
-def cut_kernel(x_hbm, low_ref, high_ref, sems):
+def cut_kernel(x_hbm, a_ref, b_ref, sems):
     rows = x_hbm.shape[0]
-    copies = [
-        pltpu.make_async_copy(x_hbm.at[row], ref.at[k], sems.at[side, k])
-        for side, ref in enumerate((low_ref, high_ref))
-        for k, row in enumerate(range(side * (rows - HALO), side * (rows - HALO) + HALO))
-    ]
+    odd = lax.axis_index("tile") % 2
+    copies = []
+    for index, ref in enumerate((a_ref, b_ref)):
+        start = (rows - HALO) * (odd if index else 1 - odd)
+        for k in range(HALO):
+            copies.append(
+                pltpu.make_async_copy(x_hbm.at[start + k], ref.at[k], sems.at[index, k])
+            )
     for copy in copies:
         copy.start()
     for copy in copies:
         copy.wait()
 
 
-def add_kernel(keep_ref, other_ref, sum_ref):
-    sum_ref[...] = (keep_ref[...] + other_ref[...].astype(F32)).astype(BF16)
-
-
-def exchange(to_next, to_previous, axis):
+def swap(rows_a, rows_b, axis):
     count = lax.axis_size(axis)
-    forward = [(i, i + 1) for i in range(count - 1)]
-    backward = [(target, source) for source, target in forward]
-    return lax.ppermute(to_next, axis, forward), lax.ppermute(to_previous, axis, backward)
+    results = []
+    for start, rows in ((0, rows_a), (1, rows_b)):
+        pairs = [(i, i + 1) for i in range(start, count - 1, 2)]
+        results.append(lax.ppermute(rows, axis, pairs + [(j, i) for i, j in pairs]))
+    return results
 
 
 def call(kernel, name, outs, specs, scratch, aliases=None, flops=0):
@@ -423,14 +434,15 @@
         return pltpu.VMEM((count, columns + 2 * EDGE, channels), F32)
 
     rim = ((HALO, columns, channels), BF16)
-    first_rows, last_rows = call(
+    sides = pltpu.VMEM((2, HALO, columns, channels), BF16)
+    rows_a, rows_b = call(
         cut_kernel,
         "cut",
         [rim, rim],
         "h>vv",
         [pltpu.SemaphoreType.DMA((2, HALO))],
     )(in_hbm(x))
-    low, high = exchange(last_rows, first_rows, "tile")
+    x_a, x_b = swap(rows_a, rows_b, "tile")
 
     grad, pre, xt, total, mask, cot_edge, back, near, far = call(
         first_kernel,
@@ -460,7 +472,7 @@
         flops=BUSY,
     )(dilations, lists, in_hbm(x), cot, weight, bias)
 
-    grad_low, grad_high, xt_halo = call(
+    grad_a, grad_b, xt_halo = call(
         rims_kernel,
         "rims",
         [
@@ -469,10 +481,10 @@
             ((2 * HALO, channels, columns), BF16),
         ],
         "svvvvvv>vvv",
-        [pads(2 * HALO), pltpu.VMEM((HALO * columns, wide_row), BF16)],
-    )(dilations, low, high, pre, cot_edge, mask, near)
-
-    from_low, from_high = exchange(grad_high, grad_low, "tile")
+        [pads(2 * HALO), pltpu.VMEM((2, HALO * columns, wide_row), BF16), sides, sides],
+    )(dilations, x_a, x_b, pre, cot_edge, mask, near)
+
+    from_a, from_b = swap(grad_a, grad_b, "tile")
 
     tap_rows = 9 * channels
     cores = lax.axis_size("dp")
@@ -491,11 +503,12 @@
             pads(2 * HALO),
             pltpu.VMEM((2 * HALO, columns, wide_row), BF16),
             pltpu.VMEM((tap_rows, channels), F32),
-        ],
-    )(dilations, grad_low, grad_high, xt, xt_halo, total)
+            sides,
+        ],
+    )(dilations, grad_a, grad_b, xt, xt_halo, total)
     if paired:
         other = lax.ppermute(send, "dp", [(0, 1), (1, 0)])
-        (both,) = call(add_kernel, "add", [(share + (channels,), BF16)], "vv>v", [])(keep, other)
+        both = (keep + other.astype(F32)).astype(BF16)
         received = lax.all_to_all(both, "tile", 0, 0, tiled=True)
     else:
         received = lax.all_to_all(
@@ -510,15 +523,16 @@
         [
             pltpu.VMEM((rows, columns, channels), BF16),
             pltpu.VMEM((rows, columns, channels), BF16),
-            pads(rows),
+            pads(rows + 2 * HALO),
             pltpu.VMEM((rows, columns, wide_row), BF16),
             pltpu.VMEM((2, HALO * columns, wide_row), BF16),
-            pltpu.VMEM((2 * HALO, columns, channels), F32),
+            sides,
+            sides,
             pltpu.SemaphoreType.DMA((2 * (rows // (2 * HALO)),)),
         ],
         flops=BUSY,
     )(
-        dilations, from_low, from_high, grad_low, grad_high,
+        dilations, from_a, from_b, grad_a, grad_b,
         grad, cot, mask, back, far,
     )
     summed = jnp.sum(received.astype(F32), axis=0)

time: 44.7 us -> 38.6 us (0.86)
  waiting for transfers between devices: 6.68 us -> 2.97 us
  starting transfers between devices: 19.6 us -> 17.5 us
  Pallas kernels: 16.6 us -> 15.6 us
  other arithmetic: 0.64 us -> 1.32 us
    ppermute x4, waiting for transfers between devices: 2.18 us -> 0.01 us  [swap(): results.append(lax.ppermute(rows, axis, pairs + [(j, i) for i, j in pairs]))]
    ppermute x4, starting transfers between devices: 10.7 us -> 8.9 us  [swap(): results.append(lax.ppermute(rows, axis, pairs + [(j, i) for i, j in pairs]))]
    ppermute x1, waiting for transfers between devices: 1.38 us -> 0.01 us  [shards(): other = lax.ppermute(send, 'dp', [(0, 1), (1, 0)])]
    convert_element_type x0 -> x1, other arithmetic: none -> 0.69 us  [shards(): both = (keep + other.astype(F32)).astype(BF16)]
    pallas_call x1 -> x0, Pallas kernels: 0.68 us -> none  [shards(): call(add_kernel, 'add', [(share + (channels,), BF16)], 'vv>v', [])]
  transfers between devices with their start and end apart: 6 -> 6, of which waited for: 3 -> 1; matrix products, arithmetic and copies ran while one was open for 0% -> 2% of each run, Pallas kernels for 32% -> 30%
where the time goes in v6:
time: 38.6 us; the launch traced here: 38.2 us
  starting transfers between devices  17.5 us (45%)
  Pallas kernels  15.6 us (40%)
  waiting for transfers between devices  2.97 us (8%)
  other arithmetic  1.32 us (3%)
  between operations  0.74 us (2%)
    ppermute x4, starting transfers between devices, swap(): results.append(lax.ppermute(rows, axis, pairs + [(j, i) for i, j in pairs]))  8.9 us
    all_to_all x1, starting transfers between devices, shards(): received = lax.all_to_all(both, 'tile', 0, 0, tiled=True)  8.58 us
    pallas_call x1, Pallas kernels, shards(): call(first_kernel, 'first', [((inner, columns, channels), BF16), ((2 * HA...  6.6 us
    pallas_call x1, Pallas kernels, shards(): call(last_kernel, 'last', [whole], 'svvvvvhvvv>h', [pltpu.VMEM((rows, col...  4.94 us
    all_to_all x1, waiting for transfers between devices, shards(): received = lax.all_to_all(both, 'tile', 0, 0, tiled=True)  2.96 us
    pallas_call x1, Pallas kernels, shards(): call(lambda *refs: taps_kernel(*refs, scale=scale, paired=paired), 'taps'...  1.67 us
    pallas_call x1, Pallas kernels, shards(): call(rims_kernel, 'rims', [rim, rim, ((2 * HALO, channels, columns), BF16...  1.27 us
    pallas_call x1, Pallas kernels, shards(): call(cut_kernel, 'cut', [rim, rim], 'h>vv', [pltpu.SemaphoreType.DMA((2,...  1.09 us
  transfers between devices with their start and end apart: 6, of which 1 were waited for; matrix products, arithmetic and copies ran while one was open for 2% of the time, Pallas kernels for 30%

profile of v6, /device:TPU:0, one launch (start us, length us, event | category | flops | bytes accessed | tf_op | source)
XLA Modules:
  0.0 38.2 jit_solution(5524851851967981630)
XLA Ops:
  0.6 1.1 %cut.1 = (bf16[2,384,128]{2,1,0:T(8,128)(2,1)S(1)}, bf16[2,384,128]{2,1,0:T(8,128)(2,1)S(1)}) custom-call(bf16[12,384,128]{2,1,0:T(8,128)(2,1)} %bitcast.7), custom_call_target="tpu_custom_call" | custom-call | tf_op jit(solution)/shard_map/cut/pallas_call | solution.py:438
  1.7 3.0 %collective-permute-start = (bf16[2,384,128]{2,1,0:T(8,128)(2,1)S(1)}, bf16[2,384,128]{2,1,0:T(8,128)(2,1)S(1)}, u32[]{:S(2)}, u32[]{:S(2)}) collective-permute-start(bf16[2,384,128]{2,1,0:T(8,128)(2,1)S(1)} %get-tuple-element.18), channel_id=1, source_target_pairs={{0,2},{4,6},{8,10},{12,14},{16,18},{20,22},{24,26},{28,30},{2,0},{... | collective-permute-start | bytes 589832 | tf_op jit(solution)/shard_map/ppermute | solution.py:392
  4.7 0.7 %collective-permute-start.1 = (bf16[2,384,128]{2,1,0:T(8,128)(2,1)S(1)}, bf16[2,384,128]{2,1,0:T(8,128)(2,1)S(1)}, u32[]{:S(2)}, u32[]{:S(2)}) collective-permute-start(bf16[2,384,128]{2,1,0:T(8,128)(2,1)S(1)} %get-tuple-element.19), channel_id=1, source_target_pairs={{2,4},{6,8},{10,12},{14,16},{18,20},{22,24},{26,28},{4,2},{8,6},{1... | collective-permute-start | bytes 589832 | tf_op jit(solution)/shard_map/ppermute | solution.py:392
  5.4 6.6 %first.1 = (bf16[8,384,128]{2,1,0:T(8,128)(2,1)S(1)}, f32[4,384,128]{2,1,0:T(8,128)S(1)}, bf16[12,128,384]{2,1,0:T(8,128)(2,1)S(1)}, f32[384,384]{1,0:T(8,128)S(...) custom-call(s32[1,16]{1,0:T(1,128)} %refs_0_.1, ...), custom_call_target="tpu_custom_call" | custom-call | flops 20000000000 | tf_op jit(solution)/shard_map/first/pallas_call | solution.py:447
  12.0 0.0 collective-permute-done.a_ref
  12.0 0.0 collective-permute-done.1.b_ref
  12.0 1.3 %rims.1 = (bf16[2,384,128]{2,1,0:T(8,128)(2,1)S(1)}, bf16[2,384,128]{2,1,0:T(8,128)(2,1)S(1)}, bf16[4,128,384]{2,1,0:T(8,128)(2,1)S(1)}) custom-call(s32[1,16]{1,0:T(1,128)} %refs_0_.1, bf16[2,384,128]{2,1,0:T(8,128)(2,1)S(1)} %collective-permute-done.a_ref, bf16[2,384,128]{2,1,0:T(8,128)(2,1)S(1)} %collective-permute-done.1.b_ref, ...), custom_call_target="tpu_custom_call" | custom-call | tf_op jit(solution)/shard_map/rims/pallas_call | solution.py:475
  13.3 1.7 %taps.1 = (f32[16,36,128]{2,1,0:T(8,128)S(1)}, bf16[16,36,128]{2,1,0:T(8,128)(2,1)S(1)}) custom-call(s32[1,16]{1,0:T(1,128)} %refs_0_.1, bf16[2,384,128]{2,1,0:T(8,128)(2,1)S(1)} %get-tuple-element.24.grad_a_ref.refs_1_, bf16[2,384,128]{2,1,0:T(8,128)(2,1)S(1)} %get-tuple-element.25.grad_b_ref.refs_2_, bf16[12,128,384]{2,1,0:T(8,128)(2,1)S(1)} %get-tuple-element.29.refs_3_, ...), custom_call_target="tpu_custom_call" | custom-call | tf_op jit(solution)/shard_map/taps/pallas_call | solution.py:494
  15.0 0.1 collective-permute-start.4
  15.1 4.6 %collective-permute-start.2 = (bf16[2,384,128]{2,1,0:T(8,128)(2,1)S(1)}, bf16[2,384,128]{2,1,0:T(8,128)(2,1)S(1)}, u32[]{:S(2)}, u32[]{:S(2)}) collective-permute-start(bf16[2,384,128]{2,1,0:T(8,128)(2,1)S(1)} %get-tuple-element.24.grad_a_ref.refs_1_), channel_id=1, source_target_pairs={{0,2},{4,6},{8,10},{12,14},{16,18},{20,22},{24,26},{28,30},{2,0},{... | collective-permute-start | bytes 589832 | tf_op jit(solution)/shard_map/ppermute | solution.py:392
  19.6 0.7 %collective-permute-start.3 = (bf16[2,384,128]{2,1,0:T(8,128)(2,1)S(1)}, bf16[2,384,128]{2,1,0:T(8,128)(2,1)S(1)}, u32[]{:S(2)}, u32[]{:S(2)}) collective-permute-start(bf16[2,384,128]{2,1,0:T(8,128)(2,1)S(1)} %get-tuple-element.25.grad_b_ref.refs_2_), channel_id=1, source_target_pairs={{2,4},{6,8},{10,12},{14,16},{18,20},{22,24},{26,28},{4,2},{8,6},{1... | collective-permute-start | bytes 589832 | tf_op jit(solution)/shard_map/ppermute | solution.py:392
  20.3 0.0 collective-permute-done.4
  20.3 0.7 %add_convert_fusion = bf16[16,36,128]{2,1,0:T(8,128)(2,1)} fusion(f32[16,36,128]{2,1,0:T(8,128)S(1)} %get-tuple-element.32, bf16[16,36,128]{2,1,0:T(8,128)(2,1)S(1)} %collective-permute-done.4), kind=kLoop, calls=%fused_computation.1 | loop fusion | flops 221184 | bytes 589824 | tf_op jit(solution)/shard_map/convert_element_type | solution.py:511
  21.0 8.6 %all-to-all-start = ((bf16[16,36,128]{2,1,0:T(8,128)(2,1)}), bf16[16,36,128]{2,1,0:T(8,128)(2,1)S(1)}, u32[]{:S(2)}, u32[]{:S(2)}) async-start(bf16[16,36,128]{2,1,0:T(8,128)(2,1)} %add_convert_fusion), calls=%async_computation | async-start | bytes 327680 | tf_op jit(solution)/shard_map/all_to_all | solution.py:512
  29.6 0.0 collective-permute-done.2.from_a_ref
  29.6 0.0 collective-permute-done.3.from_b_ref
  29.6 4.9 %last.1 = bf16[12,384,128]{2,1,0:T(8,128)(2,1)} custom-call(s32[1,16]{1,0:T(1,128)} %refs_0_.1, bf16[2,384,128]{2,1,0:T(8,128)(2,1)S(1)} %collective-permute-done.2.from_a_ref, bf16[2,384,128]{2,1,0:T(8,128)(2,1)S(1)} %collective-permute-done.3.from_b_ref, bf16[2,384,128]{2,1,0:T(8,128)(2,1)S(1)} %get-tuple-element.24.grad_a_ref.refs_1_, ...), custom_call_target="tpu_custom_call" | custom-call | flops 20000000000 | tf_op jit(solution)/shard_map/last/pallas_call | solution.py:518
  34.6 3.0 %all-to-all-done = bf16[16,36,128]{2,1,0:T(8,128)(2,1)S(1)} async-done(((bf16[16,36,128]{2,1,0:T(8,128)(2,1)}), bf16[16,36,128]{2,1,0:T(8,128)(2,1)S(1)}, u32[]{:S(2)}, u32[]{:S(2)}) %all-to-all-start) | async-done | bytes 147488 | tf_op jit(solution)/shard_map/all_to_all | solution.py:512
  37.5 0.6 %convert_reduce_fusion = f32[36,128]{1,0:T(8,128)} fusion(bf16[16,36,128]{2,1,0:T(8,128)(2,1)S(1)} %all-to-all-done), kind=kLoop, calls=%fused_computation | loop fusion | flops 142848 | bytes 165888 | tf_op jit(solution)/shard_map/reduce_sum | solution.py:538
Async XLA Ops:
  1.7 10.3 %collective-permute-start = (bf16[2,384,128]{2,1,0:T(8,128)(2,1)S(1)}, bf16[2,384,128]{2,1,0:T(8,128)(2,1)S(1)}, u32[]{:S(2)}, u32[]{:S(2)}) collective-permute-start(bf16[2,384,128]{2,1,0:T(8,128)(2,1)S(1)} %get-tuple-element.18), channel_id=1, source_target_pairs={{0,2},{4,6},{8,10},{12,14},{16,18},{20,22},{24,26},{28,30},{2,0},{... | collective-permute-start | bytes 589832 | tf_op jit(solution)/shard_map/ppermute | solution.py:392
  4.7 7.3 %collective-permute-start.1 = (bf16[2,384,128]{2,1,0:T(8,128)(2,1)S(1)}, bf16[2,384,128]{2,1,0:T(8,128)(2,1)S(1)}, u32[]{:S(2)}, u32[]{:S(2)}) collective-permute-start(bf16[2,384,128]{2,1,0:T(8,128)(2,1)S(1)} %get-tuple-element.19), channel_id=1, source_target_pairs={{2,4},{6,8},{10,12},{14,16},{18,20},{22,24},{26,28},{4,2},{8,6},{1... | collective-permute-start | bytes 589832 | tf_op jit(solution)/shard_map/ppermute | solution.py:392
  15.0 5.3 %collective-permute-start.4 = (bf16[16,36,128]{2,1,0:T(8,128)(2,1)S(1)}, bf16[16,36,128]{2,1,0:T(8,128)(2,1)S(1)}, u32[]{:S(2)}, u32[]{:S(2)}) collective-permute-start(bf16[16,36,128]{2,1,0:T(8,128)(2,1)S(1)} %get-tuple-element.33), channel_id=1, source_target_pairs={{0,1},{1,0},{2,3},{3,2},{4,5},{5,4},{6,7},{7,6},{8,9},{9,8},{10,11... | collective-permute-start | bytes 442376 | tf_op jit(solution)/shard_map/ppermute | solution.py:510
  15.1 14.5 %collective-permute-start.2 = (bf16[2,384,128]{2,1,0:T(8,128)(2,1)S(1)}, bf16[2,384,128]{2,1,0:T(8,128)(2,1)S(1)}, u32[]{:S(2)}, u32[]{:S(2)}) collective-permute-start(bf16[2,384,128]{2,1,0:T(8,128)(2,1)S(1)} %get-tuple-element.24.grad_a_ref.refs_1_), channel_id=1, source_target_pairs={{0,2},{4,6},{8,10},{12,14},{16,18},{20,22},{24,26},{28,30},{2,0},{... | collective-permute-start | bytes 589832 | tf_op jit(solution)/shard_map/ppermute | solution.py:392
  19.6 10.0 %collective-permute-start.3 = (bf16[2,384,128]{2,1,0:T(8,128)(2,1)S(1)}, bf16[2,384,128]{2,1,0:T(8,128)(2,1)S(1)}, u32[]{:S(2)}, u32[]{:S(2)}) collective-permute-start(bf16[2,384,128]{2,1,0:T(8,128)(2,1)S(1)} %get-tuple-element.25.grad_b_ref.refs_2_), channel_id=1, source_target_pairs={{2,4},{6,8},{10,12},{14,16},{18,20},{22,24},{26,28},{4,2},{8,6},{1... | collective-permute-start | bytes 589832 | tf_op jit(solution)/shard_map/ppermute | solution.py:392
  21.0 16.5 %all-to-all-start = ((bf16[16,36,128]{2,1,0:T(8,128)(2,1)}), bf16[16,36,128]{2,1,0:T(8,128)(2,1)S(1)}, u32[]{:S(2)}, u32[]{:S(2)}) async-start(bf16[16,36,128]{2,1,0:T(8,128)(2,1)} %add_convert_fusion), calls=%async_computation | async-start | bytes 327680 | tf_op jit(solution)/shard_map/all_to_all | solution.py:512

commit v7 on v6

--- a/solution.py
+++ b/solution.py
@@ -250,10 +250,11 @@
 
 def taps_kernel(
     rates_ref, grad_a_ref, grad_b_ref, xt_own_ref, xt_halo_ref, total_ref,
-    keep_ref, send_ref,
+    keep_ref, send_ref, later_ref,
     pad, gedge_ref, flat, sides, *, scale, paired,
 ):
     _, columns, channels = grad_a_ref.shape
+    later_ref[...] = grad_b_ref[...]
     by_side(grad_a_ref, grad_b_ref, sides)
     rows = xt_own_ref.shape[0]
     clear_ends(pad, 2 * HALO, columns)
@@ -384,13 +385,13 @@
         copy.wait()
 
 
-def swap(rows_a, rows_b, axis):
-    count = lax.axis_size(axis)
-    results = []
-    for start, rows in ((0, rows_a), (1, rows_b)):
-        pairs = [(i, i + 1) for i in range(start, count - 1, 2)]
-        results.append(lax.ppermute(rows, axis, pairs + [(j, i) for i, j in pairs]))
-    return results
+def add_kernel(keep_ref, other_ref, sum_ref):
+    sum_ref[...] = (keep_ref[...] + other_ref[...].astype(F32)).astype(BF16)
+
+
+def swap(rows, axis, start):
+    pairs = [(i, i + 1) for i in range(start, lax.axis_size(axis) - 1, 2)]
+    return lax.ppermute(rows, axis, pairs + [(j, i) for i, j in pairs])
 
 
 def call(kernel, name, outs, specs, scratch, aliases=None, flops=0):
@@ -442,7 +443,7 @@
         "h>vv",
         [pltpu.SemaphoreType.DMA((2, HALO))],
     )(in_hbm(x))
-    x_a, x_b = swap(rows_a, rows_b, "tile")
+    x_a, x_b = swap(rows_a, "tile", 0), swap(rows_b, "tile", 1)
 
     grad, pre, xt, total, mask, cot_edge, back, near, far = call(
         first_kernel,
@@ -484,21 +485,22 @@
         [pads(2 * HALO), pltpu.VMEM((2, HALO * columns, wide_row), BF16), sides, sides],
     )(dilations, x_a, x_b, pre, cot_edge, mask, near)
 
-    from_a, from_b = swap(grad_a, grad_b, "tile")
+    from_a = swap(grad_a, "tile", 0)
 
     tap_rows = 9 * channels
     cores = lax.axis_size("dp")
     paired = cores == 2 and tap_rows % devices == 0
     share = (devices // 2, tap_rows // devices) if paired else (1, tap_rows)
     scale = 1.0 / math.sqrt(devices * lists.shape[1] * TILE * TILE)
-    keep, send = call(
+    keep, send, later_b = call(
         lambda *refs: taps_kernel(*refs, scale=scale, paired=paired),
         "taps",
         [
             (share + (channels,), F32),
             (share + (channels,), BF16),
-        ],
-        "svvvvv>vv",
+            rim,
+        ],
+        "svvvvv>vvv",
         [
             pads(2 * HALO),
             pltpu.VMEM((2 * HALO, columns, wide_row), BF16),
@@ -506,9 +508,10 @@
             sides,
         ],
     )(dilations, grad_a, grad_b, xt, xt_halo, total)
+    from_b = swap(later_b, "tile", 1)
     if paired:
         other = lax.ppermute(send, "dp", [(0, 1), (1, 0)])
-        both = (keep + other.astype(F32)).astype(BF16)
+        (both,) = call(add_kernel, "add", [(share + (channels,), BF16)], "vv>v", [])(keep, other)
         received = lax.all_to_all(both, "tile", 0, 0, tiled=True)
     else:
         received = lax.all_to_all(
@@ -532,7 +535,7 @@
         ],
         flops=BUSY,
     )(
-        dilations, from_a, from_b, grad_a, grad_b,
+        dilations, from_a, from_b, grad_a, later_b,
         grad, cot, mask, back, far,
     )
     summed = jnp.sum(received.astype(F32), axis=0)

time: 38.6 us -> 40.2 us (1.041)
  waiting for transfers between devices: 2.97 us -> 4.57 us
  Pallas kernels: 15.6 us -> 16.6 us
  other arithmetic: 1.32 us -> 0.64 us
    all_to_all x1, starting transfers between devices: 8.58 us -> 7.17 us  [shards(): received = lax.all_to_all(both, 'tile', 0, 0, tiled=True)]
    ppermute x1, waiting for transfers between devices: 0.01 us -> 1.39 us  [shards(): other = lax.ppermute(send, 'dp', [(0, 1), (1, 0)])]
    ppermute x4, starting transfers between devices: 8.9 us -> 10.1 us  [swap(): return lax.ppermute(rows, axis, pairs + [(j, i) for i, j in pairs])]
    convert_element_type x1 -> x0, other arithmetic: 0.69 us -> none  [shards(): both = (keep + other.astype(F32)).astype(BF16)]
    pallas_call x0 -> x1, Pallas kernels: none -> 0.68 us  [shards(): call(add_kernel, 'add', [(share + (channels,), BF16)], 'vv>v', [])]
  transfers between devices with their start and end apart: 6 -> 6, of which waited for: 1 -> 2; matrix products, arithmetic and copies ran while one was open for 2% -> 0% of each run, Pallas kernels for 30% -> 31%
where the time goes in v7:
time: 40.2 us; the launch traced here: 39.8 us
  starting transfers between devices  17.3 us (43%)
  Pallas kernels  16.6 us (41%)
  waiting for transfers between devices  4.57 us (11%)
  between operations  0.73 us (2%)
  other arithmetic  0.64 us (2%)
    ppermute x4, starting transfers between devices, swap(): return lax.ppermute(rows, axis, pairs + [(j, i) for i, j in pairs])  10.1 us
    all_to_all x1, starting transfers between devices, shards(): received = lax.all_to_all(both, 'tile', 0, 0, tiled=True)  7.17 us
    pallas_call x1, Pallas kernels, shards(): call(first_kernel, 'first', [((inner, columns, channels), BF16), ((2 * HA...  6.8 us
    pallas_call x1, Pallas kernels, shards(): call(last_kernel, 'last', [whole], 'svvvvvhvvv>h', [pltpu.VMEM((rows, col...  4.94 us
    all_to_all x1, waiting for transfers between devices, shards(): received = lax.all_to_all(both, 'tile', 0, 0, tiled=True)  3.17 us
    pallas_call x1, Pallas kernels, shards(): call(lambda *refs: taps_kernel(*refs, scale=scale, paired=paired), 'taps'...  1.67 us
    pallas_call x1, Pallas kernels, shards(): call(rims_kernel, 'rims', [rim, rim, ((2 * HALO, channels, columns), BF16...  1.42 us
    ppermute x1, waiting for transfers between devices, shards(): other = lax.ppermute(send, 'dp', [(0, 1), (1, 0)])  1.39 us
  transfers between devices with their start and end apart: 6, of which 2 were waited for; matrix products, arithmetic and copies ran while one was open for 0% of the time, Pallas kernels for 31%

profile of v7, /device:TPU:0, one launch (start us, length us, event | category | flops | bytes accessed | tf_op | source)
XLA Modules:
  0.0 39.8 jit_solution(5356507325228666208)
XLA Ops:
  0.6 1.1 %cut.1 = (bf16[2,384,128]{2,1,0:T(8,128)(2,1)S(1)}, bf16[2,384,128]{2,1,0:T(8,128)(2,1)S(1)}) custom-call(bf16[12,384,128]{2,1,0:T(8,128)(2,1)} %bitcast.7), custom_call_target="tpu_custom_call" | custom-call | tf_op jit(solution)/shard_map/cut/pallas_call | solution.py:439
  1.7 3.0 %collective-permute-start = (bf16[2,384,128]{2,1,0:T(8,128)(2,1)S(1)}, bf16[2,384,128]{2,1,0:T(8,128)(2,1)S(1)}, u32[]{:S(2)}, u32[]{:S(2)}) collective-permute-start(bf16[2,384,128]{2,1,0:T(8,128)(2,1)S(1)} %get-tuple-element.19), channel_id=1, source_target_pairs={{0,2},{4,6},{8,10},{12,14},{16,18},{20,22},{24,26},{28,30},{2,0},{... | collective-permute-start | bytes 589832 | tf_op jit(solution)/shard_map/ppermute | solution.py:394
  4.7 0.7 %collective-permute-start.1 = (bf16[2,384,128]{2,1,0:T(8,128)(2,1)S(1)}, bf16[2,384,128]{2,1,0:T(8,128)(2,1)S(1)}, u32[]{:S(2)}, u32[]{:S(2)}) collective-permute-start(bf16[2,384,128]{2,1,0:T(8,128)(2,1)S(1)} %get-tuple-element.20), channel_id=1, source_target_pairs={{2,4},{6,8},{10,12},{14,16},{18,20},{22,24},{26,28},{4,2},{8,6},{1... | collective-permute-start | bytes 589832 | tf_op jit(solution)/shard_map/ppermute | solution.py:394
  5.4 6.8 %first.1 = (bf16[8,384,128]{2,1,0:T(8,128)(2,1)S(1)}, f32[4,384,128]{2,1,0:T(8,128)S(1)}, bf16[12,128,384]{2,1,0:T(8,128)(2,1)S(1)}, f32[384,384]{1,0:T(8,128)S(...) custom-call(s32[1,16]{1,0:T(1,128)} %rates_ref.5, ...), custom_call_target="tpu_custom_call" | custom-call | flops 20000000000 | tf_op jit(solution)/shard_map/first/pallas_call | solution.py:448
  12.2 0.0 collective-permute-done.a_ref
  12.2 0.0 collective-permute-done.1.b_ref
  12.2 1.4 %rims.1 = (bf16[2,384,128]{2,1,0:T(8,128)(2,1)S(1)}, bf16[2,384,128]{2,1,0:T(8,128)(2,1)S(1)}, bf16[4,128,384]{2,1,0:T(8,128)(2,1)S(1)}) custom-call(s32[1,16]{1,0:T(1,128)} %rates_ref.5, bf16[2,384,128]{2,1,0:T(8,128)(2,1)S(1)} %collective-permute-done.a_ref, bf16[2,384,128]{2,1,0:T(8,128)(2,1)S(1)} %collective-permute-done.1.b_ref, ...), custom_call_target="tpu_custom_call" | custom-call | tf_op jit(solution)/shard_map/rims/pallas_call | solution.py:476
  13.7 1.7 %taps.1 = (f32[16,36,128]{2,1,0:T(8,128)S(1)}, bf16[16,36,128]{2,1,0:T(8,128)(2,1)S(1)}, bf16[2,384,128]{2,1,0:T(8,128)(2,1)S(1)}) custom-call(s32[1,16]{1,0:T(1,128)} %rates_ref.5, bf16[2,384,128]{2,1,0:T(8,128)(2,1)S(1)} %get-tuple-element.25.refs_1_.grad_a_ref, bf16[2,384,128]{2,1,0:T(8,128)(2,1)S(1)} %get-tuple-element.26.refs_2_, ...), custom_call_target="tpu_custom_call" | custom-call | tf_op jit(solution)/shard_map/taps/pallas_call | solution.py:495
  15.3 0.7 %collective-permute-start.3 = (bf16[2,384,128]{2,1,0:T(8,128)(2,1)S(1)}, bf16[2,384,128]{2,1,0:T(8,128)(2,1)S(1)}, u32[]{:S(2)}, u32[]{:S(2)}) collective-permute-start(bf16[2,384,128]{2,1,0:T(8,128)(2,1)S(1)} %get-tuple-element.30.grad_b_ref), channel_id=1, source_target_pairs={{2,4},{6,8},{10,12},{14,16},{18,20},{22,24},{26,28},{4,2},{8,6},{1... | collective-permute-start | bytes 589832 | tf_op jit(solution)/shard_map/ppermute | solution.py:394
  16.0 5.8 %collective-permute-start.2 = (bf16[2,384,128]{2,1,0:T(8,128)(2,1)S(1)}, bf16[2,384,128]{2,1,0:T(8,128)(2,1)S(1)}, u32[]{:S(2)}, u32[]{:S(2)}) collective-permute-start(bf16[2,384,128]{2,1,0:T(8,128)(2,1)S(1)} %get-tuple-element.25.refs_1_.grad_a_ref), channel_id=1, source_target_pairs={{0,2},{4,6},{8,10},{12,14},{16,18},{20,22},{24,26},{28,30},{2,0},{... | collective-permute-start | bytes 589832 | tf_op jit(solution)/shard_map/ppermute | solution.py:394
  21.8 0.0 collective-permute-start.4
  21.8 1.4 %collective-permute-done.4.other_ref = bf16[16,36,128]{2,1,0:T(8,128)(2,1)S(1)} collective-permute-done((bf16[16,36,128]{2,1,0:T(8,128)(2,1)S(1)}, bf16[16,36,128]{2,1,0:T(8,128)(2,1)S(1)}, u32[]{:S(2)}, u32[]{:S(2)}) %collective-permute-start.4) | collective-permute-done | bytes 147488 | tf_op jit(solution)/shard_map/ppermute | solution.py:513
  23.2 0.7 %add.1 = bf16[16,36,128]{2,1,0:T(8,128)(2,1)} custom-call(f32[16,36,128]{2,1,0:T(8,128)S(1)} %get-tuple-element.34.keep_ref, bf16[16,36,128]{2,1,0:T(8,128)(2,1)S(1)} %collective-permute-done.4.other_ref), custom_call_target="tpu_custom_call" | custom-call | tf_op jit(solution)/shard_map/add/pallas_call | solution.py:514
  23.9 7.2 %all-to-all-start = ((bf16[16,36,128]{2,1,0:T(8,128)(2,1)}), bf16[16,36,128]{2,1,0:T(8,128)(2,1)S(1)}, u32[]{:S(2)}, u32[]{:S(2)}) async-start(bf16[16,36,128]{2,1,0:T(8,128)(2,1)} %add.1), calls=%async_computation | async-start | bytes 327680 | tf_op jit(solution)/shard_map/all_to_all | solution.py:515
  31.0 0.0 collective-permute-done.3.from_b_ref
  31.1 0.0 collective-permute-done.2.from_a_ref
  31.1 4.9 %last.1 = bf16[12,384,128]{2,1,0:T(8,128)(2,1)} custom-call(s32[1,16]{1,0:T(1,128)} %rates_ref.5, bf16[2,384,128]{2,1,0:T(8,128)(2,1)S(1)} %collective-permute-done.2.from_a_ref, bf16[2,384,128]{2,1,0:T(8,128)(2,1)S(1)} %collective-permute-done.3.from_b_ref, bf16[2,384,128]{2,1,0:T(8,128)(2,1)S(1)} %get-tuple-element.25.refs_1_.grad_a_ref, ...), custom_call_target="tpu_custom_call" | custom-call | flops 20000000000 | tf_op jit(solution)/shard_map/last/pallas_call | solution.py:521
  36.0 3.2 %all-to-all-done = bf16[16,36,128]{2,1,0:T(8,128)(2,1)S(1)} async-done(((bf16[16,36,128]{2,1,0:T(8,128)(2,1)}), bf16[16,36,128]{2,1,0:T(8,128)(2,1)S(1)}, u32[]{:S(2)}, u32[]{:S(2)}) %all-to-all-start) | async-done | bytes 147488 | tf_op jit(solution)/shard_map/all_to_all | solution.py:515
  39.2 0.6 %convert_reduce_fusion = f32[36,128]{1,0:T(8,128)} fusion(bf16[16,36,128]{2,1,0:T(8,128)(2,1)S(1)} %all-to-all-done), kind=kLoop, calls=%fused_computation | loop fusion | flops 142848 | bytes 165888 | tf_op jit(solution)/shard_map/reduce_sum | solution.py:541
Async XLA Ops:
  1.7 10.5 %collective-permute-start = (bf16[2,384,128]{2,1,0:T(8,128)(2,1)S(1)}, bf16[2,384,128]{2,1,0:T(8,128)(2,1)S(1)}, u32[]{:S(2)}, u32[]{:S(2)}) collective-permute-start(bf16[2,384,128]{2,1,0:T(8,128)(2,1)S(1)} %get-tuple-element.19), channel_id=1, source_target_pairs={{0,2},{4,6},{8,10},{12,14},{16,18},{20,22},{24,26},{28,30},{2,0},{... | collective-permute-start | bytes 589832 | tf_op jit(solution)/shard_map/ppermute | solution.py:394
  4.7 7.5 %collective-permute-start.1 = (bf16[2,384,128]{2,1,0:T(8,128)(2,1)S(1)}, bf16[2,384,128]{2,1,0:T(8,128)(2,1)S(1)}, u32[]{:S(2)}, u32[]{:S(2)}) collective-permute-start(bf16[2,384,128]{2,1,0:T(8,128)(2,1)S(1)} %get-tuple-element.20), channel_id=1, source_target_pairs={{2,4},{6,8},{10,12},{14,16},{18,20},{22,24},{26,28},{4,2},{8,6},{1... | collective-permute-start | bytes 589832 | tf_op jit(solution)/shard_map/ppermute | solution.py:394
  15.3 15.7 %collective-permute-start.3 = (bf16[2,384,128]{2,1,0:T(8,128)(2,1)S(1)}, bf16[2,384,128]{2,1,0:T(8,128)(2,1)S(1)}, u32[]{:S(2)}, u32[]{:S(2)}) collective-permute-start(bf16[2,384,128]{2,1,0:T(8,128)(2,1)S(1)} %get-tuple-element.30.grad_b_ref), channel_id=1, source_target_pairs={{2,4},{6,8},{10,12},{14,16},{18,20},{22,24},{26,28},{4,2},{8,6},{1... | collective-permute-start | bytes 589832 | tf_op jit(solution)/shard_map/ppermute | solution.py:394
  16.0 15.0 %collective-permute-start.2 = (bf16[2,384,128]{2,1,0:T(8,128)(2,1)S(1)}, bf16[2,384,128]{2,1,0:T(8,128)(2,1)S(1)}, u32[]{:S(2)}, u32[]{:S(2)}) collective-permute-start(bf16[2,384,128]{2,1,0:T(8,128)(2,1)S(1)} %get-tuple-element.25.refs_1_.grad_a_ref), channel_id=1, source_target_pairs={{0,2},{4,6},{8,10},{12,14},{16,18},{20,22},{24,26},{28,30},{2,0},{... | collective-permute-start | bytes 589832 | tf_op jit(solution)/shard_map/ppermute | solution.py:394
  21.8 1.4 %collective-permute-start.4 = (bf16[16,36,128]{2,1,0:T(8,128)(2,1)S(1)}, bf16[16,36,128]{2,1,0:T(8,128)(2,1)S(1)}, u32[]{:S(2)}, u32[]{:S(2)}) collective-permute-start(bf16[16,36,128]{2,1,0:T(8,128)(2,1)S(1)} %get-tuple-element.35), channel_id=1, source_target_pairs={{0,1},{1,0},{2,3},{3,2},{4,5},{5,4},{6,7},{7,6},{8,9},{9,8},{10,11... | collective-permute-start | bytes 442376 | tf_op jit(solution)/shard_map/ppermute | solution.py:513
  23.9 15.3 %all-to-all-start = ((bf16[16,36,128]{2,1,0:T(8,128)(2,1)}), bf16[16,36,128]{2,1,0:T(8,128)(2,1)S(1)}, u32[]{:S(2)}, u32[]{:S(2)}) async-start(bf16[16,36,128]{2,1,0:T(8,128)(2,1)} %add.1), calls=%async_computation | async-start | bytes 327680 | tf_op jit(solution)/shard_map/all_to_all | solution.py:515

commit v8 on v7

--- a/solution.py
+++ b/solution.py
@@ -385,8 +385,9 @@
         copy.wait()
 
 
-def add_kernel(keep_ref, other_ref, sum_ref):
+def add_kernel(keep_ref, other_ref, rows_ref, sum_ref, later_ref):
     sum_ref[...] = (keep_ref[...] + other_ref[...].astype(F32)).astype(BF16)
+    later_ref[...] = rows_ref[...]
 
 
 def swap(rows, axis, start):
@@ -507,11 +508,14 @@
             pltpu.VMEM((tap_rows, channels), F32),
             sides,
         ],
+        flops=BUSY,
     )(dilations, grad_a, grad_b, xt, xt_halo, total)
     from_b = swap(later_b, "tile", 1)
     if paired:
         other = lax.ppermute(send, "dp", [(0, 1), (1, 0)])
-        (both,) = call(add_kernel, "add", [(share + (channels,), BF16)], "vv>v", [])(keep, other)
+        both, from_a = call(
+            add_kernel, "add", [(share + (channels,), BF16), rim], "vvv>vv", []
+        )(keep, other, from_a)
         received = lax.all_to_all(both, "tile", 0, 0, tiled=True)
     else:
         received = lax.all_to_all(

time: 40.2 us -> 40.3 us (level)
    ppermute x4, starting transfers between devices: 10.1 us -> 8.71 us  [swap(): return lax.ppermute(rows, axis, pairs + [(j, i) for i, j in pairs])]
    all_to_all x1, starting transfers between devices: 7.17 us -> 8.49 us  [shards(): received = lax.all_to_all(both, 'tile', 0, 0, tiled=True)]
  transfers between devices with their start and end apart: 6 -> 6, of which waited for: 2 -> 3; matrix products, arithmetic and copies ran while one was open for 0% -> 0% of each run, Pallas kernels for 31% -> 35%
where the time goes in v8:
time: 40.3 us; the launch traced here: 39.9 us
  starting transfers between devices  17.3 us (43%)
  Pallas kernels  16.6 us (41%)
  waiting for transfers between devices  4.67 us (12%)
  between operations  0.73 us (2%)
  other arithmetic  0.64 us (2%)
    ppermute x4, starting transfers between devices, swap(): return lax.ppermute(rows, axis, pairs + [(j, i) for i, j in pairs])  8.71 us
    all_to_all x1, starting transfers between devices, shards(): received = lax.all_to_all(both, 'tile', 0, 0, tiled=True)  8.49 us
    pallas_call x1, Pallas kernels, shards(): call(first_kernel, 'first', [((inner, columns, channels), BF16), ((2 * HA...  6.8 us
    pallas_call x1, Pallas kernels, shards(): call(last_kernel, 'last', [whole], 'svvvvvhvvv>h', [pltpu.VMEM((rows, col...  4.94 us
    all_to_all x1, waiting for transfers between devices, shards(): received = lax.all_to_all(both, 'tile', 0, 0, tiled=True)  3.18 us
    pallas_call x1, Pallas kernels, shards(): call(lambda *refs: taps_kernel(*refs, scale=scale, paired=paired), 'taps'...  1.66 us
    pallas_call x1, Pallas kernels, shards(): call(rims_kernel, 'rims', [rim, rim, ((2 * HALO, channels, columns), BF16...  1.42 us
    ppermute x1, waiting for transfers between devices, shards(): other = lax.ppermute(send, 'dp', [(0, 1), (1, 0)])  1.38 us
  transfers between devices with their start and end apart: 6, of which 3 were waited for; matrix products, arithmetic and copies ran while one was open for 0% of the time, Pallas kernels for 35%

profile of v8, /device:TPU:0, one launch (start us, length us, event | category | flops | bytes accessed | tf_op | source)
XLA Modules:
  0.0 39.9 jit_solution(6523672795924952296)
XLA Ops:
  0.6 1.1 %cut.1 = (bf16[2,384,128]{2,1,0:T(8,128)(2,1)S(1)}, bf16[2,384,128]{2,1,0:T(8,128)(2,1)S(1)}) custom-call(bf16[12,384,128]{2,1,0:T(8,128)(2,1)} %bitcast.7), custom_call_target="tpu_custom_call" | custom-call | tf_op jit(solution)/shard_map/cut/pallas_call | solution.py:440
  1.7 3.0 %collective-permute-start = (bf16[2,384,128]{2,1,0:T(8,128)(2,1)S(1)}, bf16[2,384,128]{2,1,0:T(8,128)(2,1)S(1)}, u32[]{:S(2)}, u32[]{:S(2)}) collective-permute-start(bf16[2,384,128]{2,1,0:T(8,128)(2,1)S(1)} %get-tuple-element.21), channel_id=1, source_target_pairs={{0,2},{4,6},{8,10},{12,14},{16,18},{20,22},{24,26},{28,30},{2,0},{... | collective-permute-start | bytes 589832 | tf_op jit(solution)/shard_map/ppermute | solution.py:395
  4.7 0.7 %collective-permute-start.1 = (bf16[2,384,128]{2,1,0:T(8,128)(2,1)S(1)}, bf16[2,384,128]{2,1,0:T(8,128)(2,1)S(1)}, u32[]{:S(2)}, u32[]{:S(2)}) collective-permute-start(bf16[2,384,128]{2,1,0:T(8,128)(2,1)S(1)} %get-tuple-element.22), channel_id=1, source_target_pairs={{2,4},{6,8},{10,12},{14,16},{18,20},{22,24},{26,28},{4,2},{8,6},{1... | collective-permute-start | bytes 589832 | tf_op jit(solution)/shard_map/ppermute | solution.py:395
  5.4 6.8 %first.1 = (bf16[8,384,128]{2,1,0:T(8,128)(2,1)S(1)}, f32[4,384,128]{2,1,0:T(8,128)S(1)}, bf16[12,128,384]{2,1,0:T(8,128)(2,1)S(1)}, f32[384,384]{1,0:T(8,128)S(...) custom-call(s32[1,16]{1,0:T(1,128)} %rates_ref.5, ...), custom_call_target="tpu_custom_call" | custom-call | flops 20000000000 | tf_op jit(solution)/shard_map/first/pallas_call | solution.py:449
  12.2 0.0 collective-permute-done.a_ref
  12.2 0.0 collective-permute-done.1.b_ref
  12.2 1.4 %rims.1 = (bf16[2,384,128]{2,1,0:T(8,128)(2,1)S(1)}, bf16[2,384,128]{2,1,0:T(8,128)(2,1)S(1)}, bf16[4,128,384]{2,1,0:T(8,128)(2,1)S(1)}) custom-call(s32[1,16]{1,0:T(1,128)} %rates_ref.5, bf16[2,384,128]{2,1,0:T(8,128)(2,1)S(1)} %collective-permute-done.a_ref, bf16[2,384,128]{2,1,0:T(8,128)(2,1)S(1)} %collective-permute-done.1.b_ref, ...), custom_call_target="tpu_custom_call" | custom-call | tf_op jit(solution)/shard_map/rims/pallas_call | solution.py:477
  13.7 4.4 %collective-permute-start.3 = (bf16[2,384,128]{2,1,0:T(8,128)(2,1)S(1)}, bf16[2,384,128]{2,1,0:T(8,128)(2,1)S(1)}, u32[]{:S(2)}, u32[]{:S(2)}) collective-permute-start(bf16[2,384,128]{2,1,0:T(8,128)(2,1)S(1)} %get-tuple-element.27.refs_1_.grad_a_ref), channel_id=1, source_target_pairs={{0,2},{4,6},{8,10},{12,14},{16,18},{20,22},{24,26},{28,30},{2,0},{... | collective-permute-start | bytes 589832 | tf_op jit(solution)/shard_map/ppermute | solution.py:395
  18.0 1.7 %taps.1 = (f32[16,36,128]{2,1,0:T(8,128)S(1)}, bf16[16,36,128]{2,1,0:T(8,128)(2,1)S(1)}, bf16[2,384,128]{2,1,0:T(8,128)(2,1)S(1)}) custom-call(s32[1,16]{1,0:T(1,128)} %rates_ref.5, bf16[2,384,128]{2,1,0:T(8,128)(2,1)S(1)} %get-tuple-element.27.refs_1_.grad_a_ref, bf16[2,384,128]{2,1,0:T(8,128)(2,1)S(1)} %get-tuple-element.28.refs_2_, ...), custom_call_target="tpu_custom_call" | custom-call | flops 20000000000 | tf_op jit(solution)/shard_map/taps/pallas_call | solution.py:496
  19.7 0.7 %collective-permute-start.4 = (bf16[2,384,128]{2,1,0:T(8,128)(2,1)S(1)}, bf16[2,384,128]{2,1,0:T(8,128)(2,1)S(1)}, u32[]{:S(2)}, u32[]{:S(2)}) collective-permute-start(bf16[2,384,128]{2,1,0:T(8,128)(2,1)S(1)} %get-tuple-element.35.grad_b_ref), channel_id=1, source_target_pairs={{2,4},{6,8},{10,12},{14,16},{18,20},{22,24},{26,28},{4,2},{8,6},{1... | collective-permute-start | bytes 589832 | tf_op jit(solution)/shard_map/ppermute | solution.py:395
  20.4 0.1 collective-permute-start.2
  20.5 1.4 %collective-permute-done.2.other_ref = bf16[16,36,128]{2,1,0:T(8,128)(2,1)S(1)} collective-permute-done((bf16[16,36,128]{2,1,0:T(8,128)(2,1)S(1)}, bf16[16,36,128]{2,1,0:T(8,128)(2,1)S(1)}, u32[]{:S(2)}, u32[]{:S(2)}) %collective-permute-start.2) | collective-permute-done | bytes 147488 | tf_op jit(solution)/shard_map/ppermute | solution.py:515
  21.8 0.1 collective-permute-done.3.rows_ref
  21.9 0.7 %add.1 = (bf16[16,36,128]{2,1,0:T(8,128)(2,1)}, bf16[2,384,128]{2,1,0:T(8,128)(2,1)S(1)}) custom-call(f32[16,36,128]{2,1,0:T(8,128)S(1)} %get-tuple-element.32.keep_ref, bf16[16,36,128]{2,1,0:T(8,128)(2,1)S(1)} %collective-permute-done.2.other_ref, bf16[2,384,128]{2,1,0:T(8,128)(2,1)S(1)} %collective-permute-done.3.rows_ref), custom_call_target="tpu_custom_call" | custom-call | tf_op jit(solution)/shard_map/add/pallas_call | solution.py:516
  22.6 8.5 %all-to-all-start = ((bf16[16,36,128]{2,1,0:T(8,128)(2,1)}), bf16[16,36,128]{2,1,0:T(8,128)(2,1)S(1)}, u32[]{:S(2)}, u32[]{:S(2)}) async-start(bf16[16,36,128]{2,1,0:T(8,128)(2,1)} %get-tuple-element.39), calls=%async_computation | async-start | bytes 327680 | tf_op jit(solution)/shard_map/all_to_all | solution.py:519
  31.1 0.0 collective-permute-done.4.from_b_ref
  31.1 4.9 %last.1 = bf16[12,384,128]{2,1,0:T(8,128)(2,1)} custom-call(s32[1,16]{1,0:T(1,128)} %rates_ref.5, bf16[2,384,128]{2,1,0:T(8,128)(2,1)S(1)} %get-tuple-element.34.from_a_ref, bf16[2,384,128]{2,1,0:T(8,128)(2,1)S(1)} %collective-permute-done.4.from_b_ref, bf16[2,384,128]{2,1,0:T(8,128)(2,1)S(1)} %get-tuple-element.27.refs_1_.grad_a_ref, ...), custom_call_target="tpu_custom_call" | custom-call | flops 20000000000 | tf_op jit(solution)/shard_map/last/pallas_call | solution.py:525
  36.1 3.2 %all-to-all-done = bf16[16,36,128]{2,1,0:T(8,128)(2,1)S(1)} async-done(((bf16[16,36,128]{2,1,0:T(8,128)(2,1)}), bf16[16,36,128]{2,1,0:T(8,128)(2,1)S(1)}, u32[]{:S(2)}, u32[]{:S(2)}) %all-to-all-start) | async-done | bytes 147488 | tf_op jit(solution)/shard_map/all_to_all | solution.py:519
  39.3 0.6 %convert_reduce_fusion = f32[36,128]{1,0:T(8,128)} fusion(bf16[16,36,128]{2,1,0:T(8,128)(2,1)S(1)} %all-to-all-done), kind=kLoop, calls=%fused_computation | loop fusion | flops 142848 | bytes 165888 | tf_op jit(solution)/shard_map/reduce_sum | solution.py:545
Async XLA Ops:
  1.7 10.5 %collective-permute-start = (bf16[2,384,128]{2,1,0:T(8,128)(2,1)S(1)}, bf16[2,384,128]{2,1,0:T(8,128)(2,1)S(1)}, u32[]{:S(2)}, u32[]{:S(2)}) collective-permute-start(bf16[2,384,128]{2,1,0:T(8,128)(2,1)S(1)} %get-tuple-element.21), channel_id=1, source_target_pairs={{0,2},{4,6},{8,10},{12,14},{16,18},{20,22},{24,26},{28,30},{2,0},{... | collective-permute-start | bytes 589832 | tf_op jit(solution)/shard_map/ppermute | solution.py:395
  4.7 7.5 %collective-permute-start.1 = (bf16[2,384,128]{2,1,0:T(8,128)(2,1)S(1)}, bf16[2,384,128]{2,1,0:T(8,128)(2,1)S(1)}, u32[]{:S(2)}, u32[]{:S(2)}) collective-permute-start(bf16[2,384,128]{2,1,0:T(8,128)(2,1)S(1)} %get-tuple-element.22), channel_id=1, source_target_pairs={{2,4},{6,8},{10,12},{14,16},{18,20},{22,24},{26,28},{4,2},{8,6},{1... | collective-permute-start | bytes 589832 | tf_op jit(solution)/shard_map/ppermute | solution.py:395
  13.7 8.3 %collective-permute-start.3 = (bf16[2,384,128]{2,1,0:T(8,128)(2,1)S(1)}, bf16[2,384,128]{2,1,0:T(8,128)(2,1)S(1)}, u32[]{:S(2)}, u32[]{:S(2)}) collective-permute-start(bf16[2,384,128]{2,1,0:T(8,128)(2,1)S(1)} %get-tuple-element.27.refs_1_.grad_a_ref), channel_id=1, source_target_pairs={{0,2},{4,6},{8,10},{12,14},{16,18},{20,22},{24,26},{28,30},{2,0},{... | collective-permute-start | bytes 589832 | tf_op jit(solution)/shard_map/ppermute | solution.py:395
  19.7 11.4 %collective-permute-start.4 = (bf16[2,384,128]{2,1,0:T(8,128)(2,1)S(1)}, bf16[2,384,128]{2,1,0:T(8,128)(2,1)S(1)}, u32[]{:S(2)}, u32[]{:S(2)}) collective-permute-start(bf16[2,384,128]{2,1,0:T(8,128)(2,1)S(1)} %get-tuple-element.35.grad_b_ref), channel_id=1, source_target_pairs={{2,4},{6,8},{10,12},{14,16},{18,20},{22,24},{26,28},{4,2},{8,6},{1... | collective-permute-start | bytes 589832 | tf_op jit(solution)/shard_map/ppermute | solution.py:395
  20.4 1.5 %collective-permute-start.2 = (bf16[16,36,128]{2,1,0:T(8,128)(2,1)S(1)}, bf16[16,36,128]{2,1,0:T(8,128)(2,1)S(1)}, u32[]{:S(2)}, u32[]{:S(2)}) collective-permute-start(bf16[16,36,128]{2,1,0:T(8,128)(2,1)S(1)} %get-tuple-element.33), channel_id=1, source_target_pairs={{0,1},{1,0},{2,3},{3,2},{4,5},{5,4},{6,7},{7,6},{8,9},{9,8},{10,11... | collective-permute-start | bytes 442376 | tf_op jit(solution)/shard_map/ppermute | solution.py:515
  22.6 16.6 %all-to-all-start = ((bf16[16,36,128]{2,1,0:T(8,128)(2,1)}), bf16[16,36,128]{2,1,0:T(8,128)(2,1)S(1)}, u32[]{:S(2)}, u32[]{:S(2)}) async-start(bf16[16,36,128]{2,1,0:T(8,128)(2,1)} %get-tuple-element.39), calls=%async_computation | async-start | bytes 327680 | tf_op jit(solution)/shard_map/all_to_all | solution.py:519

commit v9 on v6

--- a/solution.py
+++ b/solution.py
@@ -384,6 +384,10 @@
         copy.wait()
 
 
+def add_kernel(keep_ref, other_ref, sum_ref):
+    sum_ref[...] = (keep_ref[...] + other_ref[...].astype(F32)).astype(BF16)
+
+
 def swap(rows_a, rows_b, axis):
     count = lax.axis_size(axis)
     results = []
@@ -508,7 +512,7 @@
     )(dilations, grad_a, grad_b, xt, xt_halo, total)
     if paired:
         other = lax.ppermute(send, "dp", [(0, 1), (1, 0)])
-        both = (keep + other.astype(F32)).astype(BF16)
+        (both,) = call(add_kernel, "add", [(share + (channels,), BF16)], "vv>v", [])(keep, other)
         received = lax.all_to_all(both, "tile", 0, 0, tiled=True)
     else:
         received = lax.all_to_all(

time: 38.6 us -> 40.2 us (1.041)
  waiting for transfers between devices: 2.97 us -> 4.56 us
  Pallas kernels: 15.6 us -> 16.3 us
  other arithmetic: 1.32 us -> 0.64 us
    ppermute x1, waiting for transfers between devices: 0.01 us -> 1.38 us  [shards(): other = lax.ppermute(send, 'dp', [(0, 1), (1, 0)])]
    convert_element_type x1 -> x0, other arithmetic: 0.69 us -> none  [shards(): both = (keep + other.astype(F32)).astype(BF16)]
    pallas_call x0 -> x1, Pallas kernels: none -> 0.68 us  [shards(): call(add_kernel, 'add', [(share + (channels,), BF16)], 'vv>v', [])]
  transfers between devices with their start and end apart: 6 -> 6, of which waited for: 1 -> 2; matrix products, arithmetic and copies ran while one was open for 2% -> 0% of each run, Pallas kernels for 30% -> 35%
where the time goes in v9:
time: 40.2 us; the launch traced here: 39.7 us
  starting transfers between devices  17.5 us (44%)
  Pallas kernels  16.3 us (41%)
  waiting for transfers between devices  4.56 us (11%)
  between operations  0.73 us (2%)
  other arithmetic  0.64 us (2%)
    ppermute x4, starting transfers between devices, swap(): results.append(lax.ppermute(rows, axis, pairs + [(j, i) for i, j in pairs]))  9.04 us
    all_to_all x1, starting transfers between devices, shards(): received = lax.all_to_all(both, 'tile', 0, 0, tiled=True)  8.43 us
    pallas_call x1, Pallas kernels, shards(): call(first_kernel, 'first', [((inner, columns, channels), BF16), ((2 * HA...  6.6 us
    pallas_call x1, Pallas kernels, shards(): call(last_kernel, 'last', [whole], 'svvvvvhvvv>h', [pltpu.VMEM((rows, col...  4.94 us
    all_to_all x1, waiting for transfers between devices, shards(): received = lax.all_to_all(both, 'tile', 0, 0, tiled=True)  3.17 us
    pallas_call x1, Pallas kernels, shards(): call(lambda *refs: taps_kernel(*refs, scale=scale, paired=paired), 'taps'...  1.67 us
    ppermute x1, waiting for transfers between devices, shards(): other = lax.ppermute(send, 'dp', [(0, 1), (1, 0)])  1.38 us
    pallas_call x1, Pallas kernels, shards(): call(rims_kernel, 'rims', [rim, rim, ((2 * HALO, channels, columns), BF16...  1.27 us
  transfers between devices with their start and end apart: 6, of which 2 were waited for; matrix products, arithmetic and copies ran while one was open for 0% of the time, Pallas kernels for 35%

profile of v9, /device:TPU:0, one launch (start us, length us, event | category | flops | bytes accessed | tf_op | source)
XLA Modules:
  0.0 39.7 jit_solution(16760307980842824939)
XLA Ops:
  0.6 1.1 %cut.1 = (bf16[2,384,128]{2,1,0:T(8,128)(2,1)S(1)}, bf16[2,384,128]{2,1,0:T(8,128)(2,1)S(1)}) custom-call(bf16[12,384,128]{2,1,0:T(8,128)(2,1)} %bitcast.7), custom_call_target="tpu_custom_call" | custom-call | tf_op jit(solution)/shard_map/cut/pallas_call | solution.py:442
  1.7 3.0 %collective-permute-start = (bf16[2,384,128]{2,1,0:T(8,128)(2,1)S(1)}, bf16[2,384,128]{2,1,0:T(8,128)(2,1)S(1)}, u32[]{:S(2)}, u32[]{:S(2)}) collective-permute-start(bf16[2,384,128]{2,1,0:T(8,128)(2,1)S(1)} %get-tuple-element.18), channel_id=1, source_target_pairs={{0,2},{4,6},{8,10},{12,14},{16,18},{20,22},{24,26},{28,30},{2,0},{... | collective-permute-start | bytes 589832 | tf_op jit(solution)/shard_map/ppermute | solution.py:396
  4.7 0.7 %collective-permute-start.1 = (bf16[2,384,128]{2,1,0:T(8,128)(2,1)S(1)}, bf16[2,384,128]{2,1,0:T(8,128)(2,1)S(1)}, u32[]{:S(2)}, u32[]{:S(2)}) collective-permute-start(bf16[2,384,128]{2,1,0:T(8,128)(2,1)S(1)} %get-tuple-element.19), channel_id=1, source_target_pairs={{2,4},{6,8},{10,12},{14,16},{18,20},{22,24},{26,28},{4,2},{8,6},{1... | collective-permute-start | bytes 589832 | tf_op jit(solution)/shard_map/ppermute | solution.py:396
  5.4 6.6 %first.1 = (bf16[8,384,128]{2,1,0:T(8,128)(2,1)S(1)}, f32[4,384,128]{2,1,0:T(8,128)S(1)}, bf16[12,128,384]{2,1,0:T(8,128)(2,1)S(1)}, f32[384,384]{1,0:T(8,128)S(...) custom-call(s32[1,16]{1,0:T(1,128)} %refs_0_.1, ...), custom_call_target="tpu_custom_call" | custom-call | flops 20000000000 | tf_op jit(solution)/shard_map/first/pallas_call | solution.py:451
  12.0 0.0 collective-permute-done.a_ref
  12.0 0.0 collective-permute-done.1.b_ref
  12.0 1.3 %rims.1 = (bf16[2,384,128]{2,1,0:T(8,128)(2,1)S(1)}, bf16[2,384,128]{2,1,0:T(8,128)(2,1)S(1)}, bf16[4,128,384]{2,1,0:T(8,128)(2,1)S(1)}) custom-call(s32[1,16]{1,0:T(1,128)} %refs_0_.1, bf16[2,384,128]{2,1,0:T(8,128)(2,1)S(1)} %collective-permute-done.a_ref, bf16[2,384,128]{2,1,0:T(8,128)(2,1)S(1)} %collective-permute-done.1.b_ref, ...), custom_call_target="tpu_custom_call" | custom-call | tf_op jit(solution)/shard_map/rims/pallas_call | solution.py:479
  13.3 4.7 %collective-permute-start.2 = (bf16[2,384,128]{2,1,0:T(8,128)(2,1)S(1)}, bf16[2,384,128]{2,1,0:T(8,128)(2,1)S(1)}, u32[]{:S(2)}, u32[]{:S(2)}) collective-permute-start(bf16[2,384,128]{2,1,0:T(8,128)(2,1)S(1)} %get-tuple-element.24.grad_a_ref.refs_1_), channel_id=1, source_target_pairs={{0,2},{4,6},{8,10},{12,14},{16,18},{20,22},{24,26},{28,30},{2,0},{... | collective-permute-start | bytes 589832 | tf_op jit(solution)/shard_map/ppermute | solution.py:396
  18.0 0.7 %collective-permute-start.3 = (bf16[2,384,128]{2,1,0:T(8,128)(2,1)S(1)}, bf16[2,384,128]{2,1,0:T(8,128)(2,1)S(1)}, u32[]{:S(2)}, u32[]{:S(2)}) collective-permute-start(bf16[2,384,128]{2,1,0:T(8,128)(2,1)S(1)} %get-tuple-element.25.grad_b_ref.refs_2_), channel_id=1, source_target_pairs={{2,4},{6,8},{10,12},{14,16},{18,20},{22,24},{26,28},{4,2},{8,6},{1... | collective-permute-start | bytes 589832 | tf_op jit(solution)/shard_map/ppermute | solution.py:396
  18.7 1.7 %taps.1 = (f32[16,36,128]{2,1,0:T(8,128)S(1)}, bf16[16,36,128]{2,1,0:T(8,128)(2,1)S(1)}) custom-call(s32[1,16]{1,0:T(1,128)} %refs_0_.1, bf16[2,384,128]{2,1,0:T(8,128)(2,1)S(1)} %get-tuple-element.24.grad_a_ref.refs_1_, bf16[2,384,128]{2,1,0:T(8,128)(2,1)S(1)} %get-tuple-element.25.grad_b_ref.refs_2_, bf16[12,128,384]{2,1,0:T(8,128)(2,1)S(1)} %get-tuple-element.29.refs_3_, ...), custom_call_target="tpu_custom_call" | custom-call | tf_op jit(solution)/shard_map/taps/pallas_call | solution.py:498
  20.4 0.1 collective-permute-start.4
  20.5 1.4 %collective-permute-done.4.other_ref = bf16[16,36,128]{2,1,0:T(8,128)(2,1)S(1)} collective-permute-done((bf16[16,36,128]{2,1,0:T(8,128)(2,1)S(1)}, bf16[16,36,128]{2,1,0:T(8,128)(2,1)S(1)}, u32[]{:S(2)}, u32[]{:S(2)}) %collective-permute-start.4) | collective-permute-done | bytes 147488 | tf_op jit(solution)/shard_map/ppermute | solution.py:514
  21.8 0.7 %add.1 = bf16[16,36,128]{2,1,0:T(8,128)(2,1)} custom-call(f32[16,36,128]{2,1,0:T(8,128)S(1)} %get-tuple-element.32.keep_ref, bf16[16,36,128]{2,1,0:T(8,128)(2,1)S(1)} %collective-permute-done.4.other_ref), custom_call_target="tpu_custom_call" | custom-call | tf_op jit(solution)/shard_map/add/pallas_call | solution.py:515
  22.5 8.4 %all-to-all-start = ((bf16[16,36,128]{2,1,0:T(8,128)(2,1)}), bf16[16,36,128]{2,1,0:T(8,128)(2,1)S(1)}, u32[]{:S(2)}, u32[]{:S(2)}) async-start(bf16[16,36,128]{2,1,0:T(8,128)(2,1)} %add.1), calls=%async_computation | async-start | bytes 327680 | tf_op jit(solution)/shard_map/all_to_all | solution.py:516
  31.0 0.0 collective-permute-done.2.from_a_ref
  31.0 0.0 collective-permute-done.3.from_b_ref
  31.0 4.9 %last.1 = bf16[12,384,128]{2,1,0:T(8,128)(2,1)} custom-call(s32[1,16]{1,0:T(1,128)} %refs_0_.1, bf16[2,384,128]{2,1,0:T(8,128)(2,1)S(1)} %collective-permute-done.2.from_a_ref, bf16[2,384,128]{2,1,0:T(8,128)(2,1)S(1)} %collective-permute-done.3.from_b_ref, bf16[2,384,128]{2,1,0:T(8,128)(2,1)S(1)} %get-tuple-element.24.grad_a_ref.refs_1_, ...), custom_call_target="tpu_custom_call" | custom-call | flops 20000000000 | tf_op jit(solution)/shard_map/last/pallas_call | solution.py:522
  35.9 3.2 %all-to-all-done = bf16[16,36,128]{2,1,0:T(8,128)(2,1)S(1)} async-done(((bf16[16,36,128]{2,1,0:T(8,128)(2,1)}), bf16[16,36,128]{2,1,0:T(8,128)(2,1)S(1)}, u32[]{:S(2)}, u32[]{:S(2)}) %all-to-all-start) | async-done | bytes 147488 | tf_op jit(solution)/shard_map/all_to_all | solution.py:516
  39.1 0.6 %convert_reduce_fusion = f32[36,128]{1,0:T(8,128)} fusion(bf16[16,36,128]{2,1,0:T(8,128)(2,1)S(1)} %all-to-all-done), kind=kLoop, calls=%fused_computation | loop fusion | flops 142848 | bytes 165888 | tf_op jit(solution)/shard_map/reduce_sum | solution.py:542
Async XLA Ops:
  1.7 10.3 %collective-permute-start = (bf16[2,384,128]{2,1,0:T(8,128)(2,1)S(1)}, bf16[2,384,128]{2,1,0:T(8,128)(2,1)S(1)}, u32[]{:S(2)}, u32[]{:S(2)}) collective-permute-start(bf16[2,384,128]{2,1,0:T(8,128)(2,1)S(1)} %get-tuple-element.18), channel_id=1, source_target_pairs={{0,2},{4,6},{8,10},{12,14},{16,18},{20,22},{24,26},{28,30},{2,0},{... | collective-permute-start | bytes 589832 | tf_op jit(solution)/shard_map/ppermute | solution.py:396
  4.7 7.3 %collective-permute-start.1 = (bf16[2,384,128]{2,1,0:T(8,128)(2,1)S(1)}, bf16[2,384,128]{2,1,0:T(8,128)(2,1)S(1)}, u32[]{:S(2)}, u32[]{:S(2)}) collective-permute-start(bf16[2,384,128]{2,1,0:T(8,128)(2,1)S(1)} %get-tuple-element.19), channel_id=1, source_target_pairs={{2,4},{6,8},{10,12},{14,16},{18,20},{22,24},{26,28},{4,2},{8,6},{1... | collective-permute-start | bytes 589832 | tf_op jit(solution)/shard_map/ppermute | solution.py:396
  13.3 17.6 %collective-permute-start.2 = (bf16[2,384,128]{2,1,0:T(8,128)(2,1)S(1)}, bf16[2,384,128]{2,1,0:T(8,128)(2,1)S(1)}, u32[]{:S(2)}, u32[]{:S(2)}) collective-permute-start(bf16[2,384,128]{2,1,0:T(8,128)(2,1)S(1)} %get-tuple-element.24.grad_a_ref.refs_1_), channel_id=1, source_target_pairs={{0,2},{4,6},{8,10},{12,14},{16,18},{20,22},{24,26},{28,30},{2,0},{... | collective-permute-start | bytes 589832 | tf_op jit(solution)/shard_map/ppermute | solution.py:396
  18.0 12.9 %collective-permute-start.3 = (bf16[2,384,128]{2,1,0:T(8,128)(2,1)S(1)}, bf16[2,384,128]{2,1,0:T(8,128)(2,1)S(1)}, u32[]{:S(2)}, u32[]{:S(2)}) collective-permute-start(bf16[2,384,128]{2,1,0:T(8,128)(2,1)S(1)} %get-tuple-element.25.grad_b_ref.refs_2_), channel_id=1, source_target_pairs={{2,4},{6,8},{10,12},{14,16},{18,20},{22,24},{26,28},{4,2},{8,6},{1... | collective-permute-start | bytes 589832 | tf_op jit(solution)/shard_map/ppermute | solution.py:396
  20.4 1.5 %collective-permute-start.4 = (bf16[16,36,128]{2,1,0:T(8,128)(2,1)S(1)}, bf16[16,36,128]{2,1,0:T(8,128)(2,1)S(1)}, u32[]{:S(2)}, u32[]{:S(2)}) collective-permute-start(bf16[16,36,128]{2,1,0:T(8,128)(2,1)S(1)} %get-tuple-element.33), channel_id=1, source_target_pairs={{0,1},{1,0},{2,3},{3,2},{4,5},{5,4},{6,7},{7,6},{8,9},{9,8},{10,11... | collective-permute-start | bytes 442376 | tf_op jit(solution)/shard_map/ppermute | solution.py:514
  22.5 16.6 %all-to-all-start = ((bf16[16,36,128]{2,1,0:T(8,128)(2,1)}), bf16[16,36,128]{2,1,0:T(8,128)(2,1)S(1)}, u32[]{:S(2)}, u32[]{:S(2)}) async-start(bf16[16,36,128]{2,1,0:T(8,128)(2,1)} %add.1), calls=%async_computation | async-start | bytes 327680 | tf_op jit(solution)/shard_map/all_to_all | solution.py:516

commit v10 on v6

--- a/solution.py
+++ b/solution.py
@@ -215,62 +215,47 @@
 
 
 def rims_kernel(
-    rates_ref, a_ref, b_ref, pre_ref, cot_ref, mask_ref, near_ref,
-    grad_a_ref, grad_b_ref, xt_ref,
-    pad, xcat, halo, grads,
+    rates_ref, a_ref, b_ref, pre_ref, cot_ref, mask_ref, near_ref, xt_own_ref, total_ref,
+    grad_a_ref, grad_b_ref, keep_ref, send_ref,
+    pad, xcat, halo, grads, xt_halo, gedge, flat, *, scale, paired,
 ):
     _, columns, channels = a_ref.shape
-    clear_ends(pad, 2 * HALO, columns)
+    rows = xt_own_ref.shape[0]
+    clear_ends(pad, 4 * HALO, columns)
     by_side(a_ref, b_ref, halo)
 
+    def flipped(row):
+        if row < 0:
+            return xt_halo[row + HALO]
+        return xt_own_ref[row] if row < rows else xt_halo[row - rows + HALO]
+
     def body(rate):
+        halves = []
         for side in range(2):
             used = range(HALO - rate, HALO) if side == 0 else range(rate)
             for place, k in enumerate(used):
                 value = halo[side, k] * mask_ref[2 * side]
                 part = pl.ds(place * columns, columns)
                 spread(value, pad, side * HALO + k, xcat.at[side, part], rate)
-                xt_ref[side * HALO + k] = value.T
-            sums = jnp.dot(
-                xcat[side, : rate * columns], near_ref[side], preferred_element_type=F32
+                xt_halo[side * HALO + k] = value.T
+            halves.append(
+                jnp.dot(xcat[side, : rate * columns], near_ref[side], preferred_element_type=F32)
             )
+        total = total_ref[...]
+        for side, sums in enumerate(halves):
+            edges = []
             for k in range(HALO):
-                half_pre = pre_ref[side * HALO + k]
+                slot = side * HALO + k
+                half_pre = pre_ref[slot]
                 place = k if side == 0 else k - (HALO - rate)
                 if 0 <= place < rate:
                     half_pre += 0.5 * sums[place * columns : (place + 1) * columns]
-                grad = silu_grad(cot_ref[side * HALO + k].astype(F32), half_pre)
+                grad = silu_grad(cot_ref[slot].astype(F32), half_pre)
                 grads[side, k] = grad.astype(BF16)
-
-    by_rate(rates_ref[0, lax.axis_index("tile")], body)
-    odd = lax.axis_index("tile") % 2
-    grad_a_ref[...] = grads[1 - odd]
-    grad_b_ref[...] = grads[odd]
-
-
-def taps_kernel(
-    rates_ref, grad_a_ref, grad_b_ref, xt_own_ref, xt_halo_ref, total_ref,
-    keep_ref, send_ref,
-    pad, gedge_ref, flat, sides, *, scale, paired,
-):
-    _, columns, channels = grad_a_ref.shape
-    by_side(grad_a_ref, grad_b_ref, sides)
-    rows = xt_own_ref.shape[0]
-    clear_ends(pad, 2 * HALO, columns)
-
-    def flipped(row):
-        if row < 0:
-            return xt_halo_ref[row + HALO]
-        return xt_own_ref[row] if row < rows else xt_halo_ref[row - rows + HALO]
-
-    def body(rate):
-        edges = []
-        for side in range(2):
-            for k in range(HALO):
-                slot = side * HALO + k
-                spread(sides[side, k], pad, slot, gedge_ref.at[slot], -rate)
-                edges.append((k + side * (rows - HALO), gedge_ref.at[slot]))
-        total = (total_ref[...] + tap_sums(edges, flipped, rate)) * scale
+                spread(grad, pad, 2 * HALO + slot, gedge.at[slot], -rate)
+                edges.append((k + side * (rows - HALO), gedge.at[slot]))
+            total = total + tap_sums(edges, flipped, rate)
+        total = total * scale
         for a in range(3):
             for b in range(3):
                 start = (a * 3 + b) * channels
@@ -279,6 +264,9 @@
                 ]
 
     by_rate(rates_ref[0, lax.axis_index("tile")], body)
+    odd = lax.axis_index("tile") % 2
+    grad_a_ref[...] = grads[1 - odd]
+    grad_b_ref[...] = grads[odd]
     if not paired:
         keep_ref[0] = flat[...]
         return
@@ -472,40 +460,28 @@
         flops=BUSY,
     )(dilations, lists, in_hbm(x), cot, weight, bias)
 
-    grad_a, grad_b, xt_halo = call(
-        rims_kernel,
-        "rims",
-        [
-            rim,
-            rim,
-            ((2 * HALO, channels, columns), BF16),
-        ],
-        "svvvvvv>vvv",
-        [pads(2 * HALO), pltpu.VMEM((2, HALO * columns, wide_row), BF16), sides, sides],
-    )(dilations, x_a, x_b, pre, cot_edge, mask, near)
-
-    from_a, from_b = swap(grad_a, grad_b, "tile")
-
     tap_rows = 9 * channels
     cores = lax.axis_size("dp")
     paired = cores == 2 and tap_rows % devices == 0
     share = (devices // 2, tap_rows // devices) if paired else (1, tap_rows)
     scale = 1.0 / math.sqrt(devices * lists.shape[1] * TILE * TILE)
-    keep, send = call(
-        lambda *refs: taps_kernel(*refs, scale=scale, paired=paired),
-        "taps",
+    grad_a, grad_b, keep, send = call(
+        lambda *refs: rims_kernel(*refs, scale=scale, paired=paired),
+        "rims",
+        [rim, rim, (share + (channels,), F32), (share + (channels,), BF16)],
+        "svvvvvvvv>vvvv",
         [
-            (share + (channels,), F32),
-            (share + (channels,), BF16),
-        ],
-        "svvvvv>vv",
-        [
-            pads(2 * HALO),
+            pads(4 * HALO),
+            pltpu.VMEM((2, HALO * columns, wide_row), BF16),
+            sides,
+            sides,
+            pltpu.VMEM((2 * HALO, channels, columns), BF16),
             pltpu.VMEM((2 * HALO, columns, wide_row), BF16),
             pltpu.VMEM((tap_rows, channels), F32),
-            sides,
         ],
-    )(dilations, grad_a, grad_b, xt, xt_halo, total)
+    )(dilations, x_a, x_b, pre, cot_edge, mask, near, xt, total)
+
+    from_a, from_b = swap(grad_a, grad_b, "tile")
     if paired:
         other = lax.ppermute(send, "dp", [(0, 1), (1, 0)])
         both = (keep + other.astype(F32)).astype(BF16)

time: 38.6 us -> 37.6 us (0.974)
  Pallas kernels: 15.6 us -> 14.6 us
    pallas_call x2 -> x1, Pallas kernels: 2.95 us -> 1.97 us  [shards(): call(lambda *refs: rims_kernel(*refs, scale=scale, paired=paired), 'rims'...]
  transfers between devices with their start and end apart: 6 -> 6, of which waited for: 1 -> 1; matrix products, arithmetic and copies ran while one was open for 2% -> 2% of each run, Pallas kernels for 30% -> 31%
where the time goes in v10:
time: 37.6 us; the launch traced here: 37.4 us
  starting transfers between devices  17.7 us (47%)
  Pallas kernels  14.6 us (39%)
  waiting for transfers between devices  2.98 us (8%)
  other arithmetic  1.33 us (4%)
  between operations  0.73 us (2%)
    ppermute x4, starting transfers between devices, swap(): results.append(lax.ppermute(rows, axis, pairs + [(j, i) for i, j in pairs]))  8.89 us
    all_to_all x1, starting transfers between devices, shards(): received = lax.all_to_all(both, 'tile', 0, 0, tiled=True)  8.77 us
    pallas_call x1, Pallas kernels, shards(): call(first_kernel, 'first', [((inner, columns, channels), BF16), ((2 * HA...  6.6 us
    pallas_call x1, Pallas kernels, shards(): call(last_kernel, 'last', [whole], 'svvvvvhvvv>h', [pltpu.VMEM((rows, col...  4.94 us
    all_to_all x1, waiting for transfers between devices, shards(): received = lax.all_to_all(both, 'tile', 0, 0, tiled=True)  2.96 us
    pallas_call x1, Pallas kernels, shards(): call(lambda *refs: rims_kernel(*refs, scale=scale, paired=paired), 'rims'...  1.97 us
    pallas_call x1, Pallas kernels, shards(): call(cut_kernel, 'cut', [rim, rim], 'h>vv', [pltpu.SemaphoreType.DMA((2,...  1.09 us
  transfers between devices with their start and end apart: 6, of which 1 were waited for; matrix products, arithmetic and copies ran while one was open for 2% of the time, Pallas kernels for 31%

profile of v10, /device:TPU:0, one launch (start us, length us, event | category | flops | bytes accessed | tf_op | source)
XLA Modules:
  0.0 37.4 jit_solution(14151229884357559363)
XLA Ops:
  0.6 1.1 %cut.1 = (bf16[2,384,128]{2,1,0:T(8,128)(2,1)S(1)}, bf16[2,384,128]{2,1,0:T(8,128)(2,1)S(1)}) custom-call(bf16[12,384,128]{2,1,0:T(8,128)(2,1)} %bitcast.7), custom_call_target="tpu_custom_call" | custom-call | tf_op jit(solution)/shard_map/cut/pallas_call | solution.py:426
  1.7 3.0 %collective-permute-start = (bf16[2,384,128]{2,1,0:T(8,128)(2,1)S(1)}, bf16[2,384,128]{2,1,0:T(8,128)(2,1)S(1)}, u32[]{:S(2)}, u32[]{:S(2)}) collective-permute-start(bf16[2,384,128]{2,1,0:T(8,128)(2,1)S(1)} %get-tuple-element.17), channel_id=1, source_target_pairs={{0,2},{4,6},{8,10},{12,14},{16,18},{20,22},{24,26},{28,30},{2,0},{... | collective-permute-start | bytes 589832 | tf_op jit(solution)/shard_map/ppermute | solution.py:380
  4.7 0.7 %collective-permute-start.1 = (bf16[2,384,128]{2,1,0:T(8,128)(2,1)S(1)}, bf16[2,384,128]{2,1,0:T(8,128)(2,1)S(1)}, u32[]{:S(2)}, u32[]{:S(2)}) collective-permute-start(bf16[2,384,128]{2,1,0:T(8,128)(2,1)S(1)} %get-tuple-element.18), channel_id=1, source_target_pairs={{2,4},{6,8},{10,12},{14,16},{18,20},{22,24},{26,28},{4,2},{8,6},{1... | collective-permute-start | bytes 589832 | tf_op jit(solution)/shard_map/ppermute | solution.py:380
  5.4 6.6 %first.1 = (bf16[8,384,128]{2,1,0:T(8,128)(2,1)S(1)}, f32[4,384,128]{2,1,0:T(8,128)S(1)}, bf16[12,128,384]{2,1,0:T(8,128)(2,1)S(1)}, f32[384,384]{1,0:T(8,128)S(...) custom-call(s32[1,16]{1,0:T(1,128)} %rates_ref.3, ...), custom_call_target="tpu_custom_call" | custom-call | flops 20000000000 | tf_op jit(solution)/shard_map/first/pallas_call | solution.py:435
  12.0 0.0 collective-permute-done.refs_1_
  12.0 0.0 collective-permute-done.1.refs_2_
  12.0 2.0 %rims.1 = (bf16[2,384,128]{2,1,0:T(8,128)(2,1)S(1)}, bf16[2,384,128]{2,1,0:T(8,128)(2,1)S(1)}, f32[16,36,128]{2,1,0:T(8,128)S(1)}, bf16[16,36,128]{2,1,0:T(8,128)(2,1)S(1)}) custom-call(s32[1,16]{1,0:T(1,128)} %rates_ref.3, bf16[2,384,128]{2,1,0:T(8,128)(2,1)S(1)} %collective-permute-done.refs_1_, bf16[2,384,128]{2,1,0:T(8,128)(2,1)S(1)} %collective-permute-done.1.refs_2_, ...), custom_call_target="tpu_custom_call" | custom-call | tf_op jit(solution)/shard_map/rims/pallas_call | solution.py:468
  14.0 0.1 collective-permute-start.4
  14.1 4.6 %collective-permute-start.2 = (bf16[2,384,128]{2,1,0:T(8,128)(2,1)S(1)}, bf16[2,384,128]{2,1,0:T(8,128)(2,1)S(1)}, u32[]{:S(2)}, u32[]{:S(2)}) collective-permute-start(bf16[2,384,128]{2,1,0:T(8,128)(2,1)S(1)} %get-tuple-element.25.grad_a_ref), channel_id=1, source_target_pairs={{0,2},{4,6},{8,10},{12,14},{16,18},{20,22},{24,26},{28,30},{2,0},{... | collective-permute-start | bytes 589832 | tf_op jit(solution)/shard_map/ppermute | solution.py:380
  18.7 0.7 %collective-permute-start.3 = (bf16[2,384,128]{2,1,0:T(8,128)(2,1)S(1)}, bf16[2,384,128]{2,1,0:T(8,128)(2,1)S(1)}, u32[]{:S(2)}, u32[]{:S(2)}) collective-permute-start(bf16[2,384,128]{2,1,0:T(8,128)(2,1)S(1)} %get-tuple-element.26.grad_b_ref), channel_id=1, source_target_pairs={{2,4},{6,8},{10,12},{14,16},{18,20},{22,24},{26,28},{4,2},{8,6},{1... | collective-permute-start | bytes 589832 | tf_op jit(solution)/shard_map/ppermute | solution.py:380
  19.3 0.0 collective-permute-done.4
  19.3 0.7 %add_convert_fusion = bf16[16,36,128]{2,1,0:T(8,128)(2,1)} fusion(f32[16,36,128]{2,1,0:T(8,128)S(1)} %get-tuple-element.30, bf16[16,36,128]{2,1,0:T(8,128)(2,1)S(1)} %collective-permute-done.4), kind=kLoop, calls=%fused_computation.1 | loop fusion | flops 221184 | bytes 589824 | tf_op jit(solution)/shard_map/convert_element_type | solution.py:487
  20.0 8.8 %all-to-all-start = ((bf16[16,36,128]{2,1,0:T(8,128)(2,1)}), bf16[16,36,128]{2,1,0:T(8,128)(2,1)S(1)}, u32[]{:S(2)}, u32[]{:S(2)}) async-start(bf16[16,36,128]{2,1,0:T(8,128)(2,1)} %add_convert_fusion), calls=%async_computation | async-start | bytes 327680 | tf_op jit(solution)/shard_map/all_to_all | solution.py:488
  28.8 0.0 collective-permute-done.2.from_a_ref
  28.8 0.0 collective-permute-done.3.from_b_ref
  28.8 4.9 %last.1 = bf16[12,384,128]{2,1,0:T(8,128)(2,1)} custom-call(s32[1,16]{1,0:T(1,128)} %rates_ref.3, bf16[2,384,128]{2,1,0:T(8,128)(2,1)S(1)} %collective-permute-done.2.from_a_ref, bf16[2,384,128]{2,1,0:T(8,128)(2,1)S(1)} %collective-permute-done.3.from_b_ref, bf16[2,384,128]{2,1,0:T(8,128)(2,1)S(1)} %get-tuple-element.25.grad_a_ref, ...), custom_call_target="tpu_custom_call" | custom-call | flops 20000000000 | tf_op jit(solution)/shard_map/last/pallas_call | solution.py:494
  33.8 3.0 %all-to-all-done = bf16[16,36,128]{2,1,0:T(8,128)(2,1)S(1)} async-done(((bf16[16,36,128]{2,1,0:T(8,128)(2,1)}), bf16[16,36,128]{2,1,0:T(8,128)(2,1)S(1)}, u32[]{:S(2)}, u32[]{:S(2)}) %all-to-all-start) | async-done | bytes 147488 | tf_op jit(solution)/shard_map/all_to_all | solution.py:488
  36.7 0.6 %convert_reduce_fusion = f32[36,128]{1,0:T(8,128)} fusion(bf16[16,36,128]{2,1,0:T(8,128)(2,1)S(1)} %all-to-all-done), kind=kLoop, calls=%fused_computation | loop fusion | flops 142848 | bytes 165888 | tf_op jit(solution)/shard_map/reduce_sum | solution.py:514
Async XLA Ops:
  1.7 10.3 %collective-permute-start = (bf16[2,384,128]{2,1,0:T(8,128)(2,1)S(1)}, bf16[2,384,128]{2,1,0:T(8,128)(2,1)S(1)}, u32[]{:S(2)}, u32[]{:S(2)}) collective-permute-start(bf16[2,384,128]{2,1,0:T(8,128)(2,1)S(1)} %get-tuple-element.17), channel_id=1, source_target_pairs={{0,2},{4,6},{8,10},{12,14},{16,18},{20,22},{24,26},{28,30},{2,0},{... | collective-permute-start | bytes 589832 | tf_op jit(solution)/shard_map/ppermute | solution.py:380
  4.7 7.3 %collective-permute-start.1 = (bf16[2,384,128]{2,1,0:T(8,128)(2,1)S(1)}, bf16[2,384,128]{2,1,0:T(8,128)(2,1)S(1)}, u32[]{:S(2)}, u32[]{:S(2)}) collective-permute-start(bf16[2,384,128]{2,1,0:T(8,128)(2,1)S(1)} %get-tuple-element.18), channel_id=1, source_target_pairs={{2,4},{6,8},{10,12},{14,16},{18,20},{22,24},{26,28},{4,2},{8,6},{1... | collective-permute-start | bytes 589832 | tf_op jit(solution)/shard_map/ppermute | solution.py:380
  14.0 5.3 %collective-permute-start.4 = (bf16[16,36,128]{2,1,0:T(8,128)(2,1)S(1)}, bf16[16,36,128]{2,1,0:T(8,128)(2,1)S(1)}, u32[]{:S(2)}, u32[]{:S(2)}) collective-permute-start(bf16[16,36,128]{2,1,0:T(8,128)(2,1)S(1)} %get-tuple-element.31), channel_id=1, source_target_pairs={{0,1},{1,0},{2,3},{3,2},{4,5},{5,4},{6,7},{7,6},{8,9},{9,8},{10,11... | collective-permute-start | bytes 442376 | tf_op jit(solution)/shard_map/ppermute | solution.py:486
  14.1 14.7 %collective-permute-start.2 = (bf16[2,384,128]{2,1,0:T(8,128)(2,1)S(1)}, bf16[2,384,128]{2,1,0:T(8,128)(2,1)S(1)}, u32[]{:S(2)}, u32[]{:S(2)}) collective-permute-start(bf16[2,384,128]{2,1,0:T(8,128)(2,1)S(1)} %get-tuple-element.25.grad_a_ref), channel_id=1, source_target_pairs={{0,2},{4,6},{8,10},{12,14},{16,18},{20,22},{24,26},{28,30},{2,0},{... | collective-permute-start | bytes 589832 | tf_op jit(solution)/shard_map/ppermute | solution.py:380
  18.7 10.2 %collective-permute-start.3 = (bf16[2,384,128]{2,1,0:T(8,128)(2,1)S(1)}, bf16[2,384,128]{2,1,0:T(8,128)(2,1)S(1)}, u32[]{:S(2)}, u32[]{:S(2)}) collective-permute-start(bf16[2,384,128]{2,1,0:T(8,128)(2,1)S(1)} %get-tuple-element.26.grad_b_ref), channel_id=1, source_target_pairs={{2,4},{6,8},{10,12},{14,16},{18,20},{22,24},{26,28},{4,2},{8,6},{1... | collective-permute-start | bytes 589832 | tf_op jit(solution)/shard_map/ppermute | solution.py:380
  20.0 16.7 %all-to-all-start = ((bf16[16,36,128]{2,1,0:T(8,128)(2,1)}), bf16[16,36,128]{2,1,0:T(8,128)(2,1)S(1)}, u32[]{:S(2)}, u32[]{:S(2)}) async-start(bf16[16,36,128]{2,1,0:T(8,128)(2,1)} %add_convert_fusion), calls=%async_computation | async-start | bytes 327680 | tf_op jit(solution)/shard_map/all_to_all | solution.py:488

commit v11 on v10

--- a/solution.py
+++ b/solution.py
@@ -119,9 +119,9 @@
 
 
 def first_kernel(
-    rates_ref, lists_ref, x_hbm, cot_hbm, w_hbm, bias_ref,
-    grad_ref, pre_ref, xt_ref, total_ref, mask_ref, cot_ref, back_ref, near_ref, far_ref,
-    xbuf, cbuf, wbuf, pad, xcat, gcat_ref, wide, sems,
+    rates_hbm, lists_hbm, x_hbm, cot_hbm, w_hbm, bias_hbm,
+    near_rates_ref, grad_ref, pre_ref, xt_ref, total_ref, mask_ref, cot_ref, back_ref, near_ref, far_ref,
+    rates_ref, lists_ref, bias_ref, xbuf, cbuf, wbuf, pad, xcat, gcat_ref, wide, sems,
 ):
     rows, columns, channels = x_hbm.shape
     tiles_row = columns // TILE
@@ -134,8 +134,20 @@
             loads.append(
                 pltpu.make_async_copy(source.at[part], target.at[part], sems.at[base + k])
             )
-    for load in loads:
+    small = [
+        pltpu.make_async_copy(source, target, sems.at[9 + k])
+        for k, (source, target) in enumerate(
+            ((lists_hbm, lists_ref), (rates_hbm, rates_ref), (bias_hbm, bias_ref))
+        )
+    ]
+    for load in small + loads:
         load.start()
+    for load in small:
+        load.wait()
+    last = rates_ref.shape[1] - 1
+    for k in range(3):
+        row = jnp.clip(mine + k - 1, 0, last)
+        near_rates_ref[k] = jnp.full(near_rates_ref.shape[1:], rates_ref[0, row], jnp.int32)
     for k, value in enumerate(cell_masks(lists_ref, mine, tiles_row, columns)):
         mask_ref[k] = value
     clear_ends(pad, rows, columns)
@@ -263,7 +275,7 @@
                     a * channels : (a + 1) * channels, b * channels : (b + 1) * channels
                 ]
 
-    by_rate(rates_ref[0, lax.axis_index("tile")], body)
+    by_rate(rates_ref[1, 0, 0], body)
     odd = lax.axis_index("tile") % 2
     grad_a_ref[...] = grads[1 - odd]
     grad_b_ref[...] = grads[odd]
@@ -285,8 +297,6 @@
 ):
     rows, columns, channels = cot_hbm.shape
     inner = rows - 2 * HALO
-    mine = lax.axis_index("tile")
-    last = rates_ref.shape[1] - 1
     around = 2 * HALO
     chunks = rows // around
     cots, stores = [], []
@@ -305,7 +315,7 @@
     by_side(grad_a_ref, grad_b_ref, ours)
 
     def neighbour(side):
-        rate = rates_ref[0, jnp.minimum(mine + 1, last) if side else jnp.maximum(mine - 1, 0)]
+        rate = rates_ref[2 * side, 0, 0]
         for k in range(HALO):
             part = pl.ds(k * columns, columns)
             spread(theirs[side, k], pad, rows + side * HALO + k, spare.at[side, part], -rate)
@@ -351,7 +361,7 @@
                     obuf[row] = value.astype(BF16) * mask_ref[1]
             stores[chunk].start()
 
-    by_rate(rates_ref[0, mine], body)
+    by_rate(rates_ref[1, 0, 0], body)
     for store in stores:
         store.wait()
 
@@ -432,10 +442,11 @@
     )(in_hbm(x))
     x_a, x_b = swap(rows_a, rows_b, "tile")
 
-    grad, pre, xt, total, mask, cot_edge, back, near, far = call(
+    rates, grad, pre, xt, total, mask, cot_edge, back, near, far = call(
         first_kernel,
         "first",
         [
+            ((3, 8, LANES), jnp.int32),
             ((inner, columns, channels), BF16),
             ((2 * HALO, columns, channels), F32),
             ((rows, channels, columns), BF16),
@@ -446,8 +457,11 @@
             ((2, wide_row, channels), BF16),
             ((2, wide_row, channels), BF16),
         ],
-        "svhhhv>vvvvvvvvv",
+        "hhhhhh>vvvvvvvvvv",
         [
+            pltpu.SMEM(dilations.shape, jnp.int32),
+            pltpu.VMEM(lists.shape, jnp.int32),
+            pltpu.VMEM(bias.shape, F32),
             pltpu.VMEM((rows, columns, channels), BF16),
             pltpu.VMEM((rows, columns, channels), BF16),
             pltpu.VMEM((9, channels, channels), BF16),
@@ -455,7 +469,7 @@
             pltpu.VMEM((rows, columns, wide_row), BF16),
             pltpu.VMEM((inner, columns, wide_row), BF16),
             pltpu.VMEM((4 * wide_row, 2 * channels), BF16),
-            pltpu.SemaphoreType.DMA((9,)),
+            pltpu.SemaphoreType.DMA((12,)),
         ],
         flops=BUSY,
     )(dilations, lists, in_hbm(x), cot, weight, bias)
@@ -469,7 +483,7 @@
         lambda *refs: rims_kernel(*refs, scale=scale, paired=paired),
         "rims",
         [rim, rim, (share + (channels,), F32), (share + (channels,), BF16)],
-        "svvvvvvvv>vvvv",
+        "vvvvvvvvv>vvvv",
         [
             pads(4 * HALO),
             pltpu.VMEM((2, HALO * columns, wide_row), BF16),
@@ -479,7 +493,7 @@
             pltpu.VMEM((2 * HALO, columns, wide_row), BF16),
             pltpu.VMEM((tap_rows, channels), F32),
         ],
-    )(dilations, x_a, x_b, pre, cot_edge, mask, near, xt, total)
+    )(rates, x_a, x_b, pre, cot_edge, mask, near, xt, total)
 
     from_a, from_b = swap(grad_a, grad_b, "tile")
     if paired:
@@ -495,7 +509,7 @@
         last_kernel,
         "last",
         [whole],
-        "svvvvvhvvv>h",
+        "vvvvvvhvvv>h",
         [
             pltpu.VMEM((rows, columns, channels), BF16),
             pltpu.VMEM((rows, columns, channels), BF16),
@@ -508,7 +522,7 @@
         ],
         flops=BUSY,
     )(
-        dilations, from_a, from_b, grad_a, grad_b,
+        rates, from_a, from_b, grad_a, grad_b,
         grad, cot, mask, back, far,
     )
     summed = jnp.sum(received.astype(F32), axis=0)

time: 37.6 us -> 37 us (0.984)
  Pallas kernels: 14.6 us -> 13.2 us
  waiting for transfers between devices: 2.98 us -> 3.6 us
    pallas_call x2, Pallas kernels: 11.5 us -> 10.5 us  [the longest x1 6.22 us: shards(): call(first_kernel, 'first', [((3, 8, LANES), jnp.int32), ((inner, columns...]
    all_to_all x1, waiting for transfers between devices: 2.96 us -> 3.59 us  [shards(): received = lax.all_to_all(both, 'tile', 0, 0, tiled=True)]
    pallas_call x1, Pallas kernels: 1.97 us -> 1.57 us  [shards(): call(lambda *refs: rims_kernel(*refs, scale=scale, paired=paired), 'rims'...]
    all_to_all x1, starting transfers between devices: 8.77 us -> 8.38 us  [shards(): received = lax.all_to_all(both, 'tile', 0, 0, tiled=True)]
  transfers between devices with their start and end apart: 6 -> 6, of which waited for: 1 -> 1; matrix products, arithmetic and copies ran while one was open for 2% -> 2% of each run, Pallas kernels for 31% -> 29%
where the time goes in v11:
time: 37 us; the launch traced here: 36.6 us
  starting transfers between devices  17.7 us (48%)
  Pallas kernels  13.2 us (36%)
  waiting for transfers between devices  3.6 us (10%)
  other arithmetic  1.33 us (4%)
  between operations  0.73 us (2%)
    ppermute x4, starting transfers between devices, swap(): results.append(lax.ppermute(rows, axis, pairs + [(j, i) for i, j in pairs]))  9.27 us
    all_to_all x1, starting transfers between devices, shards(): received = lax.all_to_all(both, 'tile', 0, 0, tiled=True)  8.38 us
    pallas_call x1, Pallas kernels, shards(): call(first_kernel, 'first', [((3, 8, LANES), jnp.int32), ((inner, columns...  6.22 us
    pallas_call x1, Pallas kernels, shards(): call(last_kernel, 'last', [whole], 'vvvvvvhvvv>h', [pltpu.VMEM((rows, col...  4.32 us
    all_to_all x1, waiting for transfers between devices, shards(): received = lax.all_to_all(both, 'tile', 0, 0, tiled=True)  3.59 us
    pallas_call x1, Pallas kernels, shards(): call(lambda *refs: rims_kernel(*refs, scale=scale, paired=paired), 'rims'...  1.57 us
    pallas_call x1, Pallas kernels, shards(): call(cut_kernel, 'cut', [rim, rim], 'h>vv', [pltpu.SemaphoreType.DMA((2,...  1.09 us
  transfers between devices with their start and end apart: 6, of which 1 were waited for; matrix products, arithmetic and copies ran while one was open for 2% of the time, Pallas kernels for 29%

profile of v11, /device:TPU:0, one launch (start us, length us, event | category | flops | bytes accessed | tf_op | source)
XLA Modules:
  0.0 36.6 jit_solution(16398553165617805331)
XLA Ops:
  0.6 1.1 %cut.1 = (bf16[2,384,128]{2,1,0:T(8,128)(2,1)S(1)}, bf16[2,384,128]{2,1,0:T(8,128)(2,1)S(1)}) custom-call(bf16[12,384,128]{2,1,0:T(8,128)(2,1)} %bitcast.7), custom_call_target="tpu_custom_call" | custom-call | tf_op jit(solution)/shard_map/cut/pallas_call | solution.py:436
  1.7 3.0 %collective-permute-start = (bf16[2,384,128]{2,1,0:T(8,128)(2,1)S(1)}, bf16[2,384,128]{2,1,0:T(8,128)(2,1)S(1)}, u32[]{:S(2)}, u32[]{:S(2)}) collective-permute-start(bf16[2,384,128]{2,1,0:T(8,128)(2,1)S(1)} %get-tuple-element.19), channel_id=1, source_target_pairs={{0,2},{4,6},{8,10},{12,14},{16,18},{20,22},{24,26},{28,30},{2,0},{... | collective-permute-start | bytes 589832 | tf_op jit(solution)/shard_map/ppermute | solution.py:390
  4.7 0.7 %collective-permute-start.1 = (bf16[2,384,128]{2,1,0:T(8,128)(2,1)S(1)}, bf16[2,384,128]{2,1,0:T(8,128)(2,1)S(1)}, u32[]{:S(2)}, u32[]{:S(2)}) collective-permute-start(bf16[2,384,128]{2,1,0:T(8,128)(2,1)S(1)} %get-tuple-element.20), channel_id=1, source_target_pairs={{2,4},{6,8},{10,12},{14,16},{18,20},{22,24},{26,28},{4,2},{8,6},{1... | collective-permute-start | bytes 589832 | tf_op jit(solution)/shard_map/ppermute | solution.py:390
  5.4 6.2 %first.1 = (s32[3,8,128]{2,1,0:T(8,128)S(1)}, bf16[8,384,128]{2,1,0:T(8,128)(2,1)S(1)}, f32[4,384,128]{2,1,0:T(8,128)S(1)}, bf16[12,128,384]{2,1,0:T(8,128)(2,1)...) custom-call(s32[1,16]{1,0:T(1,128)} %rates_hbm.1, ...), custom_call_target="tpu_custom_call" | custom-call | flops 20000000000 | tf_op jit(solution)/shard_map/first/pallas_call | solution.py:445
  11.6 0.0 collective-permute-done.refs_1_
  11.6 0.0 collective-permute-done.1.refs_2_
  11.6 1.6 %rims.1 = (bf16[2,384,128]{2,1,0:T(8,128)(2,1)S(1)}, bf16[2,384,128]{2,1,0:T(8,128)(2,1)S(1)}, f32[16,36,128]{2,1,0:T(8,128)S(1)}, bf16[16,36,128]{2,1,0:T(8,128)(2,1)S(1)}) custom-call(s32[3,8,128]{2,1,0:T(8,128)S(1)} %get-tuple-element.18.refs_0_.rates_ref, bf16[2,384,128]{2,1,0:T(8,128)(2,1)S(1)} %collective-permute-done.refs_1_, ...), custom_call_target="tpu_custom_call" | custom-call | tf_op jit(solution)/shard_map/rims/pallas_call | solution.py:482
  13.2 0.1 collective-permute-start.4
  13.3 4.9 %collective-permute-start.2 = (bf16[2,384,128]{2,1,0:T(8,128)(2,1)S(1)}, bf16[2,384,128]{2,1,0:T(8,128)(2,1)S(1)}, u32[]{:S(2)}, u32[]{:S(2)}) collective-permute-start(bf16[2,384,128]{2,1,0:T(8,128)(2,1)S(1)} %get-tuple-element.27.grad_a_ref), channel_id=1, source_target_pairs={{0,2},{4,6},{8,10},{12,14},{16,18},{20,22},{24,26},{28,30},{2,0},{... | collective-permute-start | bytes 589832 | tf_op jit(solution)/shard_map/ppermute | solution.py:390
  18.2 0.7 %collective-permute-start.3 = (bf16[2,384,128]{2,1,0:T(8,128)(2,1)S(1)}, bf16[2,384,128]{2,1,0:T(8,128)(2,1)S(1)}, u32[]{:S(2)}, u32[]{:S(2)}) collective-permute-start(bf16[2,384,128]{2,1,0:T(8,128)(2,1)S(1)} %get-tuple-element.28.grad_b_ref), channel_id=1, source_target_pairs={{2,4},{6,8},{10,12},{14,16},{18,20},{22,24},{26,28},{4,2},{8,6},{1... | collective-permute-start | bytes 589832 | tf_op jit(solution)/shard_map/ppermute | solution.py:390
  18.9 0.0 collective-permute-done.4
  18.9 0.7 %add_convert_fusion = bf16[16,36,128]{2,1,0:T(8,128)(2,1)} fusion(f32[16,36,128]{2,1,0:T(8,128)S(1)} %get-tuple-element.32, bf16[16,36,128]{2,1,0:T(8,128)(2,1)S(1)} %collective-permute-done.4), kind=kLoop, calls=%fused_computation.1 | loop fusion | flops 221184 | bytes 589824 | tf_op jit(solution)/shard_map/convert_element_type | solution.py:501
  19.6 8.4 %all-to-all-start = ((bf16[16,36,128]{2,1,0:T(8,128)(2,1)}), bf16[16,36,128]{2,1,0:T(8,128)(2,1)S(1)}, u32[]{:S(2)}, u32[]{:S(2)}) async-start(bf16[16,36,128]{2,1,0:T(8,128)(2,1)} %add_convert_fusion), calls=%async_computation | async-start | bytes 327680 | tf_op jit(solution)/shard_map/all_to_all | solution.py:502
  28.0 0.0 collective-permute-done.2.from_a_ref
  28.0 0.0 collective-permute-done.3.from_b_ref
  28.0 4.3 %last.1 = bf16[12,384,128]{2,1,0:T(8,128)(2,1)} custom-call(s32[3,8,128]{2,1,0:T(8,128)S(1)} %get-tuple-element.18.refs_0_.rates_ref, bf16[2,384,128]{2,1,0:T(8,128)(2,1)S(1)} %collective-permute-done.2.from_a_ref, bf16[2,384,128]{2,1,0:T(8,128)(2,1)S(1)} %collective-permute-done.3.from_b_ref, bf16[2,384,128]{2,1,0:T(8,128)(2,1)S(1)} %get-tuple-element.27.grad_a_ref, ...), custom_call_target="tpu_custom_call" | custom-call | flops 20000000000 | tf_op jit(solution)/shard_map/last/pallas_call | solution.py:508
  32.3 3.6 %all-to-all-done = bf16[16,36,128]{2,1,0:T(8,128)(2,1)S(1)} async-done(((bf16[16,36,128]{2,1,0:T(8,128)(2,1)}), bf16[16,36,128]{2,1,0:T(8,128)(2,1)S(1)}, u32[]{:S(2)}, u32[]{:S(2)}) %all-to-all-start) | async-done | bytes 147488 | tf_op jit(solution)/shard_map/all_to_all | solution.py:502
  35.9 0.6 %convert_reduce_fusion = f32[36,128]{1,0:T(8,128)} fusion(bf16[16,36,128]{2,1,0:T(8,128)(2,1)S(1)} %all-to-all-done), kind=kLoop, calls=%fused_computation | loop fusion | flops 142848 | bytes 165888 | tf_op jit(solution)/shard_map/reduce_sum | solution.py:528
Async XLA Ops:
  1.7 9.9 %collective-permute-start = (bf16[2,384,128]{2,1,0:T(8,128)(2,1)S(1)}, bf16[2,384,128]{2,1,0:T(8,128)(2,1)S(1)}, u32[]{:S(2)}, u32[]{:S(2)}) collective-permute-start(bf16[2,384,128]{2,1,0:T(8,128)(2,1)S(1)} %get-tuple-element.19), channel_id=1, source_target_pairs={{0,2},{4,6},{8,10},{12,14},{16,18},{20,22},{24,26},{28,30},{2,0},{... | collective-permute-start | bytes 589832 | tf_op jit(solution)/shard_map/ppermute | solution.py:390
  4.7 6.9 %collective-permute-start.1 = (bf16[2,384,128]{2,1,0:T(8,128)(2,1)S(1)}, bf16[2,384,128]{2,1,0:T(8,128)(2,1)S(1)}, u32[]{:S(2)}, u32[]{:S(2)}) collective-permute-start(bf16[2,384,128]{2,1,0:T(8,128)(2,1)S(1)} %get-tuple-element.20), channel_id=1, source_target_pairs={{2,4},{6,8},{10,12},{14,16},{18,20},{22,24},{26,28},{4,2},{8,6},{1... | collective-permute-start | bytes 589832 | tf_op jit(solution)/shard_map/ppermute | solution.py:390
  13.2 5.7 %collective-permute-start.4 = (bf16[16,36,128]{2,1,0:T(8,128)(2,1)S(1)}, bf16[16,36,128]{2,1,0:T(8,128)(2,1)S(1)}, u32[]{:S(2)}, u32[]{:S(2)}) collective-permute-start(bf16[16,36,128]{2,1,0:T(8,128)(2,1)S(1)} %get-tuple-element.33), channel_id=1, source_target_pairs={{0,1},{1,0},{2,3},{3,2},{4,5},{5,4},{6,7},{7,6},{8,9},{9,8},{10,11... | collective-permute-start | bytes 442376 | tf_op jit(solution)/shard_map/ppermute | solution.py:500
  13.3 14.7 %collective-permute-start.2 = (bf16[2,384,128]{2,1,0:T(8,128)(2,1)S(1)}, bf16[2,384,128]{2,1,0:T(8,128)(2,1)S(1)}, u32[]{:S(2)}, u32[]{:S(2)}) collective-permute-start(bf16[2,384,128]{2,1,0:T(8,128)(2,1)S(1)} %get-tuple-element.27.grad_a_ref), channel_id=1, source_target_pairs={{0,2},{4,6},{8,10},{12,14},{16,18},{20,22},{24,26},{28,30},{2,0},{... | collective-permute-start | bytes 589832 | tf_op jit(solution)/shard_map/ppermute | solution.py:390
  18.2 9.8 %collective-permute-start.3 = (bf16[2,384,128]{2,1,0:T(8,128)(2,1)S(1)}, bf16[2,384,128]{2,1,0:T(8,128)(2,1)S(1)}, u32[]{:S(2)}, u32[]{:S(2)}) collective-permute-start(bf16[2,384,128]{2,1,0:T(8,128)(2,1)S(1)} %get-tuple-element.28.grad_b_ref), channel_id=1, source_target_pairs={{2,4},{6,8},{10,12},{14,16},{18,20},{22,24},{26,28},{4,2},{8,6},{1... | collective-permute-start | bytes 589832 | tf_op jit(solution)/shard_map/ppermute | solution.py:390
  19.6 16.3 %all-to-all-start = ((bf16[16,36,128]{2,1,0:T(8,128)(2,1)}), bf16[16,36,128]{2,1,0:T(8,128)(2,1)S(1)}, u32[]{:S(2)}, u32[]{:S(2)}) async-start(bf16[16,36,128]{2,1,0:T(8,128)(2,1)} %add_convert_fusion), calls=%async_computation | async-start | bytes 327680 | tf_op jit(solution)/shard_map/all_to_all | solution.py:502

commit v12 on v11

--- a/solution.py
+++ b/solution.py
@@ -120,7 +120,7 @@
 
 def first_kernel(
     rates_hbm, lists_hbm, x_hbm, cot_hbm, w_hbm, bias_hbm,
-    near_rates_ref, grad_ref, pre_ref, xt_ref, total_ref, mask_ref, cot_ref, back_ref, near_ref, far_ref,
+    near_rates_ref, grad_ref, pre_ref, xt_ref, total_ref, mask_ref, cot_ref, near_ref,
     rates_ref, lists_ref, bias_ref, xbuf, cbuf, wbuf, pad, xcat, gcat_ref, wide, sems,
 ):
     rows, columns, channels = x_hbm.shape
@@ -154,20 +154,15 @@
     loads[0].wait()
     none = jnp.zeros((channels, channels), BF16)
     for col in range(3):
-        there = slice(col * channels, (col + 1) * channels)
-        turned = [wbuf[tap * 3 + col].T for tap in range(3)]
         for side in range(2):
-            near_ref[side, there] = wbuf[6 * side + col]
-            far_ref[side, there] = turned[2 - 2 * side]
+            near_ref[side, col * channels : (col + 1) * channels] = wbuf[6 * side + col]
         for row in range(4):
             start = (row * 3 + col) * channels
-            here = slice(start, start + channels)
             for out in range(2):
-                there = slice(out * channels, (out + 1) * channels)
                 tap = row - out
-                wide[here, there] = wbuf[tap * 3 + col] if 0 <= tap < 3 else none
-                tap = out + 2 - row
-                back_ref[here, there] = turned[tap] if 0 <= tap < 3 else none
+                wide[start : start + channels, out * channels : (out + 1) * channels] = (
+                    wbuf[tap * 3 + col] if 0 <= tap < 3 else none
+                )
     for load in loads[1:]:
         load.wait()
     half_bias = 0.5 * bias_ref[...]
@@ -291,9 +286,9 @@
 
 def last_kernel(
     rates_ref, from_a_ref, from_b_ref, grad_a_ref, grad_b_ref,
-    grad_ref, cot_hbm, mask_ref, back_ref, far_ref,
+    grad_ref, cot_hbm, mask_ref, w_hbm,
     out_hbm,
-    cbuf, obuf, pad, gcat, spare, theirs, ours, sems,
+    wbuf, back_ref, far_ref, cbuf, obuf, pad, gcat, spare, theirs, ours, sems,
 ):
     rows, columns, channels = cot_hbm.shape
     inner = rows - 2 * HALO
@@ -308,11 +303,25 @@
         stores.append(
             pltpu.make_async_copy(obuf.at[part], out_hbm.at[part], sems.at[chunks + k])
         )
-    for load in cots:
+    weights = pltpu.make_async_copy(w_hbm, wbuf, sems.at[2 * chunks])
+    for load in [weights] + cots:
         load.start()
     clear_ends(pad, rows + 2 * HALO, columns)
     by_side(from_a_ref, from_b_ref, theirs)
     by_side(grad_a_ref, grad_b_ref, ours)
+    weights.wait()
+    blank = jnp.zeros((channels, channels), BF16)
+    for col in range(3):
+        turned = [wbuf[tap * 3 + col].T for tap in range(3)]
+        for side in range(2):
+            far_ref[side, col * channels : (col + 1) * channels] = turned[2 - 2 * side]
+        for row in range(4):
+            start = (row * 3 + col) * channels
+            for out in range(2):
+                tap = out + 2 - row
+                back_ref[start : start + channels, out * channels : (out + 1) * channels] = (
+                    turned[tap] if 0 <= tap < 3 else blank
+                )
 
     def neighbour(side):
         rate = rates_ref[2 * side, 0, 0]
@@ -442,7 +451,7 @@
     )(in_hbm(x))
     x_a, x_b = swap(rows_a, rows_b, "tile")
 
-    rates, grad, pre, xt, total, mask, cot_edge, back, near, far = call(
+    rates, grad, pre, xt, total, mask, cot_edge, near = call(
         first_kernel,
         "first",
         [
@@ -453,11 +462,9 @@
             ((wide_row, wide_row), F32),
             ((3, columns, channels), BF16),
             ((2 * HALO, columns, channels), BF16),
-            ((4 * wide_row, 2 * channels), BF16),
-            ((2, wide_row, channels), BF16),
             ((2, wide_row, channels), BF16),
         ],
-        "hhhhhh>vvvvvvvvvv",
+        "hhhhhh>vvvvvvvv",
         [
             pltpu.SMEM(dilations.shape, jnp.int32),
             pltpu.VMEM(lists.shape, jnp.int32),
@@ -509,8 +516,11 @@
         last_kernel,
         "last",
         [whole],
-        "vvvvvvhvvv>h",
+        "vvvvvvhvh>h",
         [
+            pltpu.VMEM((9, channels, channels), BF16),
+            pltpu.VMEM((4 * wide_row, 2 * channels), BF16),
+            pltpu.VMEM((2, wide_row, channels), BF16),
             pltpu.VMEM((rows, columns, channels), BF16),
             pltpu.VMEM((rows, columns, channels), BF16),
             pads(rows + 2 * HALO),
@@ -518,12 +528,12 @@
             pltpu.VMEM((2, HALO * columns, wide_row), BF16),
             sides,
             sides,
-            pltpu.SemaphoreType.DMA((2 * (rows // (2 * HALO)),)),
+            pltpu.SemaphoreType.DMA((2 * (rows // (2 * HALO)) + 1,)),
         ],
         flops=BUSY,
     )(
         rates, from_a, from_b, grad_a, grad_b,
-        grad, cot, mask, back, far,
+        grad, cot, mask, weight,
     )
     summed = jnp.sum(received.astype(F32), axis=0)
     return (input_grad[None], summed.reshape(-1))

time: 37 us -> 37 us (level)
  Pallas kernels: 13.2 us -> 14.2 us
  waiting for transfers between devices: 3.6 us -> 2.61 us
    all_to_all x1, waiting for transfers between devices: 3.59 us -> 2.59 us  [shards(): received = lax.all_to_all(both, 'tile', 0, 0, tiled=True)]
    pallas_call x1, Pallas kernels: 4.32 us -> 5.31 us  [shards(): call(last_kernel, 'last', [whole], 'vvvvvvhvh>h', [pltpu.VMEM((9, channel...]
    all_to_all x1, starting transfers between devices: 8.38 us -> 8.78 us  [shards(): received = lax.all_to_all(both, 'tile', 0, 0, tiled=True)]
  transfers between devices with their start and end apart: 6 -> 6, of which waited for: 1 -> 1; matrix products, arithmetic and copies ran while one was open for 2% -> 2% of each run, Pallas kernels for 29% -> 31%
where the time goes in v12:
time: 37 us; the launch traced here: 36.8 us
  starting transfers between devices  17.9 us (48%)
  Pallas kernels  14.2 us (38%)
  waiting for transfers between devices  2.61 us (7%)
  other arithmetic  1.33 us (4%)
  between operations  0.73 us (2%)
    ppermute x4, starting transfers between devices, swap(): results.append(lax.ppermute(rows, axis, pairs + [(j, i) for i, j in pairs]))  9.07 us
    all_to_all x1, starting transfers between devices, shards(): received = lax.all_to_all(both, 'tile', 0, 0, tiled=True)  8.78 us
    pallas_call x1, Pallas kernels, shards(): call(first_kernel, 'first', [((3, 8, LANES), jnp.int32), ((inner, columns...  6.21 us
    pallas_call x1, Pallas kernels, shards(): call(last_kernel, 'last', [whole], 'vvvvvvhvh>h', [pltpu.VMEM((9, channel...  5.31 us
    all_to_all x1, waiting for transfers between devices, shards(): received = lax.all_to_all(both, 'tile', 0, 0, tiled=True)  2.59 us
    pallas_call x1, Pallas kernels, shards(): call(lambda *refs: rims_kernel(*refs, scale=scale, paired=paired), 'rims'...  1.57 us
    pallas_call x1, Pallas kernels, shards(): call(cut_kernel, 'cut', [rim, rim], 'h>vv', [pltpu.SemaphoreType.DMA((2,...  1.09 us
  transfers between devices with their start and end apart: 6, of which 1 were waited for; matrix products, arithmetic and copies ran while one was open for 2% of the time, Pallas kernels for 31%

profile of v12, /device:TPU:0, one launch (start us, length us, event | category | flops | bytes accessed | tf_op | source)
XLA Modules:
  0.0 36.8 jit_solution(18021437311020362241)
XLA Ops:
  0.6 1.1 %cut.1 = (bf16[2,384,128]{2,1,0:T(8,128)(2,1)S(1)}, bf16[2,384,128]{2,1,0:T(8,128)(2,1)S(1)}) custom-call(bf16[12,384,128]{2,1,0:T(8,128)(2,1)} %bitcast.7), custom_call_target="tpu_custom_call" | custom-call | tf_op jit(solution)/shard_map/cut/pallas_call | solution.py:445
  1.7 3.0 %collective-permute-start = (bf16[2,384,128]{2,1,0:T(8,128)(2,1)S(1)}, bf16[2,384,128]{2,1,0:T(8,128)(2,1)S(1)}, u32[]{:S(2)}, u32[]{:S(2)}) collective-permute-start(bf16[2,384,128]{2,1,0:T(8,128)(2,1)S(1)} %get-tuple-element.17), channel_id=1, source_target_pairs={{0,2},{4,6},{8,10},{12,14},{16,18},{20,22},{24,26},{28,30},{2,0},{... | collective-permute-start | bytes 589832 | tf_op jit(solution)/shard_map/ppermute | solution.py:399
  4.7 0.7 %collective-permute-start.1 = (bf16[2,384,128]{2,1,0:T(8,128)(2,1)S(1)}, bf16[2,384,128]{2,1,0:T(8,128)(2,1)S(1)}, u32[]{:S(2)}, u32[]{:S(2)}) collective-permute-start(bf16[2,384,128]{2,1,0:T(8,128)(2,1)S(1)} %get-tuple-element.18), channel_id=1, source_target_pairs={{2,4},{6,8},{10,12},{14,16},{18,20},{22,24},{26,28},{4,2},{8,6},{1... | collective-permute-start | bytes 589832 | tf_op jit(solution)/shard_map/ppermute | solution.py:399
  5.4 6.2 %first.1 = (s32[3,8,128]{2,1,0:T(8,128)S(1)}, bf16[8,384,128]{2,1,0:T(8,128)(2,1)S(1)}, f32[4,384,128]{2,1,0:T(8,128)S(1)}, bf16[12,128,384]{2,1,0:T(8,128)(2,1)...) custom-call(s32[1,16]{1,0:T(1,128)} %rates_hbm.1, ...), custom_call_target="tpu_custom_call" | custom-call | flops 20000000000 | tf_op jit(solution)/shard_map/first/pallas_call | solution.py:454
  11.6 0.0 collective-permute-done.refs_1_
  11.6 0.0 collective-permute-done.1.refs_2_
  11.6 1.6 %rims.1 = (bf16[2,384,128]{2,1,0:T(8,128)(2,1)S(1)}, bf16[2,384,128]{2,1,0:T(8,128)(2,1)S(1)}, f32[16,36,128]{2,1,0:T(8,128)S(1)}, bf16[16,36,128]{2,1,0:T(8,128)(2,1)S(1)}) custom-call(s32[3,8,128]{2,1,0:T(8,128)S(1)} %get-tuple-element.16.refs_0_.rates_ref, bf16[2,384,128]{2,1,0:T(8,128)(2,1)S(1)} %collective-permute-done.refs_1_, ...), custom_call_target="tpu_custom_call" | custom-call | tf_op jit(solution)/shard_map/rims/pallas_call | solution.py:489
  13.2 0.1 collective-permute-start.4
  13.3 4.7 %collective-permute-start.2 = (bf16[2,384,128]{2,1,0:T(8,128)(2,1)S(1)}, bf16[2,384,128]{2,1,0:T(8,128)(2,1)S(1)}, u32[]{:S(2)}, u32[]{:S(2)}) collective-permute-start(bf16[2,384,128]{2,1,0:T(8,128)(2,1)S(1)} %get-tuple-element.25.grad_a_ref), channel_id=1, source_target_pairs={{0,2},{4,6},{8,10},{12,14},{16,18},{20,22},{24,26},{28,30},{2,0},{... | collective-permute-start | bytes 589832 | tf_op jit(solution)/shard_map/ppermute | solution.py:399
  18.0 0.7 %collective-permute-start.3 = (bf16[2,384,128]{2,1,0:T(8,128)(2,1)S(1)}, bf16[2,384,128]{2,1,0:T(8,128)(2,1)S(1)}, u32[]{:S(2)}, u32[]{:S(2)}) collective-permute-start(bf16[2,384,128]{2,1,0:T(8,128)(2,1)S(1)} %get-tuple-element.26.grad_b_ref), channel_id=1, source_target_pairs={{2,4},{6,8},{10,12},{14,16},{18,20},{22,24},{26,28},{4,2},{8,6},{1... | collective-permute-start | bytes 589832 | tf_op jit(solution)/shard_map/ppermute | solution.py:399
  18.7 0.0 collective-permute-done.4
  18.7 0.7 %add_convert_fusion = bf16[16,36,128]{2,1,0:T(8,128)(2,1)} fusion(f32[16,36,128]{2,1,0:T(8,128)S(1)} %get-tuple-element.28, bf16[16,36,128]{2,1,0:T(8,128)(2,1)S(1)} %collective-permute-done.4), kind=kLoop, calls=%fused_computation.1 | loop fusion | flops 221184 | bytes 589824 | tf_op jit(solution)/shard_map/convert_element_type | solution.py:508
  19.4 8.8 %all-to-all-start = ((bf16[16,36,128]{2,1,0:T(8,128)(2,1)}), bf16[16,36,128]{2,1,0:T(8,128)(2,1)S(1)}, u32[]{:S(2)}, u32[]{:S(2)}) async-start(bf16[16,36,128]{2,1,0:T(8,128)(2,1)} %add_convert_fusion), calls=%async_computation | async-start | bytes 327680 | tf_op jit(solution)/shard_map/all_to_all | solution.py:509
  28.2 0.0 collective-permute-done.2.from_a_ref
  28.2 0.0 collective-permute-done.3.from_b_ref
  28.2 5.3 %last.1 = bf16[12,384,128]{2,1,0:T(8,128)(2,1)} custom-call(s32[3,8,128]{2,1,0:T(8,128)S(1)} %get-tuple-element.16.refs_0_.rates_ref, bf16[2,384,128]{2,1,0:T(8,128)(2,1)S(1)} %collective-permute-done.2.from_a_ref, bf16[2,384,128]{2,1,0:T(8,128)(2,1)S(1)} %collective-permute-done.3.from_b_ref, bf16[2,384,128]{2,1,0:T(8,128)(2,1)S(1)} %get-tuple-element.25.grad_a_ref, ...), custom_call_target="tpu_custom_call" | custom-call | flops 20000000000 | tf_op jit(solution)/shard_map/last/pallas_call | solution.py:515
  33.5 2.6 %all-to-all-done = bf16[16,36,128]{2,1,0:T(8,128)(2,1)S(1)} async-done(((bf16[16,36,128]{2,1,0:T(8,128)(2,1)}), bf16[16,36,128]{2,1,0:T(8,128)(2,1)S(1)}, u32[]{:S(2)}, u32[]{:S(2)}) %all-to-all-start) | async-done | bytes 147488 | tf_op jit(solution)/shard_map/all_to_all | solution.py:509
  36.1 0.6 %convert_reduce_fusion = f32[36,128]{1,0:T(8,128)} fusion(bf16[16,36,128]{2,1,0:T(8,128)(2,1)S(1)} %all-to-all-done), kind=kLoop, calls=%fused_computation | loop fusion | flops 142848 | bytes 165888 | tf_op jit(solution)/shard_map/reduce_sum | solution.py:538
Async XLA Ops:
  1.7 9.9 %collective-permute-start = (bf16[2,384,128]{2,1,0:T(8,128)(2,1)S(1)}, bf16[2,384,128]{2,1,0:T(8,128)(2,1)S(1)}, u32[]{:S(2)}, u32[]{:S(2)}) collective-permute-start(bf16[2,384,128]{2,1,0:T(8,128)(2,1)S(1)} %get-tuple-element.17), channel_id=1, source_target_pairs={{0,2},{4,6},{8,10},{12,14},{16,18},{20,22},{24,26},{28,30},{2,0},{... | collective-permute-start | bytes 589832 | tf_op jit(solution)/shard_map/ppermute | solution.py:399
  4.7 6.9 %collective-permute-start.1 = (bf16[2,384,128]{2,1,0:T(8,128)(2,1)S(1)}, bf16[2,384,128]{2,1,0:T(8,128)(2,1)S(1)}, u32[]{:S(2)}, u32[]{:S(2)}) collective-permute-start(bf16[2,384,128]{2,1,0:T(8,128)(2,1)S(1)} %get-tuple-element.18), channel_id=1, source_target_pairs={{2,4},{6,8},{10,12},{14,16},{18,20},{22,24},{26,28},{4,2},{8,6},{1... | collective-permute-start | bytes 589832 | tf_op jit(solution)/shard_map/ppermute | solution.py:399
  13.2 5.5 %collective-permute-start.4 = (bf16[16,36,128]{2,1,0:T(8,128)(2,1)S(1)}, bf16[16,36,128]{2,1,0:T(8,128)(2,1)S(1)}, u32[]{:S(2)}, u32[]{:S(2)}) collective-permute-start(bf16[16,36,128]{2,1,0:T(8,128)(2,1)S(1)} %get-tuple-element.29), channel_id=1, source_target_pairs={{0,1},{1,0},{2,3},{3,2},{4,5},{5,4},{6,7},{7,6},{8,9},{9,8},{10,11... | collective-permute-start | bytes 442376 | tf_op jit(solution)/shard_map/ppermute | solution.py:507
  13.3 14.9 %collective-permute-start.2 = (bf16[2,384,128]{2,1,0:T(8,128)(2,1)S(1)}, bf16[2,384,128]{2,1,0:T(8,128)(2,1)S(1)}, u32[]{:S(2)}, u32[]{:S(2)}) collective-permute-start(bf16[2,384,128]{2,1,0:T(8,128)(2,1)S(1)} %get-tuple-element.25.grad_a_ref), channel_id=1, source_target_pairs={{0,2},{4,6},{8,10},{12,14},{16,18},{20,22},{24,26},{28,30},{2,0},{... | collective-permute-start | bytes 589832 | tf_op jit(solution)/shard_map/ppermute | solution.py:399
  18.0 10.2 %collective-permute-start.3 = (bf16[2,384,128]{2,1,0:T(8,128)(2,1)S(1)}, bf16[2,384,128]{2,1,0:T(8,128)(2,1)S(1)}, u32[]{:S(2)}, u32[]{:S(2)}) collective-permute-start(bf16[2,384,128]{2,1,0:T(8,128)(2,1)S(1)} %get-tuple-element.26.grad_b_ref), channel_id=1, source_target_pairs={{2,4},{6,8},{10,12},{14,16},{18,20},{22,24},{26,28},{4,2},{8,6},{1... | collective-permute-start | bytes 589832 | tf_op jit(solution)/shard_map/ppermute | solution.py:399
  19.4 16.7 %all-to-all-start = ((bf16[16,36,128]{2,1,0:T(8,128)(2,1)}), bf16[16,36,128]{2,1,0:T(8,128)(2,1)S(1)}, u32[]{:S(2)}, u32[]{:S(2)}) async-start(bf16[16,36,128]{2,1,0:T(8,128)(2,1)} %add_convert_fusion), calls=%async_computation | async-start | bytes 327680 | tf_op jit(solution)/shard_map/all_to_all | solution.py:509

commit v13 on v11

--- a/solution.py
+++ b/solution.py
@@ -11,6 +11,7 @@
 HALO = 2
 LANES = 128
 EDGE = 8
+PACK = 16
 RATES = (1, 2)
 VMEM_LIMIT = 40 * 1024 * 1024
 BUSY = 20_000_000_000
@@ -280,13 +281,15 @@
     grad_a_ref[...] = grads[1 - odd]
     grad_b_ref[...] = grads[odd]
     if not paired:
-        keep_ref[0] = flat[...]
+        keep_ref[0] = flat[: keep_ref.shape[1]]
         return
     parts, share, _ = keep_ref.shape
+    padded = send_ref.shape[1]
+    flat[parts * 2 * share :] = jnp.zeros((flat.shape[0] - parts * 2 * share, channels), F32)
     here = lax.axis_index("dp")
     for part in range(parts):
         keep_ref[part] = flat[pl.ds((2 * part + here) * share, share)]
-        send_ref[part] = flat[pl.ds((2 * part + 1 - here) * share, share)].astype(BF16)
+        send_ref[part] = flat[pl.ds((2 * part + 1 - here) * share, padded)].astype(BF16)
 
 
 def last_kernel(
@@ -478,11 +481,12 @@
     cores = lax.axis_size("dp")
     paired = cores == 2 and tap_rows % devices == 0
     share = (devices // 2, tap_rows // devices) if paired else (1, tap_rows)
+    padded = -(-share[1] // PACK) * PACK
     scale = 1.0 / math.sqrt(devices * lists.shape[1] * TILE * TILE)
     grad_a, grad_b, keep, send = call(
         lambda *refs: rims_kernel(*refs, scale=scale, paired=paired),
         "rims",
-        [rim, rim, (share + (channels,), F32), (share + (channels,), BF16)],
+        [rim, rim, (share + (channels,), F32), ((share[0], padded, channels), BF16)],
         "vvvvvvvvv>vvvv",
         [
             pads(4 * HALO),
@@ -491,14 +495,14 @@
             sides,
             pltpu.VMEM((2 * HALO, channels, columns), BF16),
             pltpu.VMEM((2 * HALO, columns, wide_row), BF16),
-            pltpu.VMEM((tap_rows, channels), F32),
+            pltpu.VMEM((tap_rows + PACK, channels), F32),
         ],
     )(rates, x_a, x_b, pre, cot_edge, mask, near, xt, total)
 
     from_a, from_b = swap(grad_a, grad_b, "tile")
     if paired:
         other = lax.ppermute(send, "dp", [(0, 1), (1, 0)])
-        both = (keep + other.astype(F32)).astype(BF16)
+        both = (keep + other[:, : share[1]].astype(F32)).astype(BF16)
         received = lax.all_to_all(both, "tile", 0, 0, tiled=True)
     else:
         received = lax.all_to_all(

time: 37 us -> 37 us (level)
  starting transfers between devices: 17.7 us -> 18.1 us
  Pallas kernels: 13.2 us -> 12.8 us
  transfers between devices with their start and end apart: 6 -> 6, of which waited for: 1 -> 1; matrix products, arithmetic and copies ran while one was open for 2% -> 2% of each run, Pallas kernels for 29% -> 28%
where the time goes in v13:
time: 37 us; the launch traced here: 36.6 us
  starting transfers between devices  18.1 us (49%)
  Pallas kernels  12.8 us (35%)
  waiting for transfers between devices  3.57 us (10%)
  other arithmetic  1.33 us (4%)
  between operations  0.73 us (2%)
    ppermute x4, starting transfers between devices, swap(): results.append(lax.ppermute(rows, axis, pairs + [(j, i) for i, j in pairs]))  9.49 us
    all_to_all x1, starting transfers between devices, shards(): received = lax.all_to_all(both, 'tile', 0, 0, tiled=True)  8.58 us
    pallas_call x1, Pallas kernels, shards(): call(first_kernel, 'first', [((3, 8, LANES), jnp.int32), ((inner, columns...  5.99 us
    pallas_call x1, Pallas kernels, shards(): call(last_kernel, 'last', [whole], 'vvvvvvhvvv>h', [pltpu.VMEM((rows, col...  4.35 us
    all_to_all x1, waiting for transfers between devices, shards(): received = lax.all_to_all(both, 'tile', 0, 0, tiled=True)  3.55 us
    pallas_call x1, Pallas kernels, shards(): call(lambda *refs: rims_kernel(*refs, scale=scale, paired=paired), 'rims'...  1.38 us
    pallas_call x1, Pallas kernels, shards(): call(cut_kernel, 'cut', [rim, rim], 'h>vv', [pltpu.SemaphoreType.DMA((2,...  1.09 us
  transfers between devices with their start and end apart: 6, of which 1 were waited for; matrix products, arithmetic and copies ran while one was open for 2% of the time, Pallas kernels for 28%

profile of v13, /device:TPU:0, one launch (start us, length us, event | category | flops | bytes accessed | tf_op | source)
XLA Modules:
  0.0 36.6 jit_solution(12351092644136655209)
XLA Ops:
  0.6 1.1 %cut.1 = (bf16[2,384,128]{2,1,0:T(8,128)(2,1)S(1)}, bf16[2,384,128]{2,1,0:T(8,128)(2,1)S(1)}) custom-call(bf16[12,384,128]{2,1,0:T(8,128)(2,1)} %bitcast.7), custom_call_target="tpu_custom_call" | custom-call | tf_op jit(solution)/shard_map/cut/pallas_call | solution.py:439
  1.7 3.0 %collective-permute-start = (bf16[2,384,128]{2,1,0:T(8,128)(2,1)S(1)}, bf16[2,384,128]{2,1,0:T(8,128)(2,1)S(1)}, u32[]{:S(2)}, u32[]{:S(2)}) collective-permute-start(bf16[2,384,128]{2,1,0:T(8,128)(2,1)S(1)} %get-tuple-element.19), channel_id=1, source_target_pairs={{0,2},{4,6},{8,10},{12,14},{16,18},{20,22},{24,26},{28,30},{2,0},{... | collective-permute-start | bytes 589832 | tf_op jit(solution)/shard_map/ppermute | solution.py:393
  4.7 0.7 %collective-permute-start.1 = (bf16[2,384,128]{2,1,0:T(8,128)(2,1)S(1)}, bf16[2,384,128]{2,1,0:T(8,128)(2,1)S(1)}, u32[]{:S(2)}, u32[]{:S(2)}) collective-permute-start(bf16[2,384,128]{2,1,0:T(8,128)(2,1)S(1)} %get-tuple-element.20), channel_id=1, source_target_pairs={{2,4},{6,8},{10,12},{14,16},{18,20},{22,24},{26,28},{4,2},{8,6},{1... | collective-permute-start | bytes 589832 | tf_op jit(solution)/shard_map/ppermute | solution.py:393
  5.4 6.0 %first.1 = (s32[3,8,128]{2,1,0:T(8,128)S(1)}, bf16[8,384,128]{2,1,0:T(8,128)(2,1)S(1)}, f32[4,384,128]{2,1,0:T(8,128)S(1)}, bf16[12,128,384]{2,1,0:T(8,128)(2,1)...) custom-call(s32[1,16]{1,0:T(1,128)} %rates_hbm.1, ...), custom_call_target="tpu_custom_call" | custom-call | flops 20000000000 | tf_op jit(solution)/shard_map/first/pallas_call | solution.py:448
  11.4 0.0 collective-permute-done.refs_1_
  11.4 0.0 collective-permute-done.1.refs_2_
  11.4 1.4 %rims.1 = (bf16[2,384,128]{2,1,0:T(8,128)(2,1)S(1)}, bf16[2,384,128]{2,1,0:T(8,128)(2,1)S(1)}, f32[16,36,128]{2,1,0:T(8,128)S(1)}, bf16[16,48,128]{2,1,0:T(8,128)(2,1)S(1)}) custom-call(s32[3,8,128]{2,1,0:T(8,128)S(1)} %get-tuple-element.18.refs_0_.rates_ref, bf16[2,384,128]{2,1,0:T(8,128)(2,1)S(1)} %collective-permute-done.refs_1_, ...), custom_call_target="tpu_custom_call" | custom-call | tf_op jit(solution)/shard_map/rims/pallas_call | solution.py:486
  12.8 0.1 collective-permute-start.4
  12.9 5.2 %collective-permute-start.2 = (bf16[2,384,128]{2,1,0:T(8,128)(2,1)S(1)}, bf16[2,384,128]{2,1,0:T(8,128)(2,1)S(1)}, u32[]{:S(2)}, u32[]{:S(2)}) collective-permute-start(bf16[2,384,128]{2,1,0:T(8,128)(2,1)S(1)} %get-tuple-element.27.grad_a_ref), channel_id=1, source_target_pairs={{0,2},{4,6},{8,10},{12,14},{16,18},{20,22},{24,26},{28,30},{2,0},{... | collective-permute-start | bytes 589832 | tf_op jit(solution)/shard_map/ppermute | solution.py:393
  18.0 0.7 %collective-permute-start.3 = (bf16[2,384,128]{2,1,0:T(8,128)(2,1)S(1)}, bf16[2,384,128]{2,1,0:T(8,128)(2,1)S(1)}, u32[]{:S(2)}, u32[]{:S(2)}) collective-permute-start(bf16[2,384,128]{2,1,0:T(8,128)(2,1)S(1)} %get-tuple-element.28.grad_b_ref), channel_id=1, source_target_pairs={{2,4},{6,8},{10,12},{14,16},{18,20},{22,24},{26,28},{4,2},{8,6},{1... | collective-permute-start | bytes 589832 | tf_op jit(solution)/shard_map/ppermute | solution.py:393
  18.7 0.0 collective-permute-done.4
  18.7 0.7 %add_convert_fusion = bf16[16,36,128]{2,1,0:T(8,128)(2,1)} fusion(f32[16,36,128]{2,1,0:T(8,128)S(1)} %get-tuple-element.32, bf16[16,48,128]{2,1,0:T(8,128)(2,1)S(1)} %collective-permute-done.4), kind=kLoop, calls=%fused_computation.1 | loop fusion | flops 221184 | bytes 589824 | tf_op jit(solution)/shard_map/convert_element_type | solution.py:505
  19.4 8.6 %all-to-all-start = ((bf16[16,36,128]{2,1,0:T(8,128)(2,1)}), bf16[16,36,128]{2,1,0:T(8,128)(2,1)S(1)}, u32[]{:S(2)}, u32[]{:S(2)}) async-start(bf16[16,36,128]{2,1,0:T(8,128)(2,1)} %add_convert_fusion), calls=%async_computation | async-start | bytes 327680 | tf_op jit(solution)/shard_map/all_to_all | solution.py:506
  28.0 0.0 collective-permute-done.2.from_a_ref
  28.0 0.0 collective-permute-done.3.from_b_ref
  28.0 4.3 %last.1 = bf16[12,384,128]{2,1,0:T(8,128)(2,1)} custom-call(s32[3,8,128]{2,1,0:T(8,128)S(1)} %get-tuple-element.18.refs_0_.rates_ref, bf16[2,384,128]{2,1,0:T(8,128)(2,1)S(1)} %collective-permute-done.2.from_a_ref, bf16[2,384,128]{2,1,0:T(8,128)(2,1)S(1)} %collective-permute-done.3.from_b_ref, bf16[2,384,128]{2,1,0:T(8,128)(2,1)S(1)} %get-tuple-element.27.grad_a_ref, ...), custom_call_target="tpu_custom_call" | custom-call | flops 20000000000 | tf_op jit(solution)/shard_map/last/pallas_call | solution.py:512
  32.4 3.6 %all-to-all-done = bf16[16,36,128]{2,1,0:T(8,128)(2,1)S(1)} async-done(((bf16[16,36,128]{2,1,0:T(8,128)(2,1)}), bf16[16,36,128]{2,1,0:T(8,128)(2,1)S(1)}, u32[]{:S(2)}, u32[]{:S(2)}) %all-to-all-start) | async-done | bytes 147488 | tf_op jit(solution)/shard_map/all_to_all | solution.py:506
  35.9 0.6 %convert_reduce_fusion = f32[36,128]{1,0:T(8,128)} fusion(bf16[16,36,128]{2,1,0:T(8,128)(2,1)S(1)} %all-to-all-done), kind=kLoop, calls=%fused_computation | loop fusion | flops 142848 | bytes 165888 | tf_op jit(solution)/shard_map/reduce_sum | solution.py:532
Async XLA Ops:
  1.7 9.7 %collective-permute-start = (bf16[2,384,128]{2,1,0:T(8,128)(2,1)S(1)}, bf16[2,384,128]{2,1,0:T(8,128)(2,1)S(1)}, u32[]{:S(2)}, u32[]{:S(2)}) collective-permute-start(bf16[2,384,128]{2,1,0:T(8,128)(2,1)S(1)} %get-tuple-element.19), channel_id=1, source_target_pairs={{0,2},{4,6},{8,10},{12,14},{16,18},{20,22},{24,26},{28,30},{2,0},{... | collective-permute-start | bytes 589832 | tf_op jit(solution)/shard_map/ppermute | solution.py:393
  4.7 6.7 %collective-permute-start.1 = (bf16[2,384,128]{2,1,0:T(8,128)(2,1)S(1)}, bf16[2,384,128]{2,1,0:T(8,128)(2,1)S(1)}, u32[]{:S(2)}, u32[]{:S(2)}) collective-permute-start(bf16[2,384,128]{2,1,0:T(8,128)(2,1)S(1)} %get-tuple-element.20), channel_id=1, source_target_pairs={{2,4},{6,8},{10,12},{14,16},{18,20},{22,24},{26,28},{4,2},{8,6},{1... | collective-permute-start | bytes 589832 | tf_op jit(solution)/shard_map/ppermute | solution.py:393
  12.8 5.9 %collective-permute-start.4 = (bf16[16,48,128]{2,1,0:T(8,128)(2,1)S(1)}, bf16[16,48,128]{2,1,0:T(8,128)(2,1)S(1)}, u32[]{:S(2)}, u32[]{:S(2)}) collective-permute-start(bf16[16,48,128]{2,1,0:T(8,128)(2,1)S(1)} %get-tuple-element.33), channel_id=1, source_target_pairs={{0,1},{1,0},{2,3},{3,2},{4,5},{5,4},{6,7},{7,6},{8,9},{9,8},{10,11... | collective-permute-start | bytes 589832 | tf_op jit(solution)/shard_map/ppermute | solution.py:504
  12.9 15.1 %collective-permute-start.2 = (bf16[2,384,128]{2,1,0:T(8,128)(2,1)S(1)}, bf16[2,384,128]{2,1,0:T(8,128)(2,1)S(1)}, u32[]{:S(2)}, u32[]{:S(2)}) collective-permute-start(bf16[2,384,128]{2,1,0:T(8,128)(2,1)S(1)} %get-tuple-element.27.grad_a_ref), channel_id=1, source_target_pairs={{0,2},{4,6},{8,10},{12,14},{16,18},{20,22},{24,26},{28,30},{2,0},{... | collective-permute-start | bytes 589832 | tf_op jit(solution)/shard_map/ppermute | solution.py:393
  18.0 10.0 %collective-permute-start.3 = (bf16[2,384,128]{2,1,0:T(8,128)(2,1)S(1)}, bf16[2,384,128]{2,1,0:T(8,128)(2,1)S(1)}, u32[]{:S(2)}, u32[]{:S(2)}) collective-permute-start(bf16[2,384,128]{2,1,0:T(8,128)(2,1)S(1)} %get-tuple-element.28.grad_b_ref), channel_id=1, source_target_pairs={{2,4},{6,8},{10,12},{14,16},{18,20},{22,24},{26,28},{4,2},{8,6},{1... | collective-permute-start | bytes 589832 | tf_op jit(solution)/shard_map/ppermute | solution.py:393
  19.4 16.5 %all-to-all-start = ((bf16[16,36,128]{2,1,0:T(8,128)(2,1)}), bf16[16,36,128]{2,1,0:T(8,128)(2,1)S(1)}, u32[]{:S(2)}, u32[]{:S(2)}) async-start(bf16[16,36,128]{2,1,0:T(8,128)(2,1)} %add_convert_fusion), calls=%async_computation | async-start | bytes 327680 | tf_op jit(solution)/shard_map/all_to_all | solution.py:506

commit v14 on v13

--- a/solution.py
+++ b/solution.py
@@ -169,7 +169,7 @@
                 wide[here, there] = wbuf[tap * 3 + col] if 0 <= tap < 3 else none
                 tap = out + 2 - row
                 back_ref[here, there] = turned[tap] if 0 <= tap < 3 else none
-    for load in loads[1:]:
+    for load in loads[1:5]:
         load.wait()
     half_bias = 0.5 * bias_ref[...]
 
@@ -212,9 +212,14 @@
         ready = []
         summed = []
         waiting = None
+        landed = False
         for pair in row_pairs(rate, range(rows)) + [None]:
             result = convolve(pair) if pair else None
             if waiting:
+                if not landed:
+                    landed = True
+                    for load in loads[5:]:
+                        load.wait()
                 finish(*waiting)
             waiting = result
             while len(ready) >= 2:

time: 37 us -> 36.9 us (level)
  transfers between devices with their start and end apart: 6 -> 6, of which waited for: 1 -> 1; matrix products, arithmetic and copies ran while one was open for 2% -> 2% of each run, Pallas kernels for 28% -> 29%
where the time goes in v14:
time: 36.9 us; the launch traced here: 36.6 us
  starting transfers between devices  18 us (49%)
  Pallas kernels  12.9 us (35%)
  waiting for transfers between devices  3.57 us (10%)
  other arithmetic  1.33 us (4%)
  between operations  0.73 us (2%)
    ppermute x4, starting transfers between devices, swap(): results.append(lax.ppermute(rows, axis, pairs + [(j, i) for i, j in pairs]))  9.4 us
    all_to_all x1, starting transfers between devices, shards(): received = lax.all_to_all(both, 'tile', 0, 0, tiled=True)  8.58 us
    pallas_call x1, Pallas kernels, shards(): call(first_kernel, 'first', [((3, 8, LANES), jnp.int32), ((inner, columns...  6.09 us
    pallas_call x1, Pallas kernels, shards(): call(last_kernel, 'last', [whole], 'vvvvvvhvvv>h', [pltpu.VMEM((rows, col...  4.35 us
    all_to_all x1, waiting for transfers between devices, shards(): received = lax.all_to_all(both, 'tile', 0, 0, tiled=True)  3.55 us
    pallas_call x1, Pallas kernels, shards(): call(lambda *refs: rims_kernel(*refs, scale=scale, paired=paired), 'rims'...  1.38 us
    pallas_call x1, Pallas kernels, shards(): call(cut_kernel, 'cut', [rim, rim], 'h>vv', [pltpu.SemaphoreType.DMA((2,...  1.09 us
  transfers between devices with their start and end apart: 6, of which 1 were waited for; matrix products, arithmetic and copies ran while one was open for 2% of the time, Pallas kernels for 29%

profile of v14, /device:TPU:0, one launch (start us, length us, event | category | flops | bytes accessed | tf_op | source)
XLA Modules:
  0.0 36.6 jit_solution(17557908036138374183)
XLA Ops:
  0.6 1.1 %cut.1 = (bf16[2,384,128]{2,1,0:T(8,128)(2,1)S(1)}, bf16[2,384,128]{2,1,0:T(8,128)(2,1)S(1)}) custom-call(bf16[12,384,128]{2,1,0:T(8,128)(2,1)} %bitcast.7), custom_call_target="tpu_custom_call" | custom-call | tf_op jit(solution)/shard_map/cut/pallas_call | solution.py:444
  1.7 3.0 %collective-permute-start = (bf16[2,384,128]{2,1,0:T(8,128)(2,1)S(1)}, bf16[2,384,128]{2,1,0:T(8,128)(2,1)S(1)}, u32[]{:S(2)}, u32[]{:S(2)}) collective-permute-start(bf16[2,384,128]{2,1,0:T(8,128)(2,1)S(1)} %get-tuple-element.19), channel_id=1, source_target_pairs={{0,2},{4,6},{8,10},{12,14},{16,18},{20,22},{24,26},{28,30},{2,0},{... | collective-permute-start | bytes 589832 | tf_op jit(solution)/shard_map/ppermute | solution.py:398
  4.7 0.7 %collective-permute-start.1 = (bf16[2,384,128]{2,1,0:T(8,128)(2,1)S(1)}, bf16[2,384,128]{2,1,0:T(8,128)(2,1)S(1)}, u32[]{:S(2)}, u32[]{:S(2)}) collective-permute-start(bf16[2,384,128]{2,1,0:T(8,128)(2,1)S(1)} %get-tuple-element.20), channel_id=1, source_target_pairs={{2,4},{6,8},{10,12},{14,16},{18,20},{22,24},{26,28},{4,2},{8,6},{1... | collective-permute-start | bytes 589832 | tf_op jit(solution)/shard_map/ppermute | solution.py:398
  5.4 6.1 %first.1 = (s32[3,8,128]{2,1,0:T(8,128)S(1)}, bf16[8,384,128]{2,1,0:T(8,128)(2,1)S(1)}, f32[4,384,128]{2,1,0:T(8,128)S(1)}, bf16[12,128,384]{2,1,0:T(8,128)(2,1)...) custom-call(s32[1,16]{1,0:T(1,128)} %rates_hbm.1, ...), custom_call_target="tpu_custom_call" | custom-call | flops 20000000000 | tf_op jit(solution)/shard_map/first/pallas_call | solution.py:453
  11.5 0.0 collective-permute-done.refs_1_
  11.5 0.0 collective-permute-done.1.refs_2_
  11.5 1.4 %rims.1 = (bf16[2,384,128]{2,1,0:T(8,128)(2,1)S(1)}, bf16[2,384,128]{2,1,0:T(8,128)(2,1)S(1)}, f32[16,36,128]{2,1,0:T(8,128)S(1)}, bf16[16,48,128]{2,1,0:T(8,128)(2,1)S(1)}) custom-call(s32[3,8,128]{2,1,0:T(8,128)S(1)} %get-tuple-element.18.refs_0_.rates_ref, bf16[2,384,128]{2,1,0:T(8,128)(2,1)S(1)} %collective-permute-done.refs_1_, ...), custom_call_target="tpu_custom_call" | custom-call | tf_op jit(solution)/shard_map/rims/pallas_call | solution.py:491
  12.9 0.1 collective-permute-start.4
  13.0 5.1 %collective-permute-start.2 = (bf16[2,384,128]{2,1,0:T(8,128)(2,1)S(1)}, bf16[2,384,128]{2,1,0:T(8,128)(2,1)S(1)}, u32[]{:S(2)}, u32[]{:S(2)}) collective-permute-start(bf16[2,384,128]{2,1,0:T(8,128)(2,1)S(1)} %get-tuple-element.27.grad_a_ref), channel_id=1, source_target_pairs={{0,2},{4,6},{8,10},{12,14},{16,18},{20,22},{24,26},{28,30},{2,0},{... | collective-permute-start | bytes 589832 | tf_op jit(solution)/shard_map/ppermute | solution.py:398
  18.0 0.7 %collective-permute-start.3 = (bf16[2,384,128]{2,1,0:T(8,128)(2,1)S(1)}, bf16[2,384,128]{2,1,0:T(8,128)(2,1)S(1)}, u32[]{:S(2)}, u32[]{:S(2)}) collective-permute-start(bf16[2,384,128]{2,1,0:T(8,128)(2,1)S(1)} %get-tuple-element.28.grad_b_ref), channel_id=1, source_target_pairs={{2,4},{6,8},{10,12},{14,16},{18,20},{22,24},{26,28},{4,2},{8,6},{1... | collective-permute-start | bytes 589832 | tf_op jit(solution)/shard_map/ppermute | solution.py:398
  18.7 0.0 collective-permute-done.4
  18.7 0.7 %add_convert_fusion = bf16[16,36,128]{2,1,0:T(8,128)(2,1)} fusion(f32[16,36,128]{2,1,0:T(8,128)S(1)} %get-tuple-element.32, bf16[16,48,128]{2,1,0:T(8,128)(2,1)S(1)} %collective-permute-done.4), kind=kLoop, calls=%fused_computation.1 | loop fusion | flops 221184 | bytes 589824 | tf_op jit(solution)/shard_map/convert_element_type | solution.py:510
  19.4 8.6 %all-to-all-start = ((bf16[16,36,128]{2,1,0:T(8,128)(2,1)}), bf16[16,36,128]{2,1,0:T(8,128)(2,1)S(1)}, u32[]{:S(2)}, u32[]{:S(2)}) async-start(bf16[16,36,128]{2,1,0:T(8,128)(2,1)} %add_convert_fusion), calls=%async_computation | async-start | bytes 327680 | tf_op jit(solution)/shard_map/all_to_all | solution.py:511
  28.0 0.0 collective-permute-done.2.from_a_ref
  28.0 0.0 collective-permute-done.3.from_b_ref
  28.0 4.3 %last.1 = bf16[12,384,128]{2,1,0:T(8,128)(2,1)} custom-call(s32[3,8,128]{2,1,0:T(8,128)S(1)} %get-tuple-element.18.refs_0_.rates_ref, bf16[2,384,128]{2,1,0:T(8,128)(2,1)S(1)} %collective-permute-done.2.from_a_ref, bf16[2,384,128]{2,1,0:T(8,128)(2,1)S(1)} %collective-permute-done.3.from_b_ref, bf16[2,384,128]{2,1,0:T(8,128)(2,1)S(1)} %get-tuple-element.27.grad_a_ref, ...), custom_call_target="tpu_custom_call" | custom-call | flops 20000000000 | tf_op jit(solution)/shard_map/last/pallas_call | solution.py:517
  32.4 3.6 %all-to-all-done = bf16[16,36,128]{2,1,0:T(8,128)(2,1)S(1)} async-done(((bf16[16,36,128]{2,1,0:T(8,128)(2,1)}), bf16[16,36,128]{2,1,0:T(8,128)(2,1)S(1)}, u32[]{:S(2)}, u32[]{:S(2)}) %all-to-all-start) | async-done | bytes 147488 | tf_op jit(solution)/shard_map/all_to_all | solution.py:511
  35.9 0.6 %convert_reduce_fusion = f32[36,128]{1,0:T(8,128)} fusion(bf16[16,36,128]{2,1,0:T(8,128)(2,1)S(1)} %all-to-all-done), kind=kLoop, calls=%fused_computation | loop fusion | flops 142848 | bytes 165888 | tf_op jit(solution)/shard_map/reduce_sum | solution.py:537
Async XLA Ops:
  1.7 9.8 %collective-permute-start = (bf16[2,384,128]{2,1,0:T(8,128)(2,1)S(1)}, bf16[2,384,128]{2,1,0:T(8,128)(2,1)S(1)}, u32[]{:S(2)}, u32[]{:S(2)}) collective-permute-start(bf16[2,384,128]{2,1,0:T(8,128)(2,1)S(1)} %get-tuple-element.19), channel_id=1, source_target_pairs={{0,2},{4,6},{8,10},{12,14},{16,18},{20,22},{24,26},{28,30},{2,0},{... | collective-permute-start | bytes 589832 | tf_op jit(solution)/shard_map/ppermute | solution.py:398
  4.7 6.8 %collective-permute-start.1 = (bf16[2,384,128]{2,1,0:T(8,128)(2,1)S(1)}, bf16[2,384,128]{2,1,0:T(8,128)(2,1)S(1)}, u32[]{:S(2)}, u32[]{:S(2)}) collective-permute-start(bf16[2,384,128]{2,1,0:T(8,128)(2,1)S(1)} %get-tuple-element.20), channel_id=1, source_target_pairs={{2,4},{6,8},{10,12},{14,16},{18,20},{22,24},{26,28},{4,2},{8,6},{1... | collective-permute-start | bytes 589832 | tf_op jit(solution)/shard_map/ppermute | solution.py:398
  12.9 5.8 %collective-permute-start.4 = (bf16[16,48,128]{2,1,0:T(8,128)(2,1)S(1)}, bf16[16,48,128]{2,1,0:T(8,128)(2,1)S(1)}, u32[]{:S(2)}, u32[]{:S(2)}) collective-permute-start(bf16[16,48,128]{2,1,0:T(8,128)(2,1)S(1)} %get-tuple-element.33), channel_id=1, source_target_pairs={{0,1},{1,0},{2,3},{3,2},{4,5},{5,4},{6,7},{7,6},{8,9},{9,8},{10,11... | collective-permute-start | bytes 589832 | tf_op jit(solution)/shard_map/ppermute | solution.py:509
  13.0 15.0 %collective-permute-start.2 = (bf16[2,384,128]{2,1,0:T(8,128)(2,1)S(1)}, bf16[2,384,128]{2,1,0:T(8,128)(2,1)S(1)}, u32[]{:S(2)}, u32[]{:S(2)}) collective-permute-start(bf16[2,384,128]{2,1,0:T(8,128)(2,1)S(1)} %get-tuple-element.27.grad_a_ref), channel_id=1, source_target_pairs={{0,2},{4,6},{8,10},{12,14},{16,18},{20,22},{24,26},{28,30},{2,0},{... | collective-permute-start | bytes 589832 | tf_op jit(solution)/shard_map/ppermute | solution.py:398
  18.0 10.0 %collective-permute-start.3 = (bf16[2,384,128]{2,1,0:T(8,128)(2,1)S(1)}, bf16[2,384,128]{2,1,0:T(8,128)(2,1)S(1)}, u32[]{:S(2)}, u32[]{:S(2)}) collective-permute-start(bf16[2,384,128]{2,1,0:T(8,128)(2,1)S(1)} %get-tuple-element.28.grad_b_ref), channel_id=1, source_target_pairs={{2,4},{6,8},{10,12},{14,16},{18,20},{22,24},{26,28},{4,2},{8,6},{1... | collective-permute-start | bytes 589832 | tf_op jit(solution)/shard_map/ppermute | solution.py:398
  19.4 16.5 %all-to-all-start = ((bf16[16,36,128]{2,1,0:T(8,128)(2,1)}), bf16[16,36,128]{2,1,0:T(8,128)(2,1)S(1)}, u32[]{:S(2)}, u32[]{:S(2)}) async-start(bf16[16,36,128]{2,1,0:T(8,128)(2,1)} %add_convert_fusion), calls=%async_computation | async-start | bytes 327680 | tf_op jit(solution)/shard_map/all_to_all | solution.py:511
